TPU v7x, 512 devices: a whole 4x4x16 slice. The times are simulated.
512 devices in a mesh: dp: 32 (over z_hi, x, y), seq: 16 (over z_lo, core).
Axes of the slice: x: 4, y: 4, z: 16 (z_hi: 2, z_lo: 8; z = z_hi * 8 + z_lo), core: 2. Of those that a mesh axis runs over, the one named last changes fastest.
Arguments:
- tokens: bfloat16 [32, 2048, 1024], P('dp', 'seq'), may hold values from -12 to 12, as said below
- grad_out: bfloat16 [32, 2048, 1024], P('dp', 'seq'), may hold values from -6 to 6
- stacked: bfloat16 [1024, 4, 512], P('seq'), may hold values from -0.176776695 to 0.176776695, as said below
Outputs:
- layer_out: bfloat16 [32, 2048, 1024], P('dp', 'seq')
- grad_tokens: bfloat16 [32, 2048, 1024], P('dp', 'seq')
- grad_weights: float32 [1024, 4, 512], P('seq')
Inputs may be any that keep to these rules, and one draw needn't show every extreme that they name: `tokens`: activations of order one. `stacked`: entries scaled by the inverse square root of their fan-in.
All inputs are finite; a program needn't handle non-finite values.
Results may differ from a plain program's by a relative error of at most 0.035.
Values may be sent and summed in bfloat16 or wider, within the bound.
No kernel may reach another device: no remote copies, remote signals or barrier semaphores. Data moves between devices by JAX's collectives and lax.ppermute only.
A program may use at most 64 MiB of HBM per device.

v0:
```python
import math

import jax
import jax.numpy as jnp
from jax import lax
from jax.sharding import PartitionSpec as P

HEAD = 64


LOG_TWO = math.log(2.0)


def partner_2(value, axis, bit):
    return lax.ppermute(value, axis, [(i, i ^ 1 << bit) for i in range(lax.axis_size(axis))])


def pair_mean(blocks):
    widened = blocks.astype(jnp.float32)
    paired = widened.reshape(widened.shape[:-2] + (widened.shape[-2] // 2, 2, widened.shape[-1]))
    return (0.5 * (paired[..., 0, :] + paired[..., 1, :])).astype(jnp.bfloat16)


def make_term(left_inputs, left_grads, back_all, attended_flat, width):

    def grad_term(offset, length):
        part_inputs = lax.dot_general(
            left_inputs, back_all, (((0,), (0,)), ((), ())), preferred_element_type=jnp.float32
        )
        part_output = lax.dot_general(
            left_grads, attended_flat, (((0,), (0,)), ((), ())), preferred_element_type=jnp.float32
        )
        return jnp.concatenate([part_inputs, part_output], axis=1).reshape(length, 4, width)

    return grad_term


def per_device(tokens, grad_out, stacked):
    levels = lax.axis_size("seq").bit_length() - 1
    position = lax.axis_index("seq")
    sequences, leaf_rows, model_width = tokens.shape
    row_count = sequences * leaf_rows
    gathered = lax.all_gather(stacked, "seq", axis=0, tiled=True)
    width = gathered.shape[2]
    qkv_weight = gathered[:, :3, :].reshape(model_width, 3 * width)
    out_weight = gathered[:, 3, :]
    flat_tokens = tokens.reshape(row_count, model_width)
    flat_grads = grad_out.reshape(row_count, model_width)
    projected = jnp.dot(flat_tokens, qkv_weight, preferred_element_type=jnp.float32).astype(
        jnp.bfloat16
    )
    queries = projected[:, :width].reshape(sequences, leaf_rows, width)
    key_value = jnp.stack([projected[:, width : 2 * width], projected[:, 2 * width :]]).reshape(
        2, sequences, leaf_rows, width
    )
    grad_attn = jnp.dot(flat_grads, out_weight, preferred_element_type=jnp.float32).astype(
        jnp.bfloat16
    )
    grad_attn = grad_attn.reshape(sequences, leaf_rows, width)
    siblings = []
    current = key_value
    for height in range(levels):
        partner = partner_2(current, "seq", height)
        siblings.append(partner)
        if height + 1 < levels:
            lower_first = position >> height & 1 == 0
            low_half = jnp.where(lower_first, current, partner)
            high_half = jnp.where(lower_first, partner, current)
            current = pair_mean(jnp.concatenate([low_half, high_half], axis=2))
    key_sets = jnp.concatenate([key_value] + siblings, axis=2)
    key_count = key_sets.shape[2]
    offsets = jnp.maximum(jnp.arange(key_count) // leaf_rows - 1, 0).astype(jnp.float32) * LOG_TWO
    score_scale = 1.0 / math.sqrt(HEAD)
    group_heads = max(1, min(width // HEAD, 128 // HEAD))
    group_width = group_heads * HEAD
    attended_parts = []
    dquery_parts = []
    key_grad_parts = []
    value_grad_parts = []
    for column in range(0, width, group_width):
        query_part = queries[:, :, column : column + group_width].reshape(
            sequences, leaf_rows, group_heads, HEAD
        )
        key_part = key_sets[0, :, :, column : column + group_width].reshape(
            sequences, key_count, group_heads, HEAD
        )
        value_part = key_sets[1, :, :, column : column + group_width].reshape(
            sequences, key_count, group_heads, HEAD
        )
        grad_part = grad_attn[:, :, column : column + group_width].reshape(
            sequences, leaf_rows, group_heads, HEAD
        )
        scores = (
            jnp.einsum("sqhe,skhe->shqk", query_part, key_part, preferred_element_type=jnp.float32)
            * score_scale
            + offsets
        )
        row_peak = jnp.max(scores, axis=-1, keepdims=True)
        exponent = jnp.exp(scores - row_peak)
        weights = exponent / jnp.sum(exponent, axis=-1, keepdims=True)
        weights_low = weights.astype(jnp.bfloat16)
        attended = jnp.einsum(
            "shqk,skhe->sqhe", weights_low, value_part, preferred_element_type=jnp.float32
        ).astype(jnp.bfloat16)
        dprobs = jnp.einsum(
            "sqhe,skhe->shqk", grad_part, value_part, preferred_element_type=jnp.float32
        )
        rowdot = jnp.sum(weights * dprobs, axis=-1, keepdims=True)
        dscore = (weights * (dprobs - rowdot) * score_scale).astype(jnp.bfloat16)
        dquery = jnp.einsum(
            "shqk,skhe->sqhe", dscore, key_part, preferred_element_type=jnp.float32
        ).astype(jnp.bfloat16)
        key_grad = jnp.einsum(
            "shqk,sqhe->skhe", dscore, query_part, preferred_element_type=jnp.float32
        )
        value_grad = jnp.einsum(
            "shqk,sqhe->skhe", weights_low, grad_part, preferred_element_type=jnp.float32
        )
        attended_parts.append(attended.reshape(sequences, leaf_rows, group_width))
        dquery_parts.append(dquery.reshape(sequences, leaf_rows, group_width))
        key_grad_parts.append(key_grad.reshape(sequences, key_count, group_width))
        value_grad_parts.append(value_grad.reshape(sequences, key_count, group_width))
    attended_flat = jnp.concatenate(attended_parts, axis=-1).reshape(row_count, width)
    dquery_flat = jnp.concatenate(dquery_parts, axis=-1).reshape(row_count, width)
    grads = jnp.stack(
        [jnp.concatenate(key_grad_parts, axis=-1), jnp.concatenate(value_grad_parts, axis=-1)]
    )
    layer_out = lax.dot_general(
        attended_flat, out_weight, (((1,), (1,)), ((), ())), preferred_element_type=jnp.float32
    )
    layer_out = layer_out.astype(jnp.bfloat16).reshape(sequences, leaf_rows, model_width)
    carried = None
    for height in reversed(range(levels)):
        piece = grads[:, :, (height + 1) * leaf_rows : (height + 2) * leaf_rows]
        incoming = lax.optimization_barrier(piece.astype(jnp.bfloat16)).astype(jnp.float32)
        if carried is None:
            retained = jnp.zeros_like(incoming)
            outgoing = incoming
        else:
            spread = jnp.repeat(0.5 * carried, 2, axis=2)
            low_part = spread[:, :, :leaf_rows]
            high_part = spread[:, :, leaf_rows:]
            lower_first = position >> height & 1 == 0
            retained = jnp.where(lower_first, low_part, high_part)
            outgoing = jnp.where(lower_first, high_part, low_part) + incoming
        received = partner_2(outgoing.astype(jnp.bfloat16), "seq", height).astype(outgoing.dtype)
        carried = retained + received
    own_grads = (grads[:, :, :leaf_rows] + carried).astype(jnp.bfloat16)
    back_all = jnp.concatenate(
        [
            dquery_flat,
            own_grads[0].reshape(row_count, width),
            own_grads[1].reshape(row_count, width),
        ],
        axis=-1,
    )
    grad_tokens = lax.dot_general(
        back_all, qkv_weight, (((1,), (1,)), ((), ())), preferred_element_type=jnp.float32
    )
    grad_tokens = grad_tokens.astype(jnp.bfloat16).reshape(sequences, leaf_rows, model_width)
    seq_count = lax.axis_size("seq")
    dp_count = lax.axis_size("dp")
    total_tokens = row_count * seq_count * dp_count
    grad_term = make_term(flat_tokens, flat_grads, back_all, attended_flat, width)
    partial_value = lax.psum_scatter(
        grad_term(jnp.int32(0), model_width // seq_count * lax.axis_size("seq")).astype(
            jnp.bfloat16
        ),
        "seq",
        scatter_dimension=0,
        tiled=True,
    )
    summed = lax.psum(partial_value, "dp").astype(jnp.float32)
    grad_weights = summed * (1.0 / math.sqrt(total_tokens))
    return (layer_out, grad_tokens, grad_weights)


def solution(mesh):
    placed = (P("dp", "seq", None), P("dp", "seq", None), P("seq", None, None))
    return jax.shard_map(
        per_device,
        mesh=mesh,
        in_specs=placed,
        out_specs=(P("dp", "seq", None), P("dp", "seq", None), P("seq", None, None)),
        check_vma=False,
    )
```

profile of v0, /device:TPU:1, one launch (start us, length us, event | category | flops | bytes accessed | tf_op | source)
XLA Modules:
  0.0 1160.3 jit_solution(9056658756116630609)
XLA Ops:
  8.0 112.4 %all-gather.2.cloned.1.call-done = bf16[1024,4,512]{2,1,0:T(4,128)(2,1)} async-done(((bf16[64,4,512]{2,1,0:T(4,128)(2,1)}), bf16[1024,4,512]{2,1,0:T(4,128)(2,1)}) %all-gather.2.cloned.1.call-update) | async-done | bytes 4194320 | tf_op jit(solution)/shard_map/all_gather | solution.py:43
  120.3 5.5 copy.134
  129.1 4.8 collective-permute-start
  148.0 6.1 collective-permute-done.1
  164.5 4.6 slice.186
  170.4 8.7 collective-permute-done.2
  187.2 5.0 collective-permute-start.3
  203.5 13.4 %collective-permute-done.3 = bf16[2,1,128,512]{3,2,0,1:T(8,128)(2,1)} collective-permute-done((bf16[2,1,128,512]{3,2,0,1:T(8,128)(2,1)}, bf16[2,1,128,512]{3,2,0,1:T(8,128)(2,1)}, u32[]{:S(2)}, u32[]{:S(2)}) %collective-permute-start.3) | collective-permute-done | bytes 262176 | tf_op jit(solution)/shard_map/ppermute | solution.py:15
  233.7 3.6 fusion.52
  260.2 3.6 fusion.47
  274.1 3.7 fusion.42
  288.0 3.6 fusion.57
  301.7 3.3 convolution_convert_fusion.7
  307.3 14.5 %collective-permute-done.4 = bf16[2,1,128,512]{3,2,0,1:T(8,128)(2,1)} collective-permute-done((bf16[2,1,128,512]{3,2,0,1:T(8,128)(2,1)}, bf16[2,1,128,512]{3,2,0,1:T(8,128)(2,1)}, u32[]{:S(2)}, u32[]{:S(2)}) %collective-permute-start.4) | collective-permute-done | bytes 262176 | tf_op jit(solution)/shard_map/ppermute | solution.py:15
  324.1 2.9 broadcast_in_dim.13
  331.3 3.5 convolution_convert_fusion.6
  337.0 6.2 collective-permute-done.5
  345.9 2.9 broadcast_in_dim.15
  353.0 3.4 convolution_convert_fusion.9
  365.0 2.9 broadcast_in_dim.17
  379.1 7.8 copy.133
  389.0 2.9 fusion.39
  391.8 204.6 %all-reduce.6.cloned.1.call-done = bf16[1024,4,512]{2,1,0:T(4,128)(2,1)} async-done(((bf16[1024,4,512]{2,1,0:T(4,128)(2,1)}), bf16[1024,4,512]{2,1,0:T(4,128)(2,1)}) %all-reduce.6.cloned.1.call-update) | async-done | bytes 4194320
  600.4 551.5 %all-reduce.4.cloned.1.call-done = bf16[64,4,512]{2,1,0:T(4,128)(2,1)} async-done(((bf16[64,4,512]{2,1,0:T(4,128)(2,1)}), bf16[64,4,512]{2,1,0:T(4,128)(2,1)}) %all-reduce.4.cloned.1.call-update) | async-done | bytes 262160 | tf_op jit(solution)/shard_map/psum | solution.py:173
  (148 shorter events, 164.1 us)
Async XLA Ops:
  7.2 118.7 %copy-start = (bf16[1,128,1024]{2,1,0:T(8,128)(2,1)S(1)}, bf16[1,128,1024]{2,1,0:T(8,128)(2,1)}, u32[]{:S(2)}) copy-start(bf16[1,128,1024]{2,1,0:T(8,128)(2,1)} %param.3) | copy-start | bytes 786436
  7.2 113.1 %all-gather.2.cloned.1.call-start = ((), (), s32[]{:S(2)}) async-start(), calls=%async_computation | async-start | bytes 4456448 | tf_op jit(solution)/shard_map/all_gather | solution.py:43
  7.9 588.5 %all-reduce.6.cloned.1.call-start = ((), (), s32[]{:S(2)}) async-start(), calls=%async_computation.2 | async-start | bytes 8388608
  129.1 6.3 collective-permute-start
  144.4 9.7 collective-permute-start.1
  162.6 16.6 %collective-permute-start.2 = (bf16[2,1,128,512]{3,2,0,1:T(8,128)(2,1)S(1)}, bf16[2,1,128,512]{3,2,0,1:T(8,128)(2,1)S(1)}, u32[]{:S(2)}, u32[]{:S(2)}) collective-permute-start(bf16[2,1,128,512]{3,2,0,1:T(8,128)(2,1)S(1)} %fusion.80), channel_id=1, source_target_pairs={{0,4},{1,5},{2,6},{3,7},{4,0},{5,1},{6,2},{7,3},{8,12},{9,13},{10,... | collective-permute-start | bytes 786440 | tf_op jit(solution)/shard_map/ppermute | solution.py:15
  164.5 4.6 copy-start.10
  169.1 10.9 copy-start.5
  183.9 8.3 copy-start.11
  186.4 12.3 %copy-start.7 = (bf16[1,128,512]{2,1,0:T(8,128)(2,1)S(1)}, bf16[1,128,512]{2,1,0:T(8,128)(2,1)}, u32[]{:S(2)}) copy-start(bf16[1,128,512]{2,1,0:T(8,128)(2,1)} %get-tuple-element.27) | copy-start | bytes 393220
  187.2 29.6 %collective-permute-start.3 = (bf16[2,1,128,512]{3,2,0,1:T(8,128)(2,1)}, bf16[2,1,128,512]{3,2,0,1:T(8,128)(2,1)}, u32[]{:S(2)}, u32[]{:S(2)}) collective-permute-start(bf16[2,1,128,512]{3,2,0,1:T(8,128)(2,1)} %fusion.81), channel_id=1, source_target_pairs={{0,8},{1,9},{2,10},{3,11},{4,12},{5,13},{6,14},{7,15},{8,0},{9,1},... | collective-permute-start | bytes 786440 | tf_op jit(solution)/shard_map/ppermute | solution.py:15
  203.4 25.3 %copy-start.18 = (bf16[1,128,128]{1,2,0:T(8,128)(2,1)}, bf16[1,128,128]{1,2,0:T(8,128)(2,1)S(1)}, u32[]{:S(2)}) copy-start(bf16[1,128,128]{1,2,0:T(8,128)(2,1)S(1)} %copy.107) | copy-start | bytes 98308
  218.6 5.9 copy-start.15
  243.1 10.6 copy-start.14
  299.7 5.4 copy-start.16
  299.7 22.1 %collective-permute-start.4 = (bf16[2,1,128,512]{3,2,0,1:T(8,128)(2,1)}, bf16[2,1,128,512]{3,2,0,1:T(8,128)(2,1)}, u32[]{:S(2)}, u32[]{:S(2)}) collective-permute-start(bf16[2,1,128,512]{3,2,0,1:T(8,128)(2,1)} %get-tuple-element.3), channel_id=1, source_target_pairs={{0,8},{1,9},{2,10},{3,11},{4,12},{5,13},{6,14},{7,15},{8,0},{9,1},... | collective-permute-start | bytes 786440 | tf_op jit(solution)/shard_map/ppermute | solution.py:15
  329.2 14.0 %collective-permute-start.5 = (bf16[2,1,128,512]{3,2,0,1:T(8,128)(2,1)}, bf16[2,1,128,512]{3,2,0,1:T(8,128)(2,1)}, u32[]{:S(2)}, u32[]{:S(2)}) collective-permute-start(bf16[2,1,128,512]{3,2,0,1:T(8,128)(2,1)} %add_convert_fusion.2), channel_id=1, source_target_pairs={{0,4},{1,5},{2,6},{3,7},{4,0},{5,1},{6,2},{7,3},{8,12},{9,13},{10,... | collective-permute-start | bytes 786440 | tf_op jit(solution)/shard_map/ppermute | solution.py:15
  350.9 6.2 copy-start.17
  350.9 6.9 copy-start.19
  350.9 11.3 collective-permute-start.6
  367.9 6.3 copy-start.2
  367.9 6.3 copy-start.4
  369.5 4.7 collective-permute-start.7
  387.0 764.9 %all-reduce.4.cloned.1.call-start = ((), (), s32[]{:S(2)}) async-start(), calls=%async_computation.1 | async-start | bytes 524288 | tf_op jit(solution)/shard_map/psum | solution.py:173
  (7 other events, 12.7 us)
Sparse Core Ops, SparseCore 0:
  10.1 110.1 all-gather.1
  387.1 209.2 all-reduce.5
  599.9 551.9 all-reduce.3
where the time goes:
time: 1180 us; the launch traced here: 1160 us
  waiting for transfers between devices  920 us (78%)
  local copies, waits for them, and re-layouts  103 us (9%)
  matrix products  72.5 us (6%)
  other arithmetic  28.4 us (2%)
  starting transfers between devices  22.3 us (2%)
  between operations  14.8 us (1%)
    psum x1, waiting for transfers between devices, per_device(): summed = lax.psum(partial_value, 'dp').astype(jnp.float32)  551 us
    unnamed x4, waiting for transfers between devices  205 us
    all_gather x1, waiting for transfers between devices, per_device(): gathered = lax.all_gather(stacked, 'seq', axis=0, tiled=True)  112 us
    ppermute x8, waiting for transfers between devices, partner_2(): lax.ppermute(value, axis, [(i, i ^ 1 << bit) for i in range(lax.axis_size...  50.4 us
  transfers between devices with their start and end apart: 11, of which 9 were waited for; matrix products, arithmetic and copies ran while one was open for 4% of the time, Pallas kernels for 0%

commit v1 on v0

v1 whole, which is shorter than its diff:
```python
import functools
import math

import jax
import jax.numpy as jnp
import numpy as np
from jax import lax
from jax.experimental import pallas as pl
from jax.experimental.pallas import tpu as pltpu
from jax.sharding import PartitionSpec as P

HEAD = 64
LOG_TWO = math.log(2.0)
BF = jnp.bfloat16
F32 = jnp.float32

ROW_LEVELS = ((0, 256, 0), (256, 320, 2), (320, 384, 3), (384, 512, 1), (512, 576, 2), (576, 640, 3))


def nn(a, b):
    return lax.dot_general(a, b, (((1,), (0,)), ((), ())), preferred_element_type=F32)


def nt(a, b):
    return lax.dot_general(a, b, (((1,), (1,)), ((), ())), preferred_element_type=F32)


def layer_kernel(nx, ny, pos_ref, tok_ref, tokt_ref, g_ref, gt_ref, w0, p1, p2, p3, p4, m1, m2, m3, m4,
                 w_ref, part_ref, lown_ref, lsend_ref, dq_ref, gown_ref, gkeep_ref, gsend_ref,
                 kv_s, kvt_s, qm_s, gm_s, gkv_s, attt_s, dqt_s, att_s):
    zl = pos_ref[0]
    core = pos_ref[1]

    def place(index, piece):
        row = pl.multiple_of(lax.rem(zl + index + 8, 8) * 128, 128)
        w_ref[pl.ds(row, 128), :] = piece

    place(0, w0[...])
    for index, piece in ((1, p1), (2, p2), (3, p3), (-1, m1), (-2, m2), (-3, m3)):
        place(index, piece[...])
    place(4, jnp.concatenate([p4[...], m4[...]], axis=0))

    def project_keys(step, carry):
        row = pl.multiple_of(step * 128, 128)
        block = nn(tok_ref[pl.ds(row, 128), :], w_ref[:, 256:768])
        kv_s[pl.ds(row, 128), :] = block.astype(BF)
        kvt_s[:, pl.ds(row, 128)] = block.T.astype(BF)
        return carry

    lax.fori_loop(0, 5, project_keys, 0)
    queries = nn(tok_ref[0:256, :], w_ref[:, 0:256]) * 0.125
    grads = nn(g_ref[...], w_ref[:, 768:1024])
    lane = lax.broadcasted_iota(jnp.int32, (256, 128), 1)
    for head in range(4):
        pair = (head // 2) * 128
        mine = (lane >= 64) if head % 2 else (lane < 64)
        qm_s[head] = jnp.where(mine, queries[:, pair:pair + 128], 0.0).astype(BF)
        gm_s[head] = jnp.where(mine, grads[:, pair:pair + 128], 0.0).astype(BF)

    for pair in range(2):
        kcol = pair * 128
        vcol = 256 + pair * 128
        key_grad = None
        value_grad = None
        for half in range(2):
            head = 2 * pair + half
            qm = qm_s[head]
            gm = gm_s[head]
            raw = nt(kv_s[:, kcol:kcol + 128], qm)
            scores = jnp.concatenate(
                [raw[lo:hi] + level * LOG_TWO if level else raw[lo:hi] for lo, hi, level in ROW_LEVELS], axis=0)
            exponent = jnp.exp(scores - jnp.max(scores, axis=0, keepdims=True))
            weights = exponent * (1.0 / jnp.sum(exponent, axis=0, keepdims=True))
            low = weights.astype(BF)
            dprobs = nt(kv_s[:, vcol:vcol + 128], gm)
            rowdot = jnp.sum(weights * dprobs, axis=0, keepdims=True)
            dscore = (weights * (dprobs - rowdot)).astype(BF)
            rows = slice(head * 64, head * 64 + 64)
            attt_s[rows, :] = nn(kvt_s[256 + head * 64:320 + head * 64, :], low)
            dqt_s[rows, :] = nn(kvt_s[rows, :], dscore) * 0.125
            new_key = nn(dscore, qm)
            new_value = nn(low, gm)
            key_grad = new_key if key_grad is None else key_grad + new_key
            value_grad = new_value if value_grad is None else value_grad + new_value
        for col, grad in ((kcol, key_grad), (vcol, value_grad)):
            cols = slice(col, col + 128)
            gown_ref[:, cols] = grad[0:256]
            gkeep_ref[:, cols] = grad[256:384]
            gkv_s[:, cols] = grad.astype(BF)

    gsend_ref[...] = gkv_s[384:640, :]
    dq_ref[...] = dqt_s[...].T.astype(BF)
    attended = attt_s[...].T.astype(BF)
    att_s[0] = attended[0:128]
    att_s[1] = attended[128:256]

    x_rows = 64 // nx
    y_cols = 1024 // ny

    def grad_rows(step, carry):
        rows = pl.ds(pl.multiple_of(step * 128, 128), 128)
        lhs = tokt_ref[rows, :]
        att_all = jnp.concatenate([att_s[0], att_s[1]], axis=0)
        block = jnp.concatenate(
            [nn(lhs[:, 0:256], dq_ref[...]).astype(BF), nn(lhs, gkv_s[...]).astype(BF),
             nn(gt_ref[rows, :], att_all).astype(BF)], axis=1)
        for side in range(2):
            for x in range(nx):
                for y in range(ny):
                    part_ref[x * ny + y, 2 * step + side] = block[
                        side * 64 + x * x_rows:side * 64 + (x + 1) * x_rows, y * y_cols:(y + 1) * y_cols]
        return carry

    lax.fori_loop(0, 8, grad_rows, 0)
    lown_ref[...] = nt(att_s[core], w_ref[:, 768:1024])
    lsend_ref[...] = nt(att_s[1 - core], w_ref[:, 768:1024]).astype(BF)


def run_layer(nx, ny, *operands):
    vmem = pl.BlockSpec(memory_space=pltpu.VMEM)
    smem = pl.BlockSpec(memory_space=pltpu.SMEM)
    shape = jax.ShapeDtypeStruct
    return pl.pallas_call(
        functools.partial(layer_kernel, nx, ny),
        out_shape=(
            shape((1024, 1024), BF),
            shape((nx * ny, 16, 64 // nx, 1024 // ny), BF),
            shape((128, 1024), F32),
            shape((128, 1024), BF),
            shape((256, 256), BF),
            shape((256, 512), F32),
            shape((128, 512), F32),
            shape((256, 512), BF),
        ),
        in_specs=[smem] + [vmem] * (len(operands) - 1),
        out_specs=tuple([vmem] * 8),
        scratch_shapes=[
            pltpu.VMEM((640, 512), BF),
            pltpu.VMEM((512, 640), BF),
            pltpu.VMEM((4, 256, 128), BF),
            pltpu.VMEM((4, 256, 128), BF),
            pltpu.VMEM((640, 512), BF),
            pltpu.VMEM((256, 256), F32),
            pltpu.VMEM((256, 256), F32),
            pltpu.VMEM((2, 128, 256), BF),
        ],
        compiler_params=pltpu.CompilerParams(vmem_limit_bytes=40 * 1024 * 1024),
        cost_estimate=pl.CostEstimate(flops=3_500_000_000, bytes_accessed=14_000_000, transcendentals=700_000),
    )(*operands)


def coarsening():
    matrix = np.zeros((224, 256), np.float32)
    base = 0
    for level in (1, 2, 3):
        for row in range(256 >> level):
            matrix[base + row, row << level:(row + 1) << level] = 0.5 ** level
        base += 256 >> level
    return matrix


def make_device(nx, ny, dp_count, seq_count):
    nxy = nx * ny
    nzh = dp_count // nxy
    ring = nzh * 8
    core_pairs = [(i, i ^ 1) for i in range(seq_count)]

    def chip_swap(bit):
        return [(i, i ^ (2 << bit)) for i in range(seq_count)]

    def along_z(shift):
        pairs = []
        for z in range(ring):
            source = (z + shift) % ring
            for xy in range(nxy):
                for core in range(2):
                    pairs.append((((source // 8) * nxy + xy) * seq_count + (source % 8) * 2 + core,
                                  ((z // 8) * nxy + xy) * seq_count + (z % 8) * 2 + core))
        return pairs

    plus, minus = along_z(1), along_z(-1)
    plane_groups = [[zh * nxy + xy for xy in range(nxy)] for zh in range(nzh)]
    zh_pairs = [(zh * nxy + xy, ((zh + 1) % nzh) * nxy + xy) for zh in range(nzh) for xy in range(nxy)]
    coarse_matrix = coarsening()

    def swap_core(value):
        return lax.ppermute(value, "seq", core_pairs)

    def per_device(tokens, grad_out, stacked):
        seq = lax.axis_index("seq")
        zl = seq >> 1
        core = seq & 1
        first = core == 0

        def ordered(mine, other, axis):
            return jnp.where(first, jnp.concatenate([mine, other], axis), jnp.concatenate([other, mine], axis))

        shard = stacked.reshape(64, 4, 2, 256)
        keep = lax.dynamic_index_in_dim(shard, core, 2, False).reshape(64, 1024)
        give = lax.dynamic_index_in_dim(shard, 1 - core, 2, False).reshape(64, 1024)
        w0 = ordered(keep, swap_core(give), 0)
        both = ("dp", "seq")
        p1 = lax.ppermute(w0, both, plus)
        m1 = lax.ppermute(w0, both, minus)
        p2 = lax.ppermute(p1, both, plus)
        m2 = lax.ppermute(m1, both, minus)
        p3 = lax.ppermute(p2, both, plus)
        m3 = lax.ppermute(m2, both, minus)
        p4 = lax.ppermute(p3[0:64], both, plus)
        m4 = lax.ppermute(m3[64:128], both, minus)

        own = jnp.concatenate([tokens[0], grad_out[0]], axis=0)
        got = swap_core(own)
        chip_tokens = ordered(own[0:128], got[0:128], 0)
        chip_grads = ordered(own[128:256], got[128:256], 0)
        matrix = jnp.asarray(coarse_matrix, BF)
        half_tokens = lax.dynamic_slice(chip_tokens, (0, core * 512), (256, 512))
        coarse = nn(matrix, half_tokens).astype(BF)
        c1, c2, c3 = coarse[0:128], coarse[128:192], coarse[192:224]
        r3 = lax.ppermute(c3, "seq", chip_swap(2))
        second = lax.ppermute(jnp.concatenate([c2, r3], 0), "seq", chip_swap(1))
        held = jnp.concatenate([second[0:64], r3, second[64:96]], 0)
        third = lax.ppermute(jnp.concatenate([c1, held], 0), "seq", chip_swap(0))
        half_set = jnp.concatenate([held, third], 0)
        rest = ordered(half_set, swap_core(half_set), 1)
        token_set = jnp.concatenate([chip_tokens, rest], 0)

        position = jnp.stack([zl, core]).astype(jnp.int32)
        (weight, part, layer_own, layer_send, dquery, grad_own, grad_keep, grad_send) = run_layer(
            nx, ny, position, token_set, token_set.T, chip_grads, chip_grads.T,
            w0, p1, p2, p3, p4, m1, m2, m3, m4)

        if nxy > 1:
            pieces = lax.all_to_all(part, "dp", 0, 0, axis_index_groups=plane_groups, tiled=True)
        else:
            pieces = part
        plane_sum = jnp.sum(pieces.astype(F32), axis=0).astype(BF)
        columns = lax.all_to_all(plane_sum, "seq", 0, 0, tiled=True)
        rows, cols = 64 // nx, 1024 // ny
        line_sum = jnp.sum(columns.astype(F32).reshape(8, 2, rows, cols), axis=0).astype(BF)
        if nzh > 1:
            other_half = lax.ppermute(line_sum, "dp", zh_pairs)
            line_sum = (line_sum.astype(F32) + other_half.astype(F32)).astype(BF)
        spread = jnp.broadcast_to(line_sum[None], (nxy, 2, rows, cols))
        if nxy > 1:
            spread = lax.all_to_all(spread, "dp", 0, 0, axis_index_groups=plane_groups, tiled=True)
        slots = 4 // ny
        full = spread.reshape(nx, ny, 2, rows, slots, 256).transpose(0, 3, 1, 4, 2, 5).reshape(64, 4, 512)
        total = 128 * seq_count * dp_count
        grad_weights = full.astype(F32) * (1.0 / math.sqrt(total))

        layer_out = (layer_own + swap_core(layer_send).astype(F32)).astype(BF)

        b1 = lax.ppermute(grad_send, "seq", chip_swap(0))
        joined = grad_keep + b1[128:256].astype(F32)
        b2 = lax.ppermute(jnp.concatenate([joined[0:64], joined[96:128]], 0).astype(BF), "seq", chip_swap(1))
        b3 = lax.ppermute((joined[64:96] + b2[64:96].astype(F32)).astype(BF), "seq", chip_swap(2))
        returned = jnp.concatenate([b1[0:128], b2[0:64], b3], 0)
        dkv = (grad_own + nn(jnp.asarray(coarse_matrix.T, BF), returned)).astype(BF)
        back = jnp.concatenate([dquery, dkv], axis=1)
        partial = nt(back, weight[:, 0:768])
        mine = lax.dynamic_slice(partial, (core * 128, 0), (128, 1024))
        theirs = lax.dynamic_slice(partial, ((1 - core) * 128, 0), (128, 1024)).astype(BF)
        grad_tokens = (mine + swap_core(theirs).astype(F32)).astype(BF)
        return layer_out[None], grad_tokens[None], grad_weights

    return per_device


def solution(mesh):
    dp_count, seq_count = mesh.shape["dp"], mesh.shape["seq"]
    side = 4 if dp_count >= 16 else (2 if dp_count >= 4 else 1)
    specs = (P("dp", "seq", None), P("dp", "seq", None), P("seq", None, None))
    return jax.shard_map(
        make_device(side, side, dp_count, seq_count),
        mesh=mesh, in_specs=specs, out_specs=specs, check_vma=False)
```

time: 1180 us -> 200 us (0.17); the launches traced: 1160 us -> 198 us
  waiting for transfers between devices: 920 us -> 41.1 us
  starting transfers between devices: 22.3 us -> 105 us
  local copies, waits for them, and re-layouts: 103 us -> 27.8 us
  matrix products: 72.5 us -> 2.48 us
  other arithmetic: 28.4 us -> 10 us
  between operations: 14.8 us -> 1.39 us
    psum x1 -> x0, waiting for transfers between devices: 551 us -> none  [per_device(): summed = lax.psum(partial_value, 'dp').astype(jnp.float32)]
    unnamed x4 -> x0, waiting for transfers between devices: 205 us -> none
    all_gather x1 -> x0, waiting for transfers between devices: 112 us -> none  [per_device(): gathered = lax.all_gather(stacked, 'seq', axis=0, tiled=True)]
    dot_general x26 -> x5, matrix products: 63.8 us -> 2.48 us  [the longest x1 1.62 us: nt(): lax.dot_general(a, b, (((1,), (1,)), ((), ())), preferred_element_type=F32)]
    ppermute x8 -> x20, starting transfers between devices: 22.2 us -> 79.7 us  [the longest x5 21.9 us: swap_core(): return lax.ppermute(value, 'seq', core_pairs)]
    slice x24 -> x9, local copies, waits for them, and re-layouts: 40.5 us -> 1.69 us  [the longest x1 0.72 us: per_device(): p4 = lax.ppermute(p3[0:64], both, plus)]
    all_to_all x0 -> x3, starting transfers between devices: none -> 24.8 us  [the longest x1 12.6 us: per_device(): columns = lax.all_to_all(plane_sum, 'seq', 0, 0, tiled=True)]
    ppermute x8 -> x20, waiting for transfers between devices: 50.4 us -> 25.9 us  [the longest x1 9.46 us: per_device(): r3 = lax.ppermute(c3, 'seq', chip_swap(2))]
  transfers between devices with their start and end apart: 11 -> 23, of which waited for: 9 -> 10; matrix products, arithmetic and copies ran while one was open for 4% -> 10% of each run, Pallas kernels for 0% -> 0%
where the time goes in v1:
time: 200 us; the launch traced here: 198 us
  starting transfers between devices  105 us (52%)
  waiting for transfers between devices  41.1 us (21%)
  local copies, waits for them, and re-layouts  27.8 us (14%)
  Pallas kernels  10.7 us (5%)
  other arithmetic  10 us (5%)
  matrix products  2.48 us (1%)
    ppermute x5, starting transfers between devices, swap_core(): return lax.ppermute(value, 'seq', core_pairs)  21.9 us
    unnamed x80, local copies, waits for them, and re-layouts  19.8 us
    all_to_all x1, starting transfers between devices, per_device(): columns = lax.all_to_all(plane_sum, 'seq', 0, 0, tiled=True)  12.6 us
    pallas_call x1, Pallas kernels, run_layer(): pl.pallas_call(functools.partial(layer_kernel, nx, ny), out_shape=(shape(...  10.7 us
    all_to_all x1, waiting for transfers between devices, per_device(): columns = lax.all_to_all(plane_sum, 'seq', 0, 0, tiled=True)  10.4 us
    ppermute x1, waiting for transfers between devices, per_device(): r3 = lax.ppermute(c3, 'seq', chip_swap(2))  9.46 us
    all_to_all x1, starting transfers between devices, per_device(): lax.all_to_all(part, 'dp', 0, 0, axis_index_groups=plane_groups, tiled=True)  6.94 us
    ppermute x1, starting transfers between devices, per_device(): p1 = lax.ppermute(w0, both, plus)  6.65 us
  transfers between devices with their start and end apart: 23, of which 10 were waited for; matrix products, arithmetic and copies ran while one was open for 10% of the time, Pallas kernels for 0%

profile of v1, /device:TPU:1, one launch (start us, length us, event | category | flops | bytes accessed | tf_op | source)
XLA Modules:
  0.0 198.1 jit_solution(7488839651830815275)
XLA Ops:
  3.0 8.9 %collective-permute-start = (bf16[256,1024]{0,1:T(8,128)(2,1)S(1)}, bf16[256,1024]{0,1:T(8,128)(2,1)S(1)}, u32[]{:S(2)}, u32[]{:S(2)}) collective-permute-start(bf16[256,1024]{0,1:T(8,128)(2,1)S(1)} %pad_maximum_fusion.2), channel_id=1, source_target_pairs={{0,1},{1,0},{2,3},{3,2},{4,5},{5,4},{6,7},{7,6},{8,9},{9,8},{10,11... | collective-permute-start | bytes 1572872 | tf_op jit(solution)/shard_map/ppermute | solution.py:187
  15.0 3.4 %collective-permute-start.1 = (bf16[32,512]{0,1:T(8,128)(2,1)S(1)}, bf16[32,512]{0,1:T(8,128)(2,1)S(1)}, u32[]{:S(2)}, u32[]{:S(2)}) collective-permute-start(bf16[32,512]{0,1:T(8,128)(2,1)S(1)} %slice.75), channel_id=1, source_target_pairs={{0,8},{1,9},{2,10},{3,11},{4,12},{5,13},{6,14},{7,15},{8,0},{9,1},... | collective-permute-start | bytes 98312 | tf_op jit(solution)/shard_map/ppermute | solution.py:220
  20.1 2.6 %collective-permute-start.5 = (bf16[64,1024]{1,0:T(8,128)(2,1)S(1)}, bf16[64,1024]{1,0:T(8,128)(2,1)S(1)}, u32[]{:S(2)}, u32[]{:S(2)}) collective-permute-start(bf16[64,1024]{1,0:T(8,128)(2,1)S(1)} %bitcast.45), channel_id=1, source_target_pairs={{0,1},{1,0},{2,3},{3,2},{4,5},{5,4},{6,7},{7,6},{8,9},{9,8},{10,11... | collective-permute-start | bytes 393224 | tf_op jit(solution)/shard_map/ppermute | solution.py:187
  22.7 9.5 %collective-permute-done.1 = bf16[32,512]{0,1:T(8,128)(2,1)S(1)} collective-permute-done((bf16[32,512]{0,1:T(8,128)(2,1)S(1)}, bf16[32,512]{0,1:T(8,128)(2,1)S(1)}, u32[]{:S(2)}, u32[]{:S(2)}) %collective-permute-start.1) | collective-permute-done | bytes 32800 | tf_op jit(solution)/shard_map/ppermute | solution.py:220
  34.3 3.1 %collective-permute-start.10 = (bf16[128,1024]{1,0:T(8,128)(2,1)S(1)}, bf16[128,1024]{1,0:T(8,128)(2,1)S(1)}, u32[]{:S(2)}, u32[]{:S(2)}) collective-permute-start(bf16[128,1024]{1,0:T(8,128)(2,1)S(1)} %maximum_select_fusion.1.w0), channel_id=1, source_target_pairs={{270,0},{271,1},{286,16},{287,17},{302,32},{303,33},{318,48},{319,... | collective-permute-start | bytes 786440 | tf_op jit(solution)/shard_map/ppermute | solution.py:204
  37.4 6.7 %collective-permute-start.6 = (bf16[128,1024]{1,0:T(8,128)(2,1)S(1)}, bf16[128,1024]{1,0:T(8,128)(2,1)S(1)}, u32[]{:S(2)}, u32[]{:S(2)}) collective-permute-start(bf16[128,1024]{1,0:T(8,128)(2,1)S(1)} %maximum_select_fusion.1.w0), channel_id=1, source_target_pairs={{2,0},{3,1},{18,16},{19,17},{34,32},{35,33},{50,48},{51,49},{66,64... | collective-permute-start | bytes 786440 | tf_op jit(solution)/shard_map/ppermute | solution.py:203
  50.3 6.0 %collective-permute-start.7 = (bf16[128,1024]{1,0:T(8,128)(2,1)S(1)}, bf16[128,1024]{1,0:T(8,128)(2,1)S(1)}, u32[]{:S(2)}, u32[]{:S(2)}) collective-permute-start(bf16[128,1024]{1,0:T(8,128)(2,1)S(1)} %collective-permute-done.6.p1), channel_id=1, source_target_pairs={{2,0},{3,1},{18,16},{19,17},{34,32},{35,33},{50,48},{51,49},{66,64... | collective-permute-start | bytes 786440 | tf_op jit(solution)/shard_map/ppermute | solution.py:205
  57.4 2.8 %collective-permute-start.4 = (bf16[384,512]{0,1:T(8,128)(2,1)}, bf16[384,512]{0,1:T(8,128)(2,1)S(1)}, u32[]{:S(2)}, u32[]{:S(2)}) collective-permute-start(bf16[384,512]{0,1:T(8,128)(2,1)} %pad_maximum_fusion.4), channel_id=1, source_target_pairs={{0,1},{1,0},{2,3},{3,2},{4,5},{5,4},{6,7},{7,6},{8,9},{9,8},{10,11... | collective-permute-start | bytes 1179656 | tf_op jit(solution)/shard_map/ppermute | solution.py:187
  62.5 4.6 %collective-permute-start.8 = (bf16[128,1024]{1,0:T(8,128)(2,1)S(1)}, bf16[128,1024]{1,0:T(8,128)(2,1)S(1)}, u32[]{:S(2)}, u32[]{:S(2)}) collective-permute-start(bf16[128,1024]{1,0:T(8,128)(2,1)S(1)} %collective-permute-done.7.p2), channel_id=1, source_target_pairs={{2,0},{3,1},{18,16},{19,17},{34,32},{35,33},{50,48},{51,49},{66,64... | collective-permute-start | bytes 786440 | tf_op jit(solution)/shard_map/ppermute | solution.py:207
  73.7 4.6 %collective-permute-start.9 = (bf16[64,1024]{1,0:T(8,128)(2,1)}, bf16[64,1024]{1,0:T(8,128)(2,1)S(1)}, u32[]{:S(2)}, u32[]{:S(2)}) collective-permute-start(bf16[64,1024]{1,0:T(8,128)(2,1)} %slice.80), channel_id=1, source_target_pairs={{2,0},{3,1},{18,16},{19,17},{34,32},{35,33},{50,48},{51,49},{66,64... | collective-permute-start | bytes 393224 | tf_op jit(solution)/shard_map/ppermute | solution.py:209
  91.1 10.7 %shard_map.76 = (bf16[1024,1024]{1,0:T(8,128)(2,1)S(1)}, bf16[16,16,16,256]{3,2,1,0:T(8,128)(2,1)}, f32[128,1024]{1,0:T(8,128)S(1)}, bf16[128,1024]{1,0:T(8,128)...) custom-call(s32[2]{0:T(128)S(1)} %pad_add_fusion.pos_ref, ...), custom_call_target="tpu_custom_call" | custom-call | flops 3500000000 | bytes 14000000 | tf_op jit(solution)/shard_map/pallas_call | solution.py:123
  106.8 6.9 %all-to-all-start = ((bf16[16,16,16,256]{3,2,1,0:T(8,128)(2,1)}), bf16[16,16,16,256]{3,2,1,0:T(8,128)(2,1)}, u32[]{:S(2)}, u32[]{:S(2)}) async-start(bf16[16,16,16,256]{3,2,1,0:T(8,128)(2,1)} %get-tuple-element.18), calls=%async_computation | async-start | bytes 4194304 | tf_op jit(solution)/shard_map/all_to_all | solution.py:234
  115.8 5.6 %collective-permute-done.15 = bf16[256,512]{1,0:T(8,128)(2,1)S(1)} collective-permute-done((bf16[256,512]{1,0:T(8,128)(2,1)S(1)}, bf16[256,512]{1,0:T(8,128)(2,1)S(1)}, u32[]{:S(2)}, u32[]{:S(2)}) %collective-permute-start.15) | collective-permute-done | bytes 262176 | tf_op jit(solution)/shard_map/ppermute | solution.py:254
  121.5 5.0 %collective-permute-start.16 = (bf16[96,512]{1,0:T(8,128)(2,1)S(1)}, bf16[96,512]{1,0:T(8,128)(2,1)S(1)}, u32[]{:S(2)}, u32[]{:S(2)}) collective-permute-start(bf16[96,512]{1,0:T(8,128)(2,1)S(1)} %pad_maximum_fusion.7), channel_id=1, source_target_pairs={{0,4},{1,5},{2,6},{3,7},{4,0},{5,1},{6,2},{7,3},{8,12},{9,13},{10,... | collective-permute-start | bytes 294920 | tf_op jit(solution)/shard_map/ppermute | solution.py:256
  126.5 5.2 %collective-permute-start.14 = (bf16[128,1024]{1,0:T(8,128)(2,1)S(1)}, bf16[128,1024]{1,0:T(8,128)(2,1)}, u32[]{:S(2)}, u32[]{:S(2)}) collective-permute-start(bf16[128,1024]{1,0:T(8,128)(2,1)S(1)} %copy-done.12), channel_id=1, source_target_pairs={{0,1},{1,0},{2,3},{3,2},{4,5},{5,4},{6,7},{7,6},{8,9},{9,8},{10,11... | collective-permute-start | bytes 786440 | tf_op jit(solution)/shard_map/ppermute | solution.py:187
  131.7 6.1 %collective-permute-start.17 = (bf16[32,512]{1,0:T(8,128)(2,1)S(1)}, bf16[32,512]{1,0:T(8,128)(2,1)S(1)}, u32[]{:S(2)}, u32[]{:S(2)}) collective-permute-start(bf16[32,512]{1,0:T(8,128)(2,1)S(1)} %fusion.13), channel_id=1, source_target_pairs={{0,8},{1,9},{2,10},{3,11},{4,12},{5,13},{6,14},{7,15},{8,0},{9,1},... | collective-permute-start | bytes 98312 | tf_op jit(solution)/shard_map/ppermute | solution.py:257
  138.1 2.7 %collective-permute-done.17 = bf16[32,512]{1,0:T(8,128)(2,1)S(1)} collective-permute-done((bf16[32,512]{1,0:T(8,128)(2,1)S(1)}, bf16[32,512]{1,0:T(8,128)(2,1)S(1)}, u32[]{:S(2)}, u32[]{:S(2)}) %collective-permute-start.17) | collective-permute-done | bytes 32800 | tf_op jit(solution)/shard_map/ppermute | solution.py:257
  141.2 2.7 %reduce_sum.21 = bf16[16,16,256]{2,1,0:T(8,128)(2,1)} reduce(bf16[16,16,16,256]{3,2,1,0:T(8,128)(2,1)} %all-to-all-done, bf16[]{:T(256)} %constant.32.clone.1), dimensions={0}, to_apply=%region_0.1 | reduce | flops 983040 | bytes 2228226 | tf_op jit(solution)/shard_map/reduce_sum | solution.py:237
  143.9 12.6 %all-to-all-start.1 = ((bf16[16,16,256]{2,1,0:T(8,128)(2,1)}), bf16[16,16,256]{2,1,0:T(8,128)(2,1)}, u32[]{:S(2)}, u32[]{:S(2)}) async-start(bf16[16,16,256]{2,1,0:T(8,128)(2,1)} %reduce_sum.21), calls=%async_computation.1 | async-start | bytes 262144 | tf_op jit(solution)/shard_map/all_to_all | solution.py:238
  158.3 10.4 %all-to-all-done.1 = bf16[16,16,256]{2,1,0:T(8,128)(2,1)} async-done(((bf16[16,16,256]{2,1,0:T(8,128)(2,1)}), bf16[16,16,256]{2,1,0:T(8,128)(2,1)}, u32[]{:S(2)}, u32[]{:S(2)}) %all-to-all-start.1) | async-done | bytes 131104 | tf_op jit(solution)/shard_map/all_to_all | solution.py:238
  169.6 6.2 %collective-permute-start.19 = (bf16[2,16,256]{2,1,0:T(8,128)(2,1)S(1)}, bf16[2,16,256]{2,1,0:T(8,128)(2,1)S(1)}, u32[]{:S(2)}, u32[]{:S(2)}) collective-permute-start(bf16[2,16,256]{2,1,0:T(8,128)(2,1)S(1)} %reduce.1), channel_id=1, source_target_pairs={{0,256},{16,272},{32,288},{48,304},{64,320},{80,336},{96,352},{112... | collective-permute-start | bytes 49160 | tf_op jit(solution)/shard_map/ppermute | solution.py:242
  179.4 3.6 %collective-permute-done.19 = bf16[2,16,256]{2,1,0:T(8,128)(2,1)S(1)} collective-permute-done((bf16[2,16,256]{2,1,0:T(8,128)(2,1)S(1)}, bf16[2,16,256]{2,1,0:T(8,128)(2,1)S(1)}, u32[]{:S(2)}, u32[]{:S(2)}) %collective-permute-start.19) | collective-permute-done | bytes 16416 | tf_op jit(solution)/shard_map/ppermute | solution.py:242
  183.7 5.3 %all-to-all-start.2 = ((bf16[16,2,16,256]{3,2,1,0:T(8,128)(2,1)}), bf16[16,2,16,256]{3,2,1,0:T(8,128)(2,1)S(1)}, u32[]{:S(2)}, u32[]{:S(2)}) async-start(bf16[16,2,16,256]{3,2,1,0:T(8,128)(2,1)} %broadcast_in_dim.14), calls=%async_computation.2 | async-start | bytes 524288 | tf_op jit(solution)/shard_map/all_to_all | solution.py:246
  191.5 4.8 %all-to-all-done.2 = bf16[16,2,16,256]{3,2,1,0:T(8,128)(2,1)S(1)} async-done(((bf16[16,2,16,256]{3,2,1,0:T(8,128)(2,1)}), bf16[16,2,16,256]{3,2,1,0:T(8,128)(2,1)S(1)}, u32[]{:S(2)}, u32[]{:S(2)}) %all-to-all-start.2) | async-done | bytes 262176 | tf_op jit(solution)/shard_map/all_to_all | solution.py:246
  (144 shorter events, 56.9 us)
Async XLA Ops:
  3.0 10.4 %collective-permute-start = (bf16[256,1024]{0,1:T(8,128)(2,1)S(1)}, bf16[256,1024]{0,1:T(8,128)(2,1)S(1)}, u32[]{:S(2)}, u32[]{:S(2)}) collective-permute-start(bf16[256,1024]{0,1:T(8,128)(2,1)S(1)} %pad_maximum_fusion.2), channel_id=1, source_target_pairs={{0,1},{1,0},{2,3},{3,2},{4,5},{5,4},{6,7},{7,6},{8,9},{9,8},{10,11... | collective-permute-start | bytes 1572872 | tf_op jit(solution)/shard_map/ppermute | solution.py:187
  15.0 17.2 %collective-permute-start.1 = (bf16[32,512]{0,1:T(8,128)(2,1)S(1)}, bf16[32,512]{0,1:T(8,128)(2,1)S(1)}, u32[]{:S(2)}, u32[]{:S(2)}) collective-permute-start(bf16[32,512]{0,1:T(8,128)(2,1)S(1)} %slice.75), channel_id=1, source_target_pairs={{0,8},{1,9},{2,10},{3,11},{4,12},{5,13},{6,14},{7,15},{8,0},{9,1},... | collective-permute-start | bytes 98312 | tf_op jit(solution)/shard_map/ppermute | solution.py:220
  20.1 14.1 %collective-permute-start.5 = (bf16[64,1024]{1,0:T(8,128)(2,1)S(1)}, bf16[64,1024]{1,0:T(8,128)(2,1)S(1)}, u32[]{:S(2)}, u32[]{:S(2)}) collective-permute-start(bf16[64,1024]{1,0:T(8,128)(2,1)S(1)} %bitcast.45), channel_id=1, source_target_pairs={{0,1},{1,0},{2,3},{3,2},{4,5},{5,4},{6,7},{7,6},{8,9},{9,8},{10,11... | collective-permute-start | bytes 393224 | tf_op jit(solution)/shard_map/ppermute | solution.py:187
  32.3 12.4 %collective-permute-start.2 = (bf16[96,512]{0,1:T(8,128)(2,1)S(1)}, bf16[96,512]{0,1:T(8,128)(2,1)S(1)}, u32[]{:S(2)}, u32[]{:S(2)}) collective-permute-start(bf16[96,512]{0,1:T(8,128)(2,1)S(1)} %pad_maximum_fusion.6), channel_id=1, source_target_pairs={{0,4},{1,5},{2,6},{3,7},{4,0},{5,1},{6,2},{7,3},{8,12},{9,13},{10,... | collective-permute-start | bytes 294920 | tf_op jit(solution)/shard_map/ppermute | solution.py:221
  34.3 13.5 %collective-permute-start.10 = (bf16[128,1024]{1,0:T(8,128)(2,1)S(1)}, bf16[128,1024]{1,0:T(8,128)(2,1)S(1)}, u32[]{:S(2)}, u32[]{:S(2)}) collective-permute-start(bf16[128,1024]{1,0:T(8,128)(2,1)S(1)} %maximum_select_fusion.1.w0), channel_id=1, source_target_pairs={{270,0},{271,1},{286,16},{287,17},{302,32},{303,33},{318,48},{319,... | collective-permute-start | bytes 786440 | tf_op jit(solution)/shard_map/ppermute | solution.py:204
  37.4 13.0 %collective-permute-start.6 = (bf16[128,1024]{1,0:T(8,128)(2,1)S(1)}, bf16[128,1024]{1,0:T(8,128)(2,1)S(1)}, u32[]{:S(2)}, u32[]{:S(2)}) collective-permute-start(bf16[128,1024]{1,0:T(8,128)(2,1)S(1)} %maximum_select_fusion.1.w0), channel_id=1, source_target_pairs={{2,0},{3,1},{18,16},{19,17},{34,32},{35,33},{50,48},{51,49},{66,64... | collective-permute-start | bytes 786440 | tf_op jit(solution)/shard_map/ppermute | solution.py:203
  45.0 11.4 %collective-permute-start.3 = (bf16[256,512]{0,1:T(8,128)(2,1)S(1)}, bf16[256,512]{0,1:T(8,128)(2,1)S(1)}, u32[]{:S(2)}, u32[]{:S(2)}) collective-permute-start(bf16[256,512]{0,1:T(8,128)(2,1)S(1)} %pad_maximum_fusion.5), channel_id=1, source_target_pairs={{0,2},{1,3},{2,0},{3,1},{4,6},{5,7},{6,4},{7,5},{8,10},{9,11},{10,... | collective-permute-start | bytes 786440 | tf_op jit(solution)/shard_map/ppermute | solution.py:223
  47.8 12.7 %collective-permute-start.11 = (bf16[128,1024]{1,0:T(8,128)(2,1)S(1)}, bf16[128,1024]{1,0:T(8,128)(2,1)S(1)}, u32[]{:S(2)}, u32[]{:S(2)}) collective-permute-start(bf16[128,1024]{1,0:T(8,128)(2,1)S(1)} %collective-permute-done.10.m1), channel_id=1, source_target_pairs={{270,0},{271,1},{286,16},{287,17},{302,32},{303,33},{318,48},{319,... | collective-permute-start | bytes 786440 | tf_op jit(solution)/shard_map/ppermute | solution.py:206
  50.3 12.1 %collective-permute-start.7 = (bf16[128,1024]{1,0:T(8,128)(2,1)S(1)}, bf16[128,1024]{1,0:T(8,128)(2,1)S(1)}, u32[]{:S(2)}, u32[]{:S(2)}) collective-permute-start(bf16[128,1024]{1,0:T(8,128)(2,1)S(1)} %collective-permute-done.6.p1), channel_id=1, source_target_pairs={{2,0},{3,1},{18,16},{19,17},{34,32},{35,33},{50,48},{51,49},{66,64... | collective-permute-start | bytes 786440 | tf_op jit(solution)/shard_map/ppermute | solution.py:205
  57.4 20.9 %collective-permute-start.4 = (bf16[384,512]{0,1:T(8,128)(2,1)}, bf16[384,512]{0,1:T(8,128)(2,1)S(1)}, u32[]{:S(2)}, u32[]{:S(2)}) collective-permute-start(bf16[384,512]{0,1:T(8,128)(2,1)} %pad_maximum_fusion.4), channel_id=1, source_target_pairs={{0,1},{1,0},{2,3},{3,2},{4,5},{5,4},{6,7},{7,6},{8,9},{9,8},{10,11... | collective-permute-start | bytes 1179656 | tf_op jit(solution)/shard_map/ppermute | solution.py:187
  60.5 9.8 %collective-permute-start.12 = (bf16[128,1024]{1,0:T(8,128)(2,1)S(1)}, bf16[128,1024]{1,0:T(8,128)(2,1)S(1)}, u32[]{:S(2)}, u32[]{:S(2)}) collective-permute-start(bf16[128,1024]{1,0:T(8,128)(2,1)S(1)} %collective-permute-done.11.m2), channel_id=1, source_target_pairs={{270,0},{271,1},{286,16},{287,17},{302,32},{303,33},{318,48},{319,... | collective-permute-start | bytes 786440 | tf_op jit(solution)/shard_map/ppermute | solution.py:208
  62.5 10.4 %collective-permute-start.8 = (bf16[128,1024]{1,0:T(8,128)(2,1)S(1)}, bf16[128,1024]{1,0:T(8,128)(2,1)S(1)}, u32[]{:S(2)}, u32[]{:S(2)}) collective-permute-start(bf16[128,1024]{1,0:T(8,128)(2,1)S(1)} %collective-permute-done.7.p2), channel_id=1, source_target_pairs={{2,0},{3,1},{18,16},{19,17},{34,32},{35,33},{50,48},{51,49},{66,64... | collective-permute-start | bytes 786440 | tf_op jit(solution)/shard_map/ppermute | solution.py:207
  71.0 10.8 %collective-permute-start.13 = (bf16[64,1024]{1,0:T(8,128)(2,1)}, bf16[64,1024]{1,0:T(8,128)(2,1)S(1)}, u32[]{:S(2)}, u32[]{:S(2)}) collective-permute-start(bf16[64,1024]{1,0:T(8,128)(2,1)} %slice.81), channel_id=1, source_target_pairs={{270,0},{271,1},{286,16},{287,17},{302,32},{303,33},{318,48},{319,... | collective-permute-start | bytes 393224 | tf_op jit(solution)/shard_map/ppermute | solution.py:210
  73.7 8.1 %collective-permute-start.9 = (bf16[64,1024]{1,0:T(8,128)(2,1)}, bf16[64,1024]{1,0:T(8,128)(2,1)S(1)}, u32[]{:S(2)}, u32[]{:S(2)}) collective-permute-start(bf16[64,1024]{1,0:T(8,128)(2,1)} %slice.80), channel_id=1, source_target_pairs={{2,0},{3,1},{18,16},{19,17},{34,32},{35,33},{50,48},{51,49},{66,64... | collective-permute-start | bytes 393224 | tf_op jit(solution)/shard_map/ppermute | solution.py:209
  106.8 34.4 %all-to-all-start = ((bf16[16,16,16,256]{3,2,1,0:T(8,128)(2,1)}), bf16[16,16,16,256]{3,2,1,0:T(8,128)(2,1)}, u32[]{:S(2)}, u32[]{:S(2)}) async-start(bf16[16,16,16,256]{3,2,1,0:T(8,128)(2,1)} %get-tuple-element.18), calls=%async_computation | async-start | bytes 4194304 | tf_op jit(solution)/shard_map/all_to_all | solution.py:234
  113.8 7.6 %collective-permute-start.15 = (bf16[256,512]{1,0:T(8,128)(2,1)S(1)}, bf16[256,512]{1,0:T(8,128)(2,1)S(1)}, u32[]{:S(2)}, u32[]{:S(2)}) collective-permute-start(bf16[256,512]{1,0:T(8,128)(2,1)S(1)} %copy-done.22), channel_id=1, source_target_pairs={{0,2},{1,3},{2,0},{3,1},{4,6},{5,7},{6,4},{7,5},{8,10},{9,11},{10,... | collective-permute-start | bytes 786440 | tf_op jit(solution)/shard_map/ppermute | solution.py:254
  121.5 10.2 %collective-permute-start.16 = (bf16[96,512]{1,0:T(8,128)(2,1)S(1)}, bf16[96,512]{1,0:T(8,128)(2,1)S(1)}, u32[]{:S(2)}, u32[]{:S(2)}) collective-permute-start(bf16[96,512]{1,0:T(8,128)(2,1)S(1)} %pad_maximum_fusion.7), channel_id=1, source_target_pairs={{0,4},{1,5},{2,6},{3,7},{4,0},{5,1},{6,2},{7,3},{8,12},{9,13},{10,... | collective-permute-start | bytes 294920 | tf_op jit(solution)/shard_map/ppermute | solution.py:256
  126.5 62.5 %collective-permute-start.14 = (bf16[128,1024]{1,0:T(8,128)(2,1)S(1)}, bf16[128,1024]{1,0:T(8,128)(2,1)}, u32[]{:S(2)}, u32[]{:S(2)}) collective-permute-start(bf16[128,1024]{1,0:T(8,128)(2,1)S(1)} %copy-done.12), channel_id=1, source_target_pairs={{0,1},{1,0},{2,3},{3,2},{4,5},{5,4},{6,7},{7,6},{8,9},{9,8},{10,11... | collective-permute-start | bytes 786440 | tf_op jit(solution)/shard_map/ppermute | solution.py:187
  131.7 9.0 %collective-permute-start.17 = (bf16[32,512]{1,0:T(8,128)(2,1)S(1)}, bf16[32,512]{1,0:T(8,128)(2,1)S(1)}, u32[]{:S(2)}, u32[]{:S(2)}) collective-permute-start(bf16[32,512]{1,0:T(8,128)(2,1)S(1)} %fusion.13), channel_id=1, source_target_pairs={{0,8},{1,9},{2,10},{3,11},{4,12},{5,13},{6,14},{7,15},{8,0},{9,1},... | collective-permute-start | bytes 98312 | tf_op jit(solution)/shard_map/ppermute | solution.py:257
  143.9 24.7 %all-to-all-start.1 = ((bf16[16,16,256]{2,1,0:T(8,128)(2,1)}), bf16[16,16,256]{2,1,0:T(8,128)(2,1)}, u32[]{:S(2)}, u32[]{:S(2)}) async-start(bf16[16,16,256]{2,1,0:T(8,128)(2,1)} %reduce_sum.21), calls=%async_computation.1 | async-start | bytes 262144 | tf_op jit(solution)/shard_map/all_to_all | solution.py:238
  158.3 32.4 %copy-start.31 = (f32[256,1024]{1,0:T(8,128)S(1)}, f32[256,1024]{1,0:T(8,128)}, u32[]{:S(2)}) copy-start(f32[256,1024]{1,0:T(8,128)} %fusion) | copy-start | bytes 3145732
  169.6 13.4 %collective-permute-start.19 = (bf16[2,16,256]{2,1,0:T(8,128)(2,1)S(1)}, bf16[2,16,256]{2,1,0:T(8,128)(2,1)S(1)}, u32[]{:S(2)}, u32[]{:S(2)}) collective-permute-start(bf16[2,16,256]{2,1,0:T(8,128)(2,1)S(1)} %reduce.1), channel_id=1, source_target_pairs={{0,256},{16,272},{32,288},{48,304},{64,320},{80,336},{96,352},{112... | collective-permute-start | bytes 49160 | tf_op jit(solution)/shard_map/ppermute | solution.py:242
  176.9 13.8 %collective-permute-start.18 = (bf16[128,1024]{1,0:T(8,128)(2,1)S(1)}, bf16[128,1024]{1,0:T(8,128)(2,1)S(1)}, u32[]{:S(2)}, u32[]{:S(2)}) collective-permute-start(bf16[128,1024]{1,0:T(8,128)(2,1)S(1)} %dynamic-slice_convert_fusion), channel_id=1, source_target_pairs={{0,1},{1,0},{2,3},{3,2},{4,5},{5,4},{6,7},{7,6},{8,9},{9,8},{10,11... | collective-permute-start | bytes 786440 | tf_op jit(solution)/shard_map/ppermute | solution.py:187
  183.7 12.6 %all-to-all-start.2 = ((bf16[16,2,16,256]{3,2,1,0:T(8,128)(2,1)}), bf16[16,2,16,256]{3,2,1,0:T(8,128)(2,1)S(1)}, u32[]{:S(2)}, u32[]{:S(2)}) async-start(bf16[16,2,16,256]{3,2,1,0:T(8,128)(2,1)} %broadcast_in_dim.14), calls=%async_computation.2 | async-start | bytes 524288 | tf_op jit(solution)/shard_map/all_to_all | solution.py:246
  (36 other events, 316.3 us)

commit v2 on v1

--- a/solution.py
+++ b/solution.py
@@ -25,31 +25,57 @@
     return lax.dot_general(a, b, (((1,), (1,)), ((), ())), preferred_element_type=F32)
 
 
-def layer_kernel(nx, ny, pos_ref, tok_ref, tokt_ref, g_ref, gt_ref, w0, p1, p2, p3, p4, m1, m2, m3, m4,
-                 w_ref, part_ref, lown_ref, lsend_ref, dq_ref, gown_ref, gkeep_ref, gsend_ref,
-                 kv_s, kvt_s, qm_s, gm_s, gkv_s, attt_s, dqt_s, att_s):
+def layer_kernel(nx, ny, pos_ref, *refs):
+    sources, refs = refs[:11], refs[11:]
+    results, refs = refs[:8], refs[8:]
+    staged, refs = refs[:8], refs[8:]
+    (tok_s, tokt_s, g_s, gt_s, kv_s, kvt_s, qm_s, gm_s, gkv_s, attt_s, dqt_s, att_s, in_sem, w_sem, out_sem, part_sem) = refs
+    tok, tokt, g, gt, w0, r1, r2, r3, r4, x12, x34 = sources
+    w_s, part_s, lown_s, lsend_s, dq_s, gown_s, gkeep_s, gsend_s = staged
     zl = pos_ref[0]
     core = pos_ref[1]
-
-    def place(index, piece):
-        row = pl.multiple_of(lax.rem(zl + index + 8, 8) * 128, 128)
-        w_ref[pl.ds(row, 128), :] = piece
-
-    place(0, w0[...])
-    for index, piece in ((1, p1), (2, p2), (3, p3), (-1, m1), (-2, m2), (-3, m3)):
-        place(index, piece[...])
-    place(4, jnp.concatenate([p4[...], m4[...]], axis=0))
+    step_sign = 1 - 2 * core
+    cols = pl.ds(pl.multiple_of(core * 1024, 1024), 1024)
+
+    def row_of(index):
+        return pl.multiple_of(lax.rem(zl + index + 8, 8) * 128, 128)
+
+    def weight_rows(index):
+        return w_s.at[pl.ds(row_of(index), 128), :]
+
+    def opposite(which):
+        return w_s.at[pl.ds(pl.multiple_of(row_of(4) + which * 64, 64), 64), :]
+
+    moves = [(w0.at[:, cols], weight_rows(0))]
+    for k, piece in ((1, r1), (2, r2), (3, r3)):
+        moves.append((piece.at[:, cols], weight_rows(step_sign * k)))
+    moves.append((r4.at[:, cols], opposite(core)))
+    moves.append((x12.at[pl.ds(0, 128), :], weight_rows(-step_sign)))
+    moves.append((x12.at[pl.ds(128, 128), :], weight_rows(-2 * step_sign)))
+    moves.append((x34.at[pl.ds(0, 128), :], weight_rows(-3 * step_sign)))
+    moves.append((x34.at[pl.ds(128, 64), :], opposite(1 - core)))
+    weight_copies = [pltpu.make_async_copy(src, dst, w_sem.at[i]) for i, (src, dst) in enumerate(moves)]
+    inputs = [pltpu.make_async_copy(src, dst, in_sem.at[i])
+              for i, (src, dst) in enumerate(((tok, tok_s), (g, g_s), (tokt, tokt_s), (gt, gt_s)))]
+    for copy in inputs[:1] + weight_copies + inputs[1:]:
+        copy.start()
+    outputs = {i: pltpu.make_async_copy(staged[i], results[i], out_sem.at[i]) for i in (0, 2, 3, 4, 5, 6, 7)}
+    inputs[0].wait()
+    for copy in weight_copies:
+        copy.wait()
+    outputs[0].start()
 
     def project_keys(step, carry):
         row = pl.multiple_of(step * 128, 128)
-        block = nn(tok_ref[pl.ds(row, 128), :], w_ref[:, 256:768])
+        block = nn(tok_s[pl.ds(row, 128), :], w_s[:, 256:768])
         kv_s[pl.ds(row, 128), :] = block.astype(BF)
         kvt_s[:, pl.ds(row, 128)] = block.T.astype(BF)
         return carry
 
     lax.fori_loop(0, 5, project_keys, 0)
-    queries = nn(tok_ref[0:256, :], w_ref[:, 0:256]) * 0.125
-    grads = nn(g_ref[...], w_ref[:, 768:1024])
+    queries = nn(tok_s[0:256, :], w_s[:, 0:256]) * 0.125
+    inputs[1].wait()
+    grads = nn(g_s[...], w_s[:, 768:1024])
     lane = lax.broadcasted_iota(jnp.int32, (256, 128), 1)
     for head in range(4):
         pair = (head // 2) * 128
@@ -83,58 +109,77 @@
             key_grad = new_key if key_grad is None else key_grad + new_key
             value_grad = new_value if value_grad is None else value_grad + new_value
         for col, grad in ((kcol, key_grad), (vcol, value_grad)):
-            cols = slice(col, col + 128)
-            gown_ref[:, cols] = grad[0:256]
-            gkeep_ref[:, cols] = grad[256:384]
-            gkv_s[:, cols] = grad.astype(BF)
-
-    gsend_ref[...] = gkv_s[384:640, :]
-    dq_ref[...] = dqt_s[...].T.astype(BF)
+            where = slice(col, col + 128)
+            gown_s[:, where] = grad[0:256]
+            gkeep_s[:, where] = grad[256:384]
+            gkv_s[:, where] = grad.astype(BF)
+
+    gsend_s[...] = gkv_s[384:640, :]
+    dq_s[...] = dqt_s[...].T.astype(BF)
     attended = attt_s[...].T.astype(BF)
     att_s[0] = attended[0:128]
     att_s[1] = attended[128:256]
+    for index in (4, 5, 6, 7):
+        outputs[index].start()
 
     x_rows = 64 // nx
     y_cols = 1024 // ny
+    inputs[2].wait()
+    inputs[3].wait()
+
+    def part_copy(step):
+        where = pl.ds(2 * step, 2)
+        return pltpu.make_async_copy(part_s.at[:, where], results[1].at[:, where], part_sem.at[step])
 
     def grad_rows(step, carry):
         rows = pl.ds(pl.multiple_of(step * 128, 128), 128)
-        lhs = tokt_ref[rows, :]
+        lhs = tokt_s[rows, :]
         att_all = jnp.concatenate([att_s[0], att_s[1]], axis=0)
         block = jnp.concatenate(
-            [nn(lhs[:, 0:256], dq_ref[...]).astype(BF), nn(lhs, gkv_s[...]).astype(BF),
-             nn(gt_ref[rows, :], att_all).astype(BF)], axis=1)
+            [nn(lhs[:, 0:256], dq_s[...]).astype(BF), nn(lhs, gkv_s[...]).astype(BF),
+             nn(gt_s[rows, :], att_all).astype(BF)], axis=1)
         for side in range(2):
             for x in range(nx):
                 for y in range(ny):
-                    part_ref[x * ny + y, 2 * step + side] = block[
+                    part_s[x * ny + y, 2 * step + side] = block[
                         side * 64 + x * x_rows:side * 64 + (x + 1) * x_rows, y * y_cols:(y + 1) * y_cols]
+        part_copy(step).start()
         return carry
 
     lax.fori_loop(0, 8, grad_rows, 0)
-    lown_ref[...] = nt(att_s[core], w_ref[:, 768:1024])
-    lsend_ref[...] = nt(att_s[1 - core], w_ref[:, 768:1024]).astype(BF)
+    lown_s[...] = nt(att_s[core], w_s[:, 768:1024])
+    lsend_s[...] = nt(att_s[1 - core], w_s[:, 768:1024]).astype(BF)
+    outputs[2].start()
+    outputs[3].start()
+    for step in range(8):
+        part_copy(step).wait()
+    for index in (0, 2, 3, 4, 5, 6, 7):
+        outputs[index].wait()
 
 
 def run_layer(nx, ny, *operands):
-    vmem = pl.BlockSpec(memory_space=pltpu.VMEM)
+    anywhere = pl.BlockSpec(memory_space=pl.ANY)
     smem = pl.BlockSpec(memory_space=pltpu.SMEM)
-    shape = jax.ShapeDtypeStruct
+    results = (
+        ((1024, 1024), BF),
+        ((nx * ny, 16, 64 // nx, 1024 // ny), BF),
+        ((128, 1024), F32),
+        ((128, 1024), BF),
+        ((256, 256), BF),
+        ((256, 512), F32),
+        ((128, 512), F32),
+        ((256, 512), BF),
+    )
     return pl.pallas_call(
         functools.partial(layer_kernel, nx, ny),
-        out_shape=(
-            shape((1024, 1024), BF),
-            shape((nx * ny, 16, 64 // nx, 1024 // ny), BF),
-            shape((128, 1024), F32),
-            shape((128, 1024), BF),
-            shape((256, 256), BF),
-            shape((256, 512), F32),
-            shape((128, 512), F32),
-            shape((256, 512), BF),
-        ),
-        in_specs=[smem] + [vmem] * (len(operands) - 1),
-        out_specs=tuple([vmem] * 8),
-        scratch_shapes=[
+        out_shape=tuple(jax.ShapeDtypeStruct(*result) for result in results),
+        in_specs=[smem] + [anywhere] * (len(operands) - 1),
+        out_specs=tuple([anywhere] * len(results)),
+        scratch_shapes=[pltpu.VMEM(*result) for result in results] + [
+            pltpu.VMEM((640, 1024), BF),
+            pltpu.VMEM((1024, 640), BF),
+            pltpu.VMEM((256, 1024), BF),
+            pltpu.VMEM((1024, 256), BF),
             pltpu.VMEM((640, 512), BF),
             pltpu.VMEM((512, 640), BF),
             pltpu.VMEM((4, 256, 128), BF),
@@ -143,8 +188,12 @@
             pltpu.VMEM((256, 256), F32),
             pltpu.VMEM((256, 256), F32),
             pltpu.VMEM((2, 128, 256), BF),
+            pltpu.SemaphoreType.DMA((4,)),
+            pltpu.SemaphoreType.DMA((9,)),
+            pltpu.SemaphoreType.DMA((8,)),
+            pltpu.SemaphoreType.DMA((8,)),
         ],
-        compiler_params=pltpu.CompilerParams(vmem_limit_bytes=40 * 1024 * 1024),
+        compiler_params=pltpu.CompilerParams(vmem_limit_bytes=28 * 1024 * 1024),
         cost_estimate=pl.CostEstimate(flops=3_500_000_000, bytes_accessed=14_000_000, transcendentals=700_000),
     )(*operands)
 
@@ -168,19 +217,13 @@
     def chip_swap(bit):
         return [(i, i ^ (2 << bit)) for i in range(seq_count)]
 
-    def along_z(shift):
-        pairs = []
-        for z in range(ring):
-            source = (z + shift) % ring
-            for xy in range(nxy):
-                for core in range(2):
-                    pairs.append((((source // 8) * nxy + xy) * seq_count + (source % 8) * 2 + core,
-                                  ((z // 8) * nxy + xy) * seq_count + (z % 8) * 2 + core))
-        return pairs
-
-    plus, minus = along_z(1), along_z(-1)
+    def device(z, xy, core):
+        return ((z // 8) * nxy + xy) * seq_count + (z % 8) * 2 + core
+
+    ring_pairs = [(device((z + 1 - 2 * core) % ring, xy, core), device(z, xy, core))
+                  for z in range(ring) for xy in range(nxy) for core in range(2)]
+    line_groups = [[device(z, xy, core) for z in range(ring) for core in range(2)] for xy in range(nxy)]
     plane_groups = [[zh * nxy + xy for xy in range(nxy)] for zh in range(nzh)]
-    zh_pairs = [(zh * nxy + xy, ((zh + 1) % nzh) * nxy + xy) for zh in range(nzh) for xy in range(nxy)]
     coarse_matrix = coarsening()
 
     def swap_core(value):
@@ -195,21 +238,23 @@
         def ordered(mine, other, axis):
             return jnp.where(first, jnp.concatenate([mine, other], axis), jnp.concatenate([other, mine], axis))
 
-        shard = stacked.reshape(64, 4, 2, 256)
-        keep = lax.dynamic_index_in_dim(shard, core, 2, False).reshape(64, 1024)
-        give = lax.dynamic_index_in_dim(shard, 1 - core, 2, False).reshape(64, 1024)
-        w0 = ordered(keep, swap_core(give), 0)
         both = ("dp", "seq")
-        p1 = lax.ppermute(w0, both, plus)
-        m1 = lax.ppermute(w0, both, minus)
-        p2 = lax.ppermute(p1, both, plus)
-        m2 = lax.ppermute(m1, both, minus)
-        p3 = lax.ppermute(p2, both, plus)
-        m3 = lax.ppermute(m2, both, minus)
-        p4 = lax.ppermute(p3[0:64], both, plus)
-        m4 = lax.ppermute(m3[64:128], both, minus)
+        shard = stacked.reshape(64, 4, 2, 256).transpose(0, 2, 1, 3).reshape(64, 2048)
+        shard_got = swap_core(shard)
+        w0 = ordered(shard, shard_got, 0)
+        r1 = lax.ppermute(w0, both, ring_pairs)
+        r2 = lax.ppermute(r1, both, ring_pairs)
+        r3 = lax.ppermute(r2, both, ring_pairs)
+        r4 = lax.ppermute(lax.dynamic_slice(r3, (core * 64, 0), (64, 2048)), both, ring_pairs)
+
+        def other_columns(value):
+            return lax.dynamic_slice(value, (0, (1 - core) * 1024), (value.shape[0], 1024))
+
+        x12 = swap_core(jnp.concatenate([other_columns(r1), other_columns(r2)], 0))
+        x34 = swap_core(jnp.concatenate([other_columns(r3), other_columns(r4)], 0))
 
         own = jnp.concatenate([tokens[0], grad_out[0]], axis=0)
+        own, _ = lax.optimization_barrier((own, shard_got))
         got = swap_core(own)
         chip_tokens = ordered(own[0:128], got[0:128], 0)
         chip_grads = ordered(own[128:256], got[128:256], 0)
@@ -217,9 +262,9 @@
         half_tokens = lax.dynamic_slice(chip_tokens, (0, core * 512), (256, 512))
         coarse = nn(matrix, half_tokens).astype(BF)
         c1, c2, c3 = coarse[0:128], coarse[128:192], coarse[192:224]
-        r3 = lax.ppermute(c3, "seq", chip_swap(2))
-        second = lax.ppermute(jnp.concatenate([c2, r3], 0), "seq", chip_swap(1))
-        held = jnp.concatenate([second[0:64], r3, second[64:96]], 0)
+        t3, _ = lax.optimization_barrier((lax.ppermute(c3, "seq", chip_swap(2)), r1))
+        second, _ = lax.optimization_barrier((lax.ppermute(jnp.concatenate([c2, t3], 0), "seq", chip_swap(1)), r2))
+        held = jnp.concatenate([second[0:64], t3, second[64:96]], 0)
         third = lax.ppermute(jnp.concatenate([c1, held], 0), "seq", chip_swap(0))
         half_set = jnp.concatenate([held, third], 0)
         rest = ordered(half_set, swap_core(half_set), 1)
@@ -228,19 +273,17 @@
         position = jnp.stack([zl, core]).astype(jnp.int32)
         (weight, part, layer_own, layer_send, dquery, grad_own, grad_keep, grad_send) = run_layer(
             nx, ny, position, token_set, token_set.T, chip_grads, chip_grads.T,
-            w0, p1, p2, p3, p4, m1, m2, m3, m4)
+            w0, r1, r2, r3, r4, x12, x34)
 
         if nxy > 1:
             pieces = lax.all_to_all(part, "dp", 0, 0, axis_index_groups=plane_groups, tiled=True)
         else:
             pieces = part
         plane_sum = jnp.sum(pieces.astype(F32), axis=0).astype(BF)
-        columns = lax.all_to_all(plane_sum, "seq", 0, 0, tiled=True)
+        twice = jnp.concatenate([plane_sum] * nzh, axis=0)
+        columns = lax.all_to_all(twice, both, 0, 0, axis_index_groups=line_groups, tiled=True)
         rows, cols = 64 // nx, 1024 // ny
-        line_sum = jnp.sum(columns.astype(F32).reshape(8, 2, rows, cols), axis=0).astype(BF)
-        if nzh > 1:
-            other_half = lax.ppermute(line_sum, "dp", zh_pairs)
-            line_sum = (line_sum.astype(F32) + other_half.astype(F32)).astype(BF)
+        line_sum = jnp.sum(columns.astype(F32).reshape(ring, 2, rows, cols), axis=0).astype(BF)
         spread = jnp.broadcast_to(line_sum[None], (nxy, 2, rows, cols))
         if nxy > 1:
             spread = lax.all_to_all(spread, "dp", 0, 0, axis_index_groups=plane_groups, tiled=True)

time: 200 us -> 194 us (0.970)
  starting transfers between devices: 105 us -> 75.8 us
  waiting for transfers between devices: 41.1 us -> 64.5 us
  local copies, waits for them, and re-layouts: 27.8 us -> 22.4 us
  other arithmetic: 10 us -> 12.5 us
    ppermute x11 -> x6, starting transfers between devices: 42.7 us -> 14 us  [the longest x1 3.36 us: per_device(): lax.ppermute(lax.dynamic_slice(r3, (core * 64, 0), (64, 2048)), both, rin...]
    ppermute x5 -> x7, starting transfers between devices: 21.9 us -> 31.5 us  [swap_core(): return lax.ppermute(value, 'seq', core_pairs)]
    ppermute x11 -> x6, waiting for transfers between devices: 16.3 us -> 25.4 us  [the longest x1 8.58 us: per_device(): lax.ppermute(c3, 'seq', chip_swap(2))]
    all_to_all x1, waiting for transfers between devices: 10.4 us -> 16.3 us  [per_device(): lax.all_to_all(twice, both, 0, 0, axis_index_groups=line_groups, tiled=True)]
    all_to_all x1, waiting for transfers between devices: 0.01 us -> 5.68 us  [per_device(): lax.all_to_all(part, 'dp', 0, 0, axis_index_groups=plane_groups, tiled=True)]
    ppermute x1, waiting for transfers between devices: 0.01 us -> 4.5 us  [per_device(): lax.ppermute(jnp.concatenate([joined[0:64], joined[96:128]], 0).astype(BF...]
    concatenate x1 -> x4, other arithmetic: 0.11 us -> 3.51 us  [the longest x1 1.77 us: per_device(): twice = jnp.concatenate([plane_sum] * nzh, axis=0)]
    ppermute x1, starting transfers between devices: 6.09 us -> 2.7 us  [per_device(): lax.ppermute((joined[64:96] + b2[64:96].astype(F32)).astype(BF), 'seq', c...]
  transfers between devices with their start and end apart: 23 -> 20, of which waited for: 10 -> 9; matrix products, arithmetic and copies ran while one was open for 10% -> 12% of each run, Pallas kernels for 0% -> 0%
where the time goes in v2:
time: 194 us; the launch traced here: 192 us
  starting transfers between devices  75.8 us (39%)
  waiting for transfers between devices  64.5 us (33%)
  local copies, waits for them, and re-layouts  22.4 us (12%)
  other arithmetic  12.5 us (6%)
  Pallas kernels  11.5 us (6%)
  matrix products  4.13 us (2%)
    ppermute x7, starting transfers between devices, swap_core(): return lax.ppermute(value, 'seq', core_pairs)  31.5 us
    unnamed x60, local copies, waits for them, and re-layouts  17.3 us
    all_to_all x1, waiting for transfers between devices, per_device(): lax.all_to_all(twice, both, 0, 0, axis_index_groups=line_groups, tiled=True)  16.3 us
    pallas_call x1, Pallas kernels, run_layer(): pl.pallas_call(functools.partial(layer_kernel, nx, ny), out_shape=tuple((...  11.5 us
    all_to_all x1, starting transfers between devices, per_device(): lax.all_to_all(twice, both, 0, 0, axis_index_groups=line_groups, tiled=True)  9.78 us
    ppermute x1, waiting for transfers between devices, per_device(): lax.ppermute(c3, 'seq', chip_swap(2))  8.58 us
    ppermute x1, waiting for transfers between devices, per_device(): lax.ppermute(jnp.concatenate([c2, t3], 0), 'seq', chip_swap(1))  7.82 us
    ppermute x1, waiting for transfers between devices, per_device(): b1 = lax.ppermute(grad_send, 'seq', chip_swap(0))  7.58 us
  transfers between devices with their start and end apart: 20, of which 9 were waited for; matrix products, arithmetic and copies ran while one was open for 12% of the time, Pallas kernels for 0%

profile of v2, /device:TPU:1, one launch (start us, length us, event | category | flops | bytes accessed | tf_op | source)
XLA Modules:
  0.0 192.1 jit_solution(3940472773763721348)
XLA Ops:
  1.8 8.8 %collective-permute-start = (bf16[64,2048]{1,0:T(8,128)(2,1)S(1)}, bf16[64,2048]{1,0:T(8,128)(2,1)S(1)}, u32[]{:S(2)}, u32[]{:S(2)}) collective-permute-start(bf16[64,2048]{1,0:T(8,128)(2,1)S(1)} %reshape.30), channel_id=1, source_target_pairs={{0,1},{1,0},{2,3},{3,2},{4,5},{5,4},{6,7},{7,6},{8,9},{9,8},{10,11... | collective-permute-start | bytes 786440 | tf_op jit(solution)/shard_map/ppermute | solution.py:230
  14.9 6.0 %collective-permute-start.1 = (bf16[256,1024]{0,1:T(8,128)(2,1)S(1)}, bf16[256,1024]{0,1:T(8,128)(2,1)S(1)}, u32[]{:S(2)}, u32[]{:S(2)}) collective-permute-start(bf16[256,1024]{0,1:T(8,128)(2,1)S(1)} %pad_maximum_fusion.1), channel_id=1, source_target_pairs={{0,1},{1,0},{2,3},{3,2},{4,5},{5,4},{6,7},{7,6},{8,9},{9,8},{10,11... | collective-permute-start | bytes 1572872 | tf_op jit(solution)/shard_map/ppermute | solution.py:230
  21.0 4.3 %collective-permute-done.3.refs_5_ = bf16[128,2048]{1,0:T(8,128)(2,1)S(1)} collective-permute-done((bf16[128,2048]{1,0:T(8,128)(2,1)S(1)}, bf16[128,2048]{1,0:T(8,128)(2,1)S(1)}, u32[]{:S(2)}, u32[]{:S(2)}) %collective-permute-start.3) | collective-permute-done | bytes 524320 | tf_op jit(solution)/shard_map/ppermute | solution.py:245
  28.8 3.0 %collective-permute-start.2 = (bf16[32,512]{0,1:T(8,128)(2,1)S(1)}, bf16[32,512]{0,1:T(8,128)(2,1)S(1)}, u32[]{:S(2)}, u32[]{:S(2)}) collective-permute-start(bf16[32,512]{0,1:T(8,128)(2,1)S(1)} %slice.75), channel_id=1, source_target_pairs={{0,8},{1,9},{2,10},{3,11},{4,12},{5,13},{6,14},{7,15},{8,0},{9,1},... | collective-permute-start | bytes 98312 | tf_op jit(solution)/shard_map/ppermute | solution.py:265
  31.8 4.7 %collective-permute-done.5.refs_6_ = bf16[128,2048]{1,0:T(8,128)(2,1)S(1)} collective-permute-done((bf16[128,2048]{1,0:T(8,128)(2,1)S(1)}, bf16[128,2048]{1,0:T(8,128)(2,1)S(1)}, u32[]{:S(2)}, u32[]{:S(2)}) %collective-permute-start.5) | collective-permute-done | bytes 524320 | tf_op jit(solution)/shard_map/ppermute | solution.py:246
  38.5 8.6 %collective-permute-done.2 = bf16[32,512]{0,1:T(8,128)(2,1)S(1)} collective-permute-done((bf16[32,512]{0,1:T(8,128)(2,1)S(1)}, bf16[32,512]{0,1:T(8,128)(2,1)S(1)}, u32[]{:S(2)}, u32[]{:S(2)}) %collective-permute-start.2) | collective-permute-done | bytes 32800 | tf_op jit(solution)/shard_map/ppermute | solution.py:265
  47.2 1.9 collective-permute-start.4
  49.2 7.8 %collective-permute-done.4 = bf16[96,512]{0,1:T(8,128)(2,1)S(1)} collective-permute-done((bf16[96,512]{0,1:T(8,128)(2,1)S(1)}, bf16[96,512]{0,1:T(8,128)(2,1)S(1)}, u32[]{:S(2)}, u32[]{:S(2)}) %collective-permute-start.4) | collective-permute-done | bytes 98336 | tf_op jit(solution)/shard_map/ppermute | solution.py:266
  57.2 1.9 collective-permute-start.6
  59.3 3.4 %collective-permute-start.9 = (bf16[64,2048]{1,0:T(8,128)(2,1)S(1)}, bf16[64,2048]{1,0:T(8,128)(2,1)S(1)}, u32[]{:S(2)}, u32[]{:S(2)}) collective-permute-start(bf16[64,2048]{1,0:T(8,128)(2,1)S(1)} %constant_dynamic-slice_fusion.4), channel_id=1, source_target_pairs={{2,0},{271,1},{18,16},{287,17},{34,32},{303,33},{50,48},{319,49},{... | collective-permute-start | bytes 786440 | tf_op jit(solution)/shard_map/ppermute | solution.py:248
  63.5 7.1 %collective-permute-start.10 = (bf16[256,1024]{1,0:T(8,128)(2,1)}, bf16[256,1024]{1,0:T(8,128)(2,1)}, u32[]{:S(2)}, u32[]{:S(2)}) collective-permute-start(bf16[256,1024]{1,0:T(8,128)(2,1)} %pad_maximum_fusion.2), channel_id=1, source_target_pairs={{0,1},{1,0},{2,3},{3,2},{4,5},{5,4},{6,7},{7,6},{8,9},{9,8},{10,11... | collective-permute-start | bytes 1572872 | tf_op jit(solution)/shard_map/ppermute | solution.py:230
  74.4 2.4 %collective-permute-start.11 = (bf16[192,1024]{1,0:T(8,128)(2,1)}, bf16[192,1024]{1,0:T(8,128)(2,1)S(1)}, u32[]{:S(2)}, u32[]{:S(2)}) collective-permute-start(bf16[192,1024]{1,0:T(8,128)(2,1)} %pad_maximum_fusion.4), channel_id=1, source_target_pairs={{0,1},{1,0},{2,3},{3,2},{4,5},{5,4},{6,7},{7,6},{8,9},{9,8},{10,11... | collective-permute-start | bytes 1179656 | tf_op jit(solution)/shard_map/ppermute | solution.py:230
  90.5 11.5 %shard_map.76 = (bf16[1024,1024]{1,0:T(8,128)(2,1)S(1)}, bf16[16,16,16,256]{3,2,1,0:T(8,128)(2,1)}, f32[128,1024]{1,0:T(8,128)S(1)}, bf16[128,1024]{1,0:T(8,128)...) custom-call(s32[2]{0:T(128)S(1)} %pad_add_fusion.pos_ref, ...), custom_call_target="tpu_custom_call" | custom-call | flops 3500000000 | bytes 14000000 | tf_op jit(solution)/shard_map/pallas_call | solution.py:173
  106.4 6.9 %all-to-all-start = ((bf16[16,16,16,256]{3,2,1,0:T(8,128)(2,1)}), bf16[16,16,16,256]{3,2,1,0:T(8,128)(2,1)S(1)}, u32[]{:S(2)}, u32[]{:S(2)}) async-start(bf16[16,16,16,256]{3,2,1,0:T(8,128)(2,1)} %get-tuple-element.24), calls=%async_computation | async-start | bytes 4194304 | tf_op jit(solution)/shard_map/all_to_all | solution.py:279
  115.2 7.6 %collective-permute-done.13 = bf16[256,512]{1,0:T(8,128)(2,1)S(1)} collective-permute-done((bf16[256,512]{1,0:T(8,128)(2,1)S(1)}, bf16[256,512]{1,0:T(8,128)(2,1)S(1)}, u32[]{:S(2)}, u32[]{:S(2)}) %collective-permute-start.13) | collective-permute-done | bytes 262176 | tf_op jit(solution)/shard_map/ppermute | solution.py:297
  124.8 3.0 %collective-permute-start.12 = (bf16[128,1024]{1,0:T(8,128)(2,1)S(1)}, bf16[128,1024]{1,0:T(8,128)(2,1)}, u32[]{:S(2)}, u32[]{:S(2)}) collective-permute-start(bf16[128,1024]{1,0:T(8,128)(2,1)S(1)} %copy-done.18), channel_id=1, source_target_pairs={{0,1},{1,0},{2,3},{3,2},{4,5},{5,4},{6,7},{7,6},{8,9},{9,8},{10,11... | collective-permute-start | bytes 786440 | tf_op jit(solution)/shard_map/ppermute | solution.py:230
  127.9 4.5 %collective-permute-done.14 = bf16[96,512]{1,0:T(8,128)(2,1)S(1)} collective-permute-done((bf16[96,512]{1,0:T(8,128)(2,1)S(1)}, bf16[96,512]{1,0:T(8,128)(2,1)S(1)}, u32[]{:S(2)}, u32[]{:S(2)}) %collective-permute-start.14) | collective-permute-done | bytes 98336 | tf_op jit(solution)/shard_map/ppermute | solution.py:299
  133.0 2.7 %collective-permute-start.15 = (bf16[32,512]{1,0:T(8,128)(2,1)}, bf16[32,512]{1,0:T(8,128)(2,1)}, u32[]{:S(2)}, u32[]{:S(2)}) collective-permute-start(bf16[32,512]{1,0:T(8,128)(2,1)} %fusion.11), channel_id=1, source_target_pairs={{0,8},{1,9},{2,10},{3,11},{4,12},{5,13},{6,14},{7,15},{8,0},{9,1},... | collective-permute-start | bytes 98312 | tf_op jit(solution)/shard_map/ppermute | solution.py:300
  136.7 5.7 %all-to-all-done = bf16[16,16,16,256]{3,2,1,0:T(8,128)(2,1)S(1)} async-done(((bf16[16,16,16,256]{3,2,1,0:T(8,128)(2,1)}), bf16[16,16,16,256]{3,2,1,0:T(8,128)(2,1)S(1)}, u32[]{:S(2)}, u32[]{:S(2)}) %all-to-all-start) | async-done | bytes 2097184 | tf_op jit(solution)/shard_map/all_to_all | solution.py:279
  145.2 9.8 %all-to-all-start.1 = ((bf16[32,16,256]{2,1,0:T(8,128)(2,1)}), bf16[32,16,256]{2,1,0:T(8,128)(2,1)S(1)}, u32[]{:S(2)}, u32[]{:S(2)}) async-start(bf16[32,16,256]{2,1,0:T(8,128)(2,1)} %pad_maximum_fusion.6), calls=%async_computation.1 | async-start | bytes 524288 | tf_op jit(solution)/shard_map/all_to_all | solution.py:284
  158.3 2.3 %collective-permute-start.16 = (bf16[128,1024]{1,0:T(8,128)(2,1)S(1)}, bf16[128,1024]{1,0:T(8,128)(2,1)S(1)}, u32[]{:S(2)}, u32[]{:S(2)}) collective-permute-start(bf16[128,1024]{1,0:T(8,128)(2,1)S(1)} %dynamic-slice_convert_fusion), channel_id=1, source_target_pairs={{0,1},{1,0},{2,3},{3,2},{4,5},{5,4},{6,7},{7,6},{8,9},{9,8},{10,11... | collective-permute-start | bytes 786440 | tf_op jit(solution)/shard_map/ppermute | solution.py:230
  160.6 16.3 %all-to-all-done.1 = bf16[32,16,256]{2,1,0:T(8,128)(2,1)S(1)} async-done(((bf16[32,16,256]{2,1,0:T(8,128)(2,1)}), bf16[32,16,256]{2,1,0:T(8,128)(2,1)S(1)}, u32[]{:S(2)}, u32[]{:S(2)}) %all-to-all-start.1) | async-done | bytes 262176 | tf_op jit(solution)/shard_map/all_to_all | solution.py:284
  177.7 5.1 %all-to-all-start.2 = ((bf16[16,2,16,256]{3,2,1,0:T(8,128)(2,1)}), bf16[16,2,16,256]{3,2,1,0:T(8,128)(2,1)S(1)}, u32[]{:S(2)}, u32[]{:S(2)}) async-start(bf16[16,2,16,256]{3,2,1,0:T(8,128)(2,1)} %broadcast_in_dim.14), calls=%async_computation.2 | async-start | bytes 524288 | tf_op jit(solution)/shard_map/all_to_all | solution.py:289
  185.3 5.0 %all-to-all-done.2 = bf16[16,2,16,256]{3,2,1,0:T(8,128)(2,1)S(1)} async-done(((bf16[16,2,16,256]{3,2,1,0:T(8,128)(2,1)}), bf16[16,2,16,256]{3,2,1,0:T(8,128)(2,1)S(1)}, u32[]{:S(2)}, u32[]{:S(2)}) %all-to-all-start.2) | async-done | bytes 262176 | tf_op jit(solution)/shard_map/all_to_all | solution.py:289
  (123 shorter events, 50.5 us)
Async XLA Ops:
  1.8 11.1 %collective-permute-start = (bf16[64,2048]{1,0:T(8,128)(2,1)S(1)}, bf16[64,2048]{1,0:T(8,128)(2,1)S(1)}, u32[]{:S(2)}, u32[]{:S(2)}) collective-permute-start(bf16[64,2048]{1,0:T(8,128)(2,1)S(1)} %reshape.30), channel_id=1, source_target_pairs={{0,1},{1,0},{2,3},{3,2},{4,5},{5,4},{6,7},{7,6},{8,9},{9,8},{10,11... | collective-permute-start | bytes 786440 | tf_op jit(solution)/shard_map/ppermute | solution.py:230
  13.0 12.3 %collective-permute-start.3 = (bf16[128,2048]{1,0:T(8,128)(2,1)S(1)}, bf16[128,2048]{1,0:T(8,128)(2,1)S(1)}, u32[]{:S(2)}, u32[]{:S(2)}) collective-permute-start(bf16[128,2048]{1,0:T(8,128)(2,1)S(1)} %maximum_select_fusion.2.refs_4_), channel_id=1, source_target_pairs={{2,0},{271,1},{18,16},{287,17},{34,32},{303,33},{50,48},{319,49},{... | collective-permute-start | bytes 1572872 | tf_op jit(solution)/shard_map/ppermute | solution.py:245
  14.9 12.3 %collective-permute-start.1 = (bf16[256,1024]{0,1:T(8,128)(2,1)S(1)}, bf16[256,1024]{0,1:T(8,128)(2,1)S(1)}, u32[]{:S(2)}, u32[]{:S(2)}) collective-permute-start(bf16[256,1024]{0,1:T(8,128)(2,1)S(1)} %pad_maximum_fusion.1), channel_id=1, source_target_pairs={{0,1},{1,0},{2,3},{3,2},{4,5},{5,4},{6,7},{7,6},{8,9},{9,8},{10,11... | collective-permute-start | bytes 1572872 | tf_op jit(solution)/shard_map/ppermute | solution.py:230
  25.3 23.8 %copy-start.9 = (bf16[128,2048]{1,0:T(8,128)(2,1)}, bf16[128,2048]{1,0:T(8,128)(2,1)S(1)}, u32[]{:S(2)}) copy-start(bf16[128,2048]{1,0:T(8,128)(2,1)S(1)} %collective-permute-done.3.refs_5_) | copy-start | bytes 1572868
  25.3 11.1 %collective-permute-start.5 = (bf16[128,2048]{1,0:T(8,128)(2,1)S(1)}, bf16[128,2048]{1,0:T(8,128)(2,1)S(1)}, u32[]{:S(2)}, u32[]{:S(2)}) collective-permute-start(bf16[128,2048]{1,0:T(8,128)(2,1)S(1)} %collective-permute-done.3.refs_5_), channel_id=1, source_target_pairs={{2,0},{271,1},{18,16},{287,17},{34,32},{303,33},{50,48},{319,49},{... | collective-permute-start | bytes 1572872 | tf_op jit(solution)/shard_map/ppermute | solution.py:246
  28.8 18.3 %collective-permute-start.2 = (bf16[32,512]{0,1:T(8,128)(2,1)S(1)}, bf16[32,512]{0,1:T(8,128)(2,1)S(1)}, u32[]{:S(2)}, u32[]{:S(2)}) collective-permute-start(bf16[32,512]{0,1:T(8,128)(2,1)S(1)} %slice.75), channel_id=1, source_target_pairs={{0,8},{1,9},{2,10},{3,11},{4,12},{5,13},{6,14},{7,15},{8,0},{9,1},... | collective-permute-start | bytes 98312 | tf_op jit(solution)/shard_map/ppermute | solution.py:265
  36.5 22.8 %copy-start.11 = (bf16[128,2048]{1,0:T(8,128)(2,1)}, bf16[128,2048]{1,0:T(8,128)(2,1)S(1)}, u32[]{:S(2)}) copy-start(bf16[128,2048]{1,0:T(8,128)(2,1)S(1)} %collective-permute-done.5.refs_6_) | copy-start | bytes 1572868
  36.5 22.7 %collective-permute-start.8 = (bf16[128,2048]{1,0:T(8,128)(2,1)S(1)}, bf16[128,2048]{1,0:T(8,128)(2,1)S(1)}, u32[]{:S(2)}, u32[]{:S(2)}) collective-permute-start(bf16[128,2048]{1,0:T(8,128)(2,1)S(1)} %collective-permute-done.5.refs_6_), channel_id=1, source_target_pairs={{2,0},{271,1},{18,16},{287,17},{34,32},{303,33},{50,48},{319,49},{... | collective-permute-start | bytes 1572872 | tf_op jit(solution)/shard_map/ppermute | solution.py:247
  47.2 9.8 %collective-permute-start.4 = (bf16[96,512]{0,1:T(8,128)(2,1)S(1)}, bf16[96,512]{0,1:T(8,128)(2,1)S(1)}, u32[]{:S(2)}, u32[]{:S(2)}) collective-permute-start(bf16[96,512]{0,1:T(8,128)(2,1)S(1)} %pad_maximum_fusion.7), channel_id=1, source_target_pairs={{0,4},{1,5},{2,6},{3,7},{4,0},{5,1},{6,2},{7,3},{8,12},{9,13},{10,... | collective-permute-start | bytes 294920 | tf_op jit(solution)/shard_map/ppermute | solution.py:266
  57.2 13.4 %collective-permute-start.6 = (bf16[256,512]{0,1:T(8,128)(2,1)S(1)}, bf16[256,512]{0,1:T(8,128)(2,1)S(1)}, u32[]{:S(2)}, u32[]{:S(2)}) collective-permute-start(bf16[256,512]{0,1:T(8,128)(2,1)S(1)} %pad_maximum_fusion.5), channel_id=1, source_target_pairs={{0,2},{1,3},{2,0},{3,1},{4,6},{5,7},{6,4},{7,5},{8,10},{9,11},{10,... | collective-permute-start | bytes 786440 | tf_op jit(solution)/shard_map/ppermute | solution.py:268
  59.3 14.3 %collective-permute-start.9 = (bf16[64,2048]{1,0:T(8,128)(2,1)S(1)}, bf16[64,2048]{1,0:T(8,128)(2,1)S(1)}, u32[]{:S(2)}, u32[]{:S(2)}) collective-permute-start(bf16[64,2048]{1,0:T(8,128)(2,1)S(1)} %constant_dynamic-slice_fusion.4), channel_id=1, source_target_pairs={{2,0},{271,1},{18,16},{287,17},{34,32},{303,33},{50,48},{319,49},{... | collective-permute-start | bytes 786440 | tf_op jit(solution)/shard_map/ppermute | solution.py:248
  63.5 19.1 %collective-permute-start.10 = (bf16[256,1024]{1,0:T(8,128)(2,1)}, bf16[256,1024]{1,0:T(8,128)(2,1)}, u32[]{:S(2)}, u32[]{:S(2)}) collective-permute-start(bf16[256,1024]{1,0:T(8,128)(2,1)} %pad_maximum_fusion.2), channel_id=1, source_target_pairs={{0,1},{1,0},{2,3},{3,2},{4,5},{5,4},{6,7},{7,6},{8,9},{9,8},{10,11... | collective-permute-start | bytes 1572872 | tf_op jit(solution)/shard_map/ppermute | solution.py:230
  71.6 6.4 %collective-permute-start.7 = (bf16[384,512]{0,1:T(8,128)(2,1)}, bf16[384,512]{0,1:T(8,128)(2,1)}, u32[]{:S(2)}, u32[]{:S(2)}) collective-permute-start(bf16[384,512]{0,1:T(8,128)(2,1)} %pad_maximum_fusion.3), channel_id=1, source_target_pairs={{0,1},{1,0},{2,3},{3,2},{4,5},{5,4},{6,7},{7,6},{8,9},{9,8},{10,11... | collective-permute-start | bytes 1179656 | tf_op jit(solution)/shard_map/ppermute | solution.py:230
  74.4 8.2 %collective-permute-start.11 = (bf16[192,1024]{1,0:T(8,128)(2,1)}, bf16[192,1024]{1,0:T(8,128)(2,1)S(1)}, u32[]{:S(2)}, u32[]{:S(2)}) collective-permute-start(bf16[192,1024]{1,0:T(8,128)(2,1)} %pad_maximum_fusion.4), channel_id=1, source_target_pairs={{0,1},{1,0},{2,3},{3,2},{4,5},{5,4},{6,7},{7,6},{8,9},{9,8},{10,11... | collective-permute-start | bytes 1179656 | tf_op jit(solution)/shard_map/ppermute | solution.py:230
  106.4 36.0 %all-to-all-start = ((bf16[16,16,16,256]{3,2,1,0:T(8,128)(2,1)}), bf16[16,16,16,256]{3,2,1,0:T(8,128)(2,1)S(1)}, u32[]{:S(2)}, u32[]{:S(2)}) async-start(bf16[16,16,16,256]{3,2,1,0:T(8,128)(2,1)} %get-tuple-element.24), calls=%async_computation | async-start | bytes 4194304 | tf_op jit(solution)/shard_map/all_to_all | solution.py:279
  113.3 9.5 %collective-permute-start.13 = (bf16[256,512]{1,0:T(8,128)(2,1)S(1)}, bf16[256,512]{1,0:T(8,128)(2,1)S(1)}, u32[]{:S(2)}, u32[]{:S(2)}) collective-permute-start(bf16[256,512]{1,0:T(8,128)(2,1)S(1)} %copy-done.20), channel_id=1, source_target_pairs={{0,2},{1,3},{2,0},{3,1},{4,6},{5,7},{6,4},{7,5},{8,10},{9,11},{10,... | collective-permute-start | bytes 786440 | tf_op jit(solution)/shard_map/ppermute | solution.py:297
  122.8 19.6 %copy-start.25 = (bf16[256,512]{1,0:T(8,128)(2,1)}, bf16[256,512]{1,0:T(8,128)(2,1)S(1)}, u32[]{:S(2)}) copy-start(bf16[256,512]{1,0:T(8,128)(2,1)S(1)} %collective-permute-done.13) | copy-start | bytes 786436
  122.9 9.5 %collective-permute-start.14 = (bf16[96,512]{1,0:T(8,128)(2,1)S(1)}, bf16[96,512]{1,0:T(8,128)(2,1)S(1)}, u32[]{:S(2)}, u32[]{:S(2)}) collective-permute-start(bf16[96,512]{1,0:T(8,128)(2,1)S(1)} %pad_maximum_fusion.8), channel_id=1, source_target_pairs={{0,4},{1,5},{2,6},{3,7},{4,0},{5,1},{6,2},{7,3},{8,12},{9,13},{10,... | collective-permute-start | bytes 294920 | tf_op jit(solution)/shard_map/ppermute | solution.py:299
  124.8 58.0 %collective-permute-start.12 = (bf16[128,1024]{1,0:T(8,128)(2,1)S(1)}, bf16[128,1024]{1,0:T(8,128)(2,1)}, u32[]{:S(2)}, u32[]{:S(2)}) collective-permute-start(bf16[128,1024]{1,0:T(8,128)(2,1)S(1)} %copy-done.18), channel_id=1, source_target_pairs={{0,1},{1,0},{2,3},{3,2},{4,5},{5,4},{6,7},{7,6},{8,9},{9,8},{10,11... | collective-permute-start | bytes 786440 | tf_op jit(solution)/shard_map/ppermute | solution.py:230
  133.0 22.0 %collective-permute-start.15 = (bf16[32,512]{1,0:T(8,128)(2,1)}, bf16[32,512]{1,0:T(8,128)(2,1)}, u32[]{:S(2)}, u32[]{:S(2)}) collective-permute-start(bf16[32,512]{1,0:T(8,128)(2,1)} %fusion.11), channel_id=1, source_target_pairs={{0,8},{1,9},{2,10},{3,11},{4,12},{5,13},{6,14},{7,15},{8,0},{9,1},... | collective-permute-start | bytes 98312 | tf_op jit(solution)/shard_map/ppermute | solution.py:300
  145.2 31.8 %all-to-all-start.1 = ((bf16[32,16,256]{2,1,0:T(8,128)(2,1)}), bf16[32,16,256]{2,1,0:T(8,128)(2,1)S(1)}, u32[]{:S(2)}, u32[]{:S(2)}) async-start(bf16[32,16,256]{2,1,0:T(8,128)(2,1)} %pad_maximum_fusion.6), calls=%async_computation.1 | async-start | bytes 524288 | tf_op jit(solution)/shard_map/all_to_all | solution.py:284
  158.3 24.6 %copy-start.3 = (f32[128,1024]{1,0:T(8,128)S(1)}, f32[128,1024]{1,0:T(8,128)}, u32[]{:S(2)}) copy-start(f32[128,1024]{1,0:T(8,128)} %copy-done.2) | copy-start | bytes 1572868
  158.3 26.2 %collective-permute-start.16 = (bf16[128,1024]{1,0:T(8,128)(2,1)S(1)}, bf16[128,1024]{1,0:T(8,128)(2,1)S(1)}, u32[]{:S(2)}, u32[]{:S(2)}) collective-permute-start(bf16[128,1024]{1,0:T(8,128)(2,1)S(1)} %dynamic-slice_convert_fusion), channel_id=1, source_target_pairs={{0,1},{1,0},{2,3},{3,2},{4,5},{5,4},{6,7},{7,6},{8,9},{9,8},{10,11... | collective-permute-start | bytes 786440 | tf_op jit(solution)/shard_map/ppermute | solution.py:230
  177.7 12.6 %all-to-all-start.2 = ((bf16[16,2,16,256]{3,2,1,0:T(8,128)(2,1)}), bf16[16,2,16,256]{3,2,1,0:T(8,128)(2,1)S(1)}, u32[]{:S(2)}, u32[]{:S(2)}) async-start(bf16[16,2,16,256]{3,2,1,0:T(8,128)(2,1)} %broadcast_in_dim.14), calls=%async_computation.2 | async-start | bytes 524288 | tf_op jit(solution)/shard_map/all_to_all | solution.py:289
  (24 other events, 109.7 us)

commit v3 on v2

--- a/solution.py
+++ b/solution.py
@@ -26,34 +26,22 @@
 
 
 def layer_kernel(nx, ny, pos_ref, *refs):
-    sources, refs = refs[:11], refs[11:]
+    sources, refs = refs[:8], refs[8:]
     results, refs = refs[:8], refs[8:]
     staged, refs = refs[:8], refs[8:]
     (tok_s, tokt_s, g_s, gt_s, kv_s, kvt_s, qm_s, gm_s, gkv_s, attt_s, dqt_s, att_s, in_sem, w_sem, out_sem, part_sem) = refs
-    tok, tokt, g, gt, w0, r1, r2, r3, r4, x12, x34 = sources
+    tok, tokt, g, gt, n1, n2, n3, n4 = sources
     w_s, part_s, lown_s, lsend_s, dq_s, gown_s, gkeep_s, gsend_s = staged
     zl = pos_ref[0]
     core = pos_ref[1]
-    step_sign = 1 - 2 * core
-    cols = pl.ds(pl.multiple_of(core * 1024, 1024), 1024)
-
-    def row_of(index):
-        return pl.multiple_of(lax.rem(zl + index + 8, 8) * 128, 128)
-
-    def weight_rows(index):
-        return w_s.at[pl.ds(row_of(index), 128), :]
-
-    def opposite(which):
-        return w_s.at[pl.ds(pl.multiple_of(row_of(4) + which * 64, 64), 64), :]
-
-    moves = [(w0.at[:, cols], weight_rows(0))]
-    for k, piece in ((1, r1), (2, r2), (3, r3)):
-        moves.append((piece.at[:, cols], weight_rows(step_sign * k)))
-    moves.append((r4.at[:, cols], opposite(core)))
-    moves.append((x12.at[pl.ds(0, 128), :], weight_rows(-step_sign)))
-    moves.append((x12.at[pl.ds(128, 128), :], weight_rows(-2 * step_sign)))
-    moves.append((x34.at[pl.ds(0, 128), :], weight_rows(-3 * step_sign)))
-    moves.append((x34.at[pl.ds(128, 64), :], opposite(1 - core)))
+    even = lax.rem(zl + core, 2) == 0
+    base = jnp.where(even, zl, zl + 7)
+    turn = jnp.where(even, 2, -2)
+    moves = []
+    for piece, start in ((n1, base), (n2, base - turn), (n3, base + turn), (n4, base + 4)):
+        for k in range(2):
+            row = pl.multiple_of(lax.rem(start + k + 8, 8) * 128, 128)
+            moves.append((piece.at[pl.ds(128 * k, 128), :], w_s.at[pl.ds(row, 128), :]))
     weight_copies = [pltpu.make_async_copy(src, dst, w_sem.at[i]) for i, (src, dst) in enumerate(moves)]
     inputs = [pltpu.make_async_copy(src, dst, in_sem.at[i])
               for i, (src, dst) in enumerate(((tok, tok_s), (g, g_s), (tokt, tokt_s), (gt, gt_s)))]
@@ -189,11 +177,11 @@
             pltpu.VMEM((256, 256), F32),
             pltpu.VMEM((2, 128, 256), BF),
             pltpu.SemaphoreType.DMA((4,)),
-            pltpu.SemaphoreType.DMA((9,)),
+            pltpu.SemaphoreType.DMA((8,)),
             pltpu.SemaphoreType.DMA((8,)),
             pltpu.SemaphoreType.DMA((8,)),
         ],
-        compiler_params=pltpu.CompilerParams(vmem_limit_bytes=28 * 1024 * 1024),
+        compiler_params=pltpu.CompilerParams(vmem_limit_bytes=60 * 1024 * 1024),
         cost_estimate=pl.CostEstimate(flops=3_500_000_000, bytes_accessed=14_000_000, transcendentals=700_000),
     )(*operands)
 
@@ -220,9 +208,14 @@
     def device(z, xy, core):
         return ((z // 8) * nxy + xy) * seq_count + (z % 8) * 2 + core
 
-    ring_pairs = [(device((z + 1 - 2 * core) % ring, xy, core), device(z, xy, core))
-                  for z in range(ring) for xy in range(nxy) for core in range(2)]
-    line_groups = [[device(z, xy, core) for z in range(ring) for core in range(2)] for xy in range(nxy)]
+    def swaps(turn):
+        return [(device((z + 1 if (z + core + turn) % 2 == 0 else z - 1) % ring, xy, core), device(z, xy, core))
+                for z in range(ring) for xy in range(nxy) for core in range(2)]
+
+    swap_even, swap_odd = swaps(0), swaps(1)
+    quad_groups = [[4 * quad + i for i in range(4)] for quad in range(seq_count // 4)]
+    line_groups = [[(zh * nxy + xy) * seq_count + 4 * quad + i for zh in range(nzh) for quad in range(4)]
+                   for xy in range(nxy) for i in range(4)]
     plane_groups = [[zh * nxy + xy for xy in range(nxy)] for zh in range(nzh)]
     coarse_matrix = coarsening()
 
@@ -239,19 +232,17 @@
             return jnp.where(first, jnp.concatenate([mine, other], axis), jnp.concatenate([other, mine], axis))
 
         both = ("dp", "seq")
-        shard = stacked.reshape(64, 4, 2, 256).transpose(0, 2, 1, 3).reshape(64, 2048)
-        shard_got = swap_core(shard)
-        w0 = ordered(shard, shard_got, 0)
-        r1 = lax.ppermute(w0, both, ring_pairs)
-        r2 = lax.ppermute(r1, both, ring_pairs)
-        r3 = lax.ppermute(r2, both, ring_pairs)
-        r4 = lax.ppermute(lax.dynamic_slice(r3, (core * 64, 0), (64, 2048)), both, ring_pairs)
-
-        def other_columns(value):
-            return lax.dynamic_slice(value, (0, (1 - core) * 1024), (value.shape[0], 1024))
-
-        x12 = swap_core(jnp.concatenate([other_columns(r1), other_columns(r2)], 0))
-        x34 = swap_core(jnp.concatenate([other_columns(r3), other_columns(r4)], 0))
+        shard = stacked.reshape(64, 4, 2, 256)
+        keep = lax.dynamic_index_in_dim(shard, core, 2, False).reshape(64, 1024)
+        give = lax.dynamic_index_in_dim(shard, 1 - core, 2, False).reshape(64, 1024)
+        shard_got = swap_core(give)
+        w0 = ordered(keep, shard_got, 0)
+        w1 = lax.ppermute(w0, both, swap_even)
+        even = (zl + core) & 1 == 0
+        n1 = jnp.where(even, jnp.concatenate([w0, w1], 0), jnp.concatenate([w1, w0], 0))
+        n2 = lax.ppermute(n1, both, swap_odd)
+        n3 = lax.ppermute(n2, both, swap_even)
+        n4 = lax.ppermute(n3, both, swap_odd)
 
         own = jnp.concatenate([tokens[0], grad_out[0]], axis=0)
         own, _ = lax.optimization_barrier((own, shard_got))
@@ -262,8 +253,8 @@
         half_tokens = lax.dynamic_slice(chip_tokens, (0, core * 512), (256, 512))
         coarse = nn(matrix, half_tokens).astype(BF)
         c1, c2, c3 = coarse[0:128], coarse[128:192], coarse[192:224]
-        t3, _ = lax.optimization_barrier((lax.ppermute(c3, "seq", chip_swap(2)), r1))
-        second, _ = lax.optimization_barrier((lax.ppermute(jnp.concatenate([c2, t3], 0), "seq", chip_swap(1)), r2))
+        t3 = lax.ppermute(c3, "seq", chip_swap(2))
+        second = lax.ppermute(jnp.concatenate([c2, t3], 0), "seq", chip_swap(1))
         held = jnp.concatenate([second[0:64], t3, second[64:96]], 0)
         third = lax.ppermute(jnp.concatenate([c1, held], 0), "seq", chip_swap(0))
         half_set = jnp.concatenate([held, third], 0)
@@ -273,17 +264,21 @@
         position = jnp.stack([zl, core]).astype(jnp.int32)
         (weight, part, layer_own, layer_send, dquery, grad_own, grad_keep, grad_send) = run_layer(
             nx, ny, position, token_set, token_set.T, chip_grads, chip_grads.T,
-            w0, r1, r2, r3, r4, x12, x34)
+            n1, n2, n3, n4)
 
         if nxy > 1:
             pieces = lax.all_to_all(part, "dp", 0, 0, axis_index_groups=plane_groups, tiled=True)
         else:
             pieces = part
         plane_sum = jnp.sum(pieces.astype(F32), axis=0).astype(BF)
-        twice = jnp.concatenate([plane_sum] * nzh, axis=0)
-        columns = lax.all_to_all(twice, both, 0, 0, axis_index_groups=line_groups, tiled=True)
         rows, cols = 64 // nx, 1024 // ny
-        line_sum = jnp.sum(columns.astype(F32).reshape(ring, 2, rows, cols), axis=0).astype(BF)
+        by_chip = plane_sum.reshape(4, 4, rows, cols).transpose(1, 0, 2, 3)
+        by_chip = lax.all_to_all(by_chip, "seq", 0, 0, axis_index_groups=quad_groups, tiled=True)
+        quad_sum = jnp.sum(by_chip.astype(F32).reshape(2, 2, 4, rows, cols), axis=0).astype(BF)
+        by_quad = quad_sum.transpose(1, 0, 2, 3)
+        by_quad = lax.all_to_all(jnp.concatenate([by_quad] * nzh, axis=0), both, 0, 0,
+                                 axis_index_groups=line_groups, tiled=True)
+        line_sum = jnp.sum(by_quad.astype(F32), axis=0).astype(BF)
         spread = jnp.broadcast_to(line_sum[None], (nxy, 2, rows, cols))
         if nxy > 1:
             spread = lax.all_to_all(spread, "dp", 0, 0, axis_index_groups=plane_groups, tiled=True)

time: 194 us -> 178 us (0.918)
  the two profiles are of different devices: /device:TPU:1 before, /device:TPU:32 now
where the time goes in v3:
time: 178 us; the launch traced here: 177 us
  starting transfers between devices  82.7 us (46%)
  waiting for transfers between devices  61.7 us (35%)
  Pallas kernels  13.1 us (7%)
  local copies, waits for them, and re-layouts  9.94 us (6%)
  other arithmetic  5.67 us (3%)
  matrix products  2.86 us (2%)
    pallas_call x1, Pallas kernels, run_layer(): pl.pallas_call(functools.partial(layer_kernel, nx, ny), out_shape=tuple((...  13.1 us
    all_to_all x1, waiting for transfers between devices, per_device(): lax.all_to_all(jnp.concatenate([by_quad] * nzh, axis=0), both, 0, 0, axis...  11.9 us
    ppermute x5, starting transfers between devices, swap_core(): return lax.ppermute(value, 'seq', core_pairs)  9.86 us
    ppermute x1, starting transfers between devices, per_device(): second = lax.ppermute(jnp.concatenate([c2, t3], 0), 'seq', chip_swap(1))  9.44 us
    ppermute x1, starting transfers between devices, per_device(): t3 = lax.ppermute(c3, 'seq', chip_swap(2))  7.54 us
    ppermute x1, starting transfers between devices, per_device(): w1 = lax.ppermute(w0, both, swap_even)  7.39 us
    ppermute x1, starting transfers between devices, per_device(): b1 = lax.ppermute(grad_send, 'seq', chip_swap(0))  7.27 us
    all_to_all x1, starting transfers between devices, per_device(): lax.all_to_all(part, 'dp', 0, 0, axis_index_groups=plane_groups, tiled=True)  7.18 us
  transfers between devices with their start and end apart: 19, of which 13 were waited for; matrix products, arithmetic and copies ran while one was open for 8% of the time, Pallas kernels for 0%

profile of v3, /device:TPU:32, one launch (start us, length us, event | category | flops | bytes accessed | tf_op | source)
XLA Modules:
  0.0 177.2 jit_solution(10045800558895929385)
XLA Ops:
  8.8 7.4 %collective-permute-start.6 = (bf16[128,1024]{1,0:T(8,128)(2,1)S(1)}, bf16[128,1024]{1,0:T(8,128)(2,1)S(1)}, u32[]{:S(2)}, u32[]{:S(2)}) collective-permute-start(bf16[128,1024]{1,0:T(8,128)(2,1)S(1)} %maximum_select_fusion.4), channel_id=1, source_target_pairs={{2,0},{271,1},{18,16},{287,17},{34,32},{303,33},{50,48},{319,49},{... | collective-permute-start | bytes 786440 | tf_op jit(solution)/shard_map/ppermute | solution.py:240
  16.3 4.3 %collective-permute-done.6 = bf16[128,1024]{1,0:T(8,128)(2,1)S(1)} collective-permute-done((bf16[128,1024]{1,0:T(8,128)(2,1)S(1)}, bf16[128,1024]{1,0:T(8,128)(2,1)S(1)}, u32[]{:S(2)}, u32[]{:S(2)}) %collective-permute-start.6) | collective-permute-done | bytes 262176 | tf_op jit(solution)/shard_map/ppermute | solution.py:240
  23.4 7.5 %collective-permute-start.2 = (bf16[32,512]{0,1:T(8,128)(2,1)S(1)}, bf16[32,512]{0,1:T(8,128)(2,1)S(1)}, u32[]{:S(2)}, u32[]{:S(2)}) collective-permute-start(bf16[32,512]{0,1:T(8,128)(2,1)S(1)} %slice.75), channel_id=1, source_target_pairs={{0,8},{1,9},{2,10},{3,11},{4,12},{5,13},{6,14},{7,15},{8,0},{9,1},... | collective-permute-start | bytes 98312 | tf_op jit(solution)/shard_map/ppermute | solution.py:256
  31.0 4.9 %collective-permute-done.2 = bf16[32,512]{0,1:T(8,128)(2,1)S(1)} collective-permute-done((bf16[32,512]{0,1:T(8,128)(2,1)S(1)}, bf16[32,512]{0,1:T(8,128)(2,1)S(1)}, u32[]{:S(2)}, u32[]{:S(2)}) %collective-permute-start.2) | collective-permute-done | bytes 32800 | tf_op jit(solution)/shard_map/ppermute | solution.py:256
  36.0 9.4 %collective-permute-start.3 = (bf16[96,512]{0,1:T(8,128)(2,1)S(1)}, bf16[96,512]{0,1:T(8,128)(2,1)S(1)}, u32[]{:S(2)}, u32[]{:S(2)}) collective-permute-start(bf16[96,512]{0,1:T(8,128)(2,1)S(1)} %pad_maximum_fusion.4), channel_id=1, source_target_pairs={{0,4},{1,5},{2,6},{3,7},{4,0},{5,1},{6,2},{7,3},{8,12},{9,13},{10,... | collective-permute-start | bytes 294920 | tf_op jit(solution)/shard_map/ppermute | solution.py:257
  45.5 5.5 %collective-permute-done.3 = bf16[96,512]{0,1:T(8,128)(2,1)S(1)} collective-permute-done((bf16[96,512]{0,1:T(8,128)(2,1)S(1)}, bf16[96,512]{0,1:T(8,128)(2,1)S(1)}, u32[]{:S(2)}, u32[]{:S(2)}) %collective-permute-start.3) | collective-permute-done | bytes 98336 | tf_op jit(solution)/shard_map/ppermute | solution.py:257
  51.3 4.9 %collective-permute-start.4 = (bf16[256,512]{0,1:T(8,128)(2,1)S(1)}, bf16[256,512]{0,1:T(8,128)(2,1)S(1)}, u32[]{:S(2)}, u32[]{:S(2)}) collective-permute-start(bf16[256,512]{0,1:T(8,128)(2,1)S(1)} %pad_maximum_fusion.3), channel_id=1, source_target_pairs={{0,2},{1,3},{2,0},{3,1},{4,6},{5,7},{6,4},{7,5},{8,10},{9,11},{10,... | collective-permute-start | bytes 786440 | tf_op jit(solution)/shard_map/ppermute | solution.py:259
  58.2 3.7 %collective-permute-done.4 = bf16[256,512]{0,1:T(8,128)(2,1)S(1)} collective-permute-done((bf16[256,512]{0,1:T(8,128)(2,1)S(1)}, bf16[256,512]{0,1:T(8,128)(2,1)S(1)}, u32[]{:S(2)}, u32[]{:S(2)}) %collective-permute-start.4) | collective-permute-done | bytes 262176 | tf_op jit(solution)/shard_map/ppermute | solution.py:259
  64.0 3.6 %collective-permute-done.8.refs_6_ = bf16[256,1024]{1,0:T(8,128)(2,1)} collective-permute-done((bf16[256,1024]{1,0:T(8,128)(2,1)}, bf16[256,1024]{1,0:T(8,128)(2,1)}, u32[]{:S(2)}, u32[]{:S(2)}) %collective-permute-start.8) | collective-permute-done | bytes 524320 | tf_op jit(solution)/shard_map/ppermute | solution.py:244
  67.6 2.8 %collective-permute-start.9 = (bf16[256,1024]{1,0:T(8,128)(2,1)}, bf16[256,1024]{1,0:T(8,128)(2,1)}, u32[]{:S(2)}, u32[]{:S(2)}) collective-permute-start(bf16[256,1024]{1,0:T(8,128)(2,1)} %collective-permute-done.8.refs_6_), channel_id=1, source_target_pairs={{270,0},{3,1},{286,16},{19,17},{302,32},{35,33},{318,48},{51,49},{... | collective-permute-start | bytes 1572872 | tf_op jit(solution)/shard_map/ppermute | solution.py:245
  75.7 3.3 %collective-permute-done.9.refs_7_ = bf16[256,1024]{1,0:T(8,128)(2,1)} collective-permute-done((bf16[256,1024]{1,0:T(8,128)(2,1)}, bf16[256,1024]{1,0:T(8,128)(2,1)}, u32[]{:S(2)}, u32[]{:S(2)}) %collective-permute-start.9) | collective-permute-done | bytes 524320 | tf_op jit(solution)/shard_map/ppermute | solution.py:245
  79.0 13.1 %shard_map.76 = (bf16[1024,1024]{1,0:T(8,128)(2,1)}, bf16[16,16,16,256]{3,2,1,0:T(8,128)(2,1)}, f32[128,1024]{1,0:T(8,128)}, bf16[128,1024]{1,0:T(8,128)(2,1)}, ...) custom-call(s32[2]{0:T(128)} %pad_add_fusion.pos_ref, ...), custom_call_target="tpu_custom_call" | custom-call | flops 3500000000 | bytes 14000000 | tf_op jit(solution)/shard_map/pallas_call | solution.py:161
  92.1 7.2 %all-to-all-start = ((bf16[16,16,16,256]{3,2,1,0:T(8,128)(2,1)}), bf16[16,16,16,256]{3,2,1,0:T(8,128)(2,1)S(1)}, u32[]{:S(2)}, u32[]{:S(2)}) async-start(bf16[16,16,16,256]{3,2,1,0:T(8,128)(2,1)} %get-tuple-element.20), calls=%async_computation | async-start | bytes 4194304 | tf_op jit(solution)/shard_map/all_to_all | solution.py:270
  99.3 7.3 %collective-permute-start.11 = (bf16[256,512]{1,0:T(8,128)(2,1)S(1)}, bf16[256,512]{1,0:T(8,128)(2,1)S(1)}, u32[]{:S(2)}, u32[]{:S(2)}) collective-permute-start(bf16[256,512]{1,0:T(8,128)(2,1)S(1)} %copy-done.11), channel_id=1, source_target_pairs={{0,2},{1,3},{2,0},{3,1},{4,6},{5,7},{6,4},{7,5},{8,10},{9,11},{10,... | collective-permute-start | bytes 786440 | tf_op jit(solution)/shard_map/ppermute | solution.py:292
  106.6 5.1 %collective-permute-done.11 = bf16[256,512]{1,0:T(8,128)(2,1)S(1)} collective-permute-done((bf16[256,512]{1,0:T(8,128)(2,1)S(1)}, bf16[256,512]{1,0:T(8,128)(2,1)S(1)}, u32[]{:S(2)}, u32[]{:S(2)}) %collective-permute-start.11) | collective-permute-done | bytes 262176 | tf_op jit(solution)/shard_map/ppermute | solution.py:292
  115.6 3.6 %collective-permute-done.12 = bf16[96,512]{1,0:T(8,128)(2,1)S(1)} collective-permute-done((bf16[96,512]{1,0:T(8,128)(2,1)S(1)}, bf16[96,512]{1,0:T(8,128)(2,1)S(1)}, u32[]{:S(2)}, u32[]{:S(2)}) %collective-permute-start.12) | collective-permute-done | bytes 98336 | tf_op jit(solution)/shard_map/ppermute | solution.py:294
  119.3 3.9 %collective-permute-start.13 = (bf16[32,512]{1,0:T(8,128)(2,1)S(1)}, bf16[32,512]{1,0:T(8,128)(2,1)S(1)}, u32[]{:S(2)}, u32[]{:S(2)}) collective-permute-start(bf16[32,512]{1,0:T(8,128)(2,1)S(1)} %fusion.11), channel_id=1, source_target_pairs={{0,8},{1,9},{2,10},{3,11},{4,12},{5,13},{6,14},{7,15},{8,0},{9,1},... | collective-permute-start | bytes 98312 | tf_op jit(solution)/shard_map/ppermute | solution.py:295
  123.4 5.4 %all-to-all-done = bf16[16,16,16,256]{3,2,1,0:T(8,128)(2,1)S(1)} async-done(((bf16[16,16,16,256]{3,2,1,0:T(8,128)(2,1)}), bf16[16,16,16,256]{3,2,1,0:T(8,128)(2,1)S(1)}, u32[]{:S(2)}, u32[]{:S(2)}) %all-to-all-start) | async-done | bytes 2097184 | tf_op jit(solution)/shard_map/all_to_all | solution.py:270
  129.8 4.3 %all-to-all-start.1 = ((bf16[4,4,16,256]{3,2,1,0:T(8,128)(2,1)}), bf16[4,4,16,256]{3,2,1,0:T(8,128)(2,1)S(1)}, u32[]{:S(2)}, u32[]{:S(2)}) async-start(bf16[4,4,16,256]{3,2,1,0:T(8,128)(2,1)} %copy.83), calls=%async_computation.1 | async-start | bytes 262144 | tf_op jit(solution)/shard_map/all_to_all | solution.py:276
  134.5 2.5 %all-to-all-done.1 = bf16[4,4,16,256]{3,2,1,0:T(8,128)(2,1)S(1)} async-done(((bf16[4,4,16,256]{3,2,1,0:T(8,128)(2,1)}), bf16[4,4,16,256]{3,2,1,0:T(8,128)(2,1)S(1)}, u32[]{:S(2)}, u32[]{:S(2)}) %all-to-all-start.1) | async-done | bytes 131104 | tf_op jit(solution)/shard_map/all_to_all | solution.py:276
  137.7 6.5 %all-to-all-start.2 = ((bf16[8,2,16,256]{3,2,1,0:T(8,128)(2,1)}), bf16[8,2,16,256]{3,2,1,0:T(8,128)(2,1)S(1)}, u32[]{:S(2)}, u32[]{:S(2)}) async-start(bf16[8,2,16,256]{3,2,1,0:T(8,128)(2,1)} %copy.84), calls=%async_computation.2 | async-start | bytes 262144 | tf_op jit(solution)/shard_map/all_to_all | solution.py:279
  148.5 11.9 %all-to-all-done.2 = bf16[8,2,16,256]{3,2,1,0:T(8,128)(2,1)S(1)} async-done(((bf16[8,2,16,256]{3,2,1,0:T(8,128)(2,1)}), bf16[8,2,16,256]{3,2,1,0:T(8,128)(2,1)S(1)}, u32[]{:S(2)}, u32[]{:S(2)}) %all-to-all-start.2) | async-done | bytes 131104 | tf_op jit(solution)/shard_map/all_to_all | solution.py:279
  161.1 5.9 %all-to-all-start.3 = ((bf16[16,2,16,256]{3,2,1,0:T(8,128)(2,1)}), bf16[16,2,16,256]{3,2,1,0:T(8,128)(2,1)S(1)}, u32[]{:S(2)}, u32[]{:S(2)}) async-start(bf16[16,2,16,256]{3,2,1,0:T(8,128)(2,1)} %broadcast_in_dim.14), calls=%async_computation.3 | async-start | bytes 524288 | tf_op jit(solution)/shard_map/all_to_all | solution.py:284
  168.5 6.9 %all-to-all-done.3 = bf16[16,2,16,256]{3,2,1,0:T(8,128)(2,1)S(1)} async-done(((bf16[16,2,16,256]{3,2,1,0:T(8,128)(2,1)}), bf16[16,2,16,256]{3,2,1,0:T(8,128)(2,1)S(1)}, u32[]{:S(2)}, u32[]{:S(2)}) %all-to-all-start.3) | async-done | bytes 262176 | tf_op jit(solution)/shard_map/all_to_all | solution.py:284
  (91 shorter events, 35.0 us)
Async XLA Ops:
  3.4 3.2 %collective-permute-start = (bf16[64,1024]{1,0:T(8,128)(2,1)S(1)}, bf16[64,1024]{1,0:T(8,128)(2,1)S(1)}, u32[]{:S(2)}, u32[]{:S(2)}) collective-permute-start(bf16[64,1024]{1,0:T(8,128)(2,1)S(1)} %bitcast.50), channel_id=1, source_target_pairs={{0,1},{1,0},{2,3},{3,2},{4,5},{5,4},{6,7},{7,6},{8,9},{9,8},{10,11... | collective-permute-start | bytes 393224 | tf_op jit(solution)/shard_map/ppermute | solution.py:223
  6.7 16.0 %collective-permute-start.1 = (bf16[256,1024]{0,1:T(8,128)(2,1)S(1)}, bf16[256,1024]{0,1:T(8,128)(2,1)S(1)}, u32[]{:S(2)}, u32[]{:S(2)}) collective-permute-start(bf16[256,1024]{0,1:T(8,128)(2,1)S(1)} %pad_maximum_fusion.1), channel_id=1, source_target_pairs={{0,1},{1,0},{2,3},{3,2},{4,5},{5,4},{6,7},{7,6},{8,9},{9,8},{10,11... | collective-permute-start | bytes 1572872 | tf_op jit(solution)/shard_map/ppermute | solution.py:223
  8.8 11.7 %collective-permute-start.6 = (bf16[128,1024]{1,0:T(8,128)(2,1)S(1)}, bf16[128,1024]{1,0:T(8,128)(2,1)S(1)}, u32[]{:S(2)}, u32[]{:S(2)}) collective-permute-start(bf16[128,1024]{1,0:T(8,128)(2,1)S(1)} %maximum_select_fusion.4), channel_id=1, source_target_pairs={{2,0},{271,1},{18,16},{287,17},{34,32},{303,33},{50,48},{319,49},{... | collective-permute-start | bytes 786440 | tf_op jit(solution)/shard_map/ppermute | solution.py:240
  20.7 35.5 %collective-permute-start.7 = (bf16[256,1024]{1,0:T(8,128)(2,1)S(1)}, bf16[256,1024]{1,0:T(8,128)(2,1)}, u32[]{:S(2)}, u32[]{:S(2)}) collective-permute-start(bf16[256,1024]{1,0:T(8,128)(2,1)S(1)} %maximum_select_fusion.3.refs_4_), channel_id=1, source_target_pairs={{270,0},{3,1},{286,16},{19,17},{302,32},{35,33},{318,48},{51,49},{... | collective-permute-start | bytes 1572872 | tf_op jit(solution)/shard_map/ppermute | solution.py:243
  23.4 12.5 %collective-permute-start.2 = (bf16[32,512]{0,1:T(8,128)(2,1)S(1)}, bf16[32,512]{0,1:T(8,128)(2,1)S(1)}, u32[]{:S(2)}, u32[]{:S(2)}) collective-permute-start(bf16[32,512]{0,1:T(8,128)(2,1)S(1)} %slice.75), channel_id=1, source_target_pairs={{0,8},{1,9},{2,10},{3,11},{4,12},{5,13},{6,14},{7,15},{8,0},{9,1},... | collective-permute-start | bytes 98312 | tf_op jit(solution)/shard_map/ppermute | solution.py:256
  36.0 15.0 %collective-permute-start.3 = (bf16[96,512]{0,1:T(8,128)(2,1)S(1)}, bf16[96,512]{0,1:T(8,128)(2,1)S(1)}, u32[]{:S(2)}, u32[]{:S(2)}) collective-permute-start(bf16[96,512]{0,1:T(8,128)(2,1)S(1)} %pad_maximum_fusion.4), channel_id=1, source_target_pairs={{0,4},{1,5},{2,6},{3,7},{4,0},{5,1},{6,2},{7,3},{8,12},{9,13},{10,... | collective-permute-start | bytes 294920 | tf_op jit(solution)/shard_map/ppermute | solution.py:257
  51.3 10.6 %collective-permute-start.4 = (bf16[256,512]{0,1:T(8,128)(2,1)S(1)}, bf16[256,512]{0,1:T(8,128)(2,1)S(1)}, u32[]{:S(2)}, u32[]{:S(2)}) collective-permute-start(bf16[256,512]{0,1:T(8,128)(2,1)S(1)} %pad_maximum_fusion.3), channel_id=1, source_target_pairs={{0,2},{1,3},{2,0},{3,1},{4,6},{5,7},{6,4},{7,5},{8,10},{9,11},{10,... | collective-permute-start | bytes 786440 | tf_op jit(solution)/shard_map/ppermute | solution.py:259
  56.2 11.4 %collective-permute-start.8 = (bf16[256,1024]{1,0:T(8,128)(2,1)}, bf16[256,1024]{1,0:T(8,128)(2,1)}, u32[]{:S(2)}, u32[]{:S(2)}) collective-permute-start(bf16[256,1024]{1,0:T(8,128)(2,1)} %collective-permute-done.7.refs_5_), channel_id=1, source_target_pairs={{2,0},{271,1},{18,16},{287,17},{34,32},{303,33},{50,48},{319,49},{... | collective-permute-start | bytes 1572872 | tf_op jit(solution)/shard_map/ppermute | solution.py:244
  62.1 10.2 %collective-permute-start.5 = (bf16[384,512]{0,1:T(8,128)(2,1)S(1)}, bf16[384,512]{0,1:T(8,128)(2,1)S(1)}, u32[]{:S(2)}, u32[]{:S(2)}) collective-permute-start(bf16[384,512]{0,1:T(8,128)(2,1)S(1)} %pad_maximum_fusion.2), channel_id=1, source_target_pairs={{0,1},{1,0},{2,3},{3,2},{4,5},{5,4},{6,7},{7,6},{8,9},{9,8},{10,11... | collective-permute-start | bytes 1179656 | tf_op jit(solution)/shard_map/ppermute | solution.py:223
  67.6 11.4 %collective-permute-start.9 = (bf16[256,1024]{1,0:T(8,128)(2,1)}, bf16[256,1024]{1,0:T(8,128)(2,1)}, u32[]{:S(2)}, u32[]{:S(2)}) collective-permute-start(bf16[256,1024]{1,0:T(8,128)(2,1)} %collective-permute-done.8.refs_6_), channel_id=1, source_target_pairs={{270,0},{3,1},{286,16},{19,17},{302,32},{35,33},{318,48},{51,49},{... | collective-permute-start | bytes 1572872 | tf_op jit(solution)/shard_map/ppermute | solution.py:245
  92.1 19.6 %copy-start.4 = (f32[128,512]{1,0:T(8,128)S(1)}, f32[128,512]{1,0:T(8,128)}, u32[]{:S(2)}) copy-start(f32[128,512]{1,0:T(8,128)} %get-tuple-element.18) | copy-start | bytes 786436
  92.1 31.1 %copy-start.10 = (bf16[256,64]{1,0:T(8,128)(2,1)S(1)}, bf16[256,64]{1,0:T(8,128)(2,1)}, u32[]{:S(2)}) copy-start(bf16[256,64]{1,0:T(8,128)(2,1)} %constant.41) | copy-start | bytes 98308
  92.1 36.7 %all-to-all-start = ((bf16[16,16,16,256]{3,2,1,0:T(8,128)(2,1)}), bf16[16,16,16,256]{3,2,1,0:T(8,128)(2,1)S(1)}, u32[]{:S(2)}, u32[]{:S(2)}) async-start(bf16[16,16,16,256]{3,2,1,0:T(8,128)(2,1)} %get-tuple-element.20), calls=%async_computation | async-start | bytes 4194304 | tf_op jit(solution)/shard_map/all_to_all | solution.py:270
  99.3 12.4 %collective-permute-start.11 = (bf16[256,512]{1,0:T(8,128)(2,1)S(1)}, bf16[256,512]{1,0:T(8,128)(2,1)S(1)}, u32[]{:S(2)}, u32[]{:S(2)}) collective-permute-start(bf16[256,512]{1,0:T(8,128)(2,1)S(1)} %copy-done.11), channel_id=1, source_target_pairs={{0,2},{1,3},{2,0},{3,1},{4,6},{5,7},{6,4},{7,5},{8,10},{9,11},{10,... | collective-permute-start | bytes 786440 | tf_op jit(solution)/shard_map/ppermute | solution.py:292
  111.7 7.5 %collective-permute-start.12 = (bf16[96,512]{1,0:T(8,128)(2,1)S(1)}, bf16[96,512]{1,0:T(8,128)(2,1)S(1)}, u32[]{:S(2)}, u32[]{:S(2)}) collective-permute-start(bf16[96,512]{1,0:T(8,128)(2,1)S(1)} %pad_maximum_fusion.6), channel_id=1, source_target_pairs={{0,4},{1,5},{2,6},{3,7},{4,0},{5,1},{6,2},{7,3},{8,12},{9,13},{10,... | collective-permute-start | bytes 294920 | tf_op jit(solution)/shard_map/ppermute | solution.py:294
  113.7 53.3 %collective-permute-start.10 = (bf16[128,1024]{1,0:T(8,128)(2,1)}, bf16[128,1024]{1,0:T(8,128)(2,1)S(1)}, u32[]{:S(2)}, u32[]{:S(2)}) collective-permute-start(bf16[128,1024]{1,0:T(8,128)(2,1)} %get-tuple-element.14), channel_id=1, source_target_pairs={{0,1},{1,0},{2,3},{3,2},{4,5},{5,4},{6,7},{7,6},{8,9},{9,8},{10,11... | collective-permute-start | bytes 786440 | tf_op jit(solution)/shard_map/ppermute | solution.py:223
  119.3 14.8 %copy-start.9 = (bf16[256,32]{1,0:T(8,128)(2,1)S(1)}, bf16[256,32]{1,0:T(8,128)(2,1)}, u32[]{:S(2)}) copy-start(bf16[256,32]{1,0:T(8,128)(2,1)} %constant.42) | copy-start | bytes 49156
  119.3 14.7 %collective-permute-start.13 = (bf16[32,512]{1,0:T(8,128)(2,1)S(1)}, bf16[32,512]{1,0:T(8,128)(2,1)S(1)}, u32[]{:S(2)}, u32[]{:S(2)}) collective-permute-start(bf16[32,512]{1,0:T(8,128)(2,1)S(1)} %fusion.11), channel_id=1, source_target_pairs={{0,8},{1,9},{2,10},{3,11},{4,12},{5,13},{6,14},{7,15},{8,0},{9,1},... | collective-permute-start | bytes 98312 | tf_op jit(solution)/shard_map/ppermute | solution.py:295
  123.4 10.9 %copy-start.8 = (bf16[256,128]{1,0:T(8,128)(2,1)S(1)}, bf16[256,128]{1,0:T(8,128)(2,1)}, u32[]{:S(2)}) copy-start(bf16[256,128]{1,0:T(8,128)(2,1)} %constant.40) | copy-start | bytes 196612
  129.8 7.2 %all-to-all-start.1 = ((bf16[4,4,16,256]{3,2,1,0:T(8,128)(2,1)}), bf16[4,4,16,256]{3,2,1,0:T(8,128)(2,1)S(1)}, u32[]{:S(2)}, u32[]{:S(2)}) async-start(bf16[4,4,16,256]{3,2,1,0:T(8,128)(2,1)} %copy.83), calls=%async_computation.1 | async-start | bytes 262144 | tf_op jit(solution)/shard_map/all_to_all | solution.py:276
  137.7 22.6 %all-to-all-start.2 = ((bf16[8,2,16,256]{3,2,1,0:T(8,128)(2,1)}), bf16[8,2,16,256]{3,2,1,0:T(8,128)(2,1)S(1)}, u32[]{:S(2)}, u32[]{:S(2)}) async-start(bf16[8,2,16,256]{3,2,1,0:T(8,128)(2,1)} %copy.84), calls=%async_computation.2 | async-start | bytes 262144 | tf_op jit(solution)/shard_map/all_to_all | solution.py:279
  146.3 20.6 %copy-start.1 = (f32[128,1024]{1,0:T(8,128)S(1)}, f32[128,1024]{1,0:T(8,128)}, u32[]{:S(2)}) copy-start(f32[128,1024]{1,0:T(8,128)} %get-tuple-element.13) | copy-start | bytes 1572868
  146.4 21.3 %collective-permute-start.14 = (bf16[128,1024]{1,0:T(8,128)(2,1)S(1)}, bf16[128,1024]{1,0:T(8,128)(2,1)S(1)}, u32[]{:S(2)}, u32[]{:S(2)}) collective-permute-start(bf16[128,1024]{1,0:T(8,128)(2,1)S(1)} %dynamic-slice_convert_fusion), channel_id=1, source_target_pairs={{0,1},{1,0},{2,3},{3,2},{4,5},{5,4},{6,7},{7,6},{8,9},{9,8},{10,11... | collective-permute-start | bytes 786440 | tf_op jit(solution)/shard_map/ppermute | solution.py:223
  161.1 14.3 %all-to-all-start.3 = ((bf16[16,2,16,256]{3,2,1,0:T(8,128)(2,1)}), bf16[16,2,16,256]{3,2,1,0:T(8,128)(2,1)S(1)}, u32[]{:S(2)}, u32[]{:S(2)}) async-start(bf16[16,2,16,256]{3,2,1,0:T(8,128)(2,1)} %broadcast_in_dim.14), calls=%async_computation.3 | async-start | bytes 524288 | tf_op jit(solution)/shard_map/all_to_all | solution.py:284
  (8 other events, 49.2 us)

commit v4 on v3

--- a/solution.py
+++ b/solution.py
@@ -26,11 +26,11 @@
 
 
 def layer_kernel(nx, ny, pos_ref, *refs):
-    sources, refs = refs[:8], refs[8:]
+    sources, refs = refs[:12], refs[12:]
     results, refs = refs[:8], refs[8:]
     staged, refs = refs[:8], refs[8:]
     (tok_s, tokt_s, g_s, gt_s, kv_s, kvt_s, qm_s, gm_s, gkv_s, attt_s, dqt_s, att_s, in_sem, w_sem, out_sem, part_sem) = refs
-    tok, tokt, g, gt, n1, n2, n3, n4 = sources
+    own, ownt, mine, minet, other, othert, g, gt, n1, n2, n3, n4 = sources
     w_s, part_s, lown_s, lsend_s, dq_s, gown_s, gkeep_s, gsend_s = staged
     zl = pos_ref[0]
     core = pos_ref[1]
@@ -43,13 +43,23 @@
             row = pl.multiple_of(lax.rem(start + k + 8, 8) * 128, 128)
             moves.append((piece.at[pl.ds(128 * k, 128), :], w_s.at[pl.ds(row, 128), :]))
     weight_copies = [pltpu.make_async_copy(src, dst, w_sem.at[i]) for i, (src, dst) in enumerate(moves)]
-    inputs = [pltpu.make_async_copy(src, dst, in_sem.at[i])
-              for i, (src, dst) in enumerate(((tok, tok_s), (g, g_s), (tokt, tokt_s), (gt, gt_s)))]
-    for copy in inputs[:1] + weight_copies + inputs[1:]:
+    here = pl.ds(pl.multiple_of(core * 512, 512), 512)
+    there = pl.ds(pl.multiple_of((1 - core) * 512, 512), 512)
+    pairs = (
+        (own, tok_s.at[pl.ds(0, 256), :]),
+        (mine, tok_s.at[pl.ds(256, 384), here]),
+        (other, tok_s.at[pl.ds(256, 384), there]),
+        (g, g_s),
+        (ownt, tokt_s.at[:, pl.ds(0, 256)]),
+        (minet, tokt_s.at[here, pl.ds(256, 384)]),
+        (othert, tokt_s.at[there, pl.ds(256, 384)]),
+        (gt, gt_s),
+    )
+    inputs = [pltpu.make_async_copy(src, dst, in_sem.at[i]) for i, (src, dst) in enumerate(pairs)]
+    for copy in inputs[:3] + weight_copies + inputs[3:]:
         copy.start()
     outputs = {i: pltpu.make_async_copy(staged[i], results[i], out_sem.at[i]) for i in (0, 2, 3, 4, 5, 6, 7)}
-    inputs[0].wait()
-    for copy in weight_copies:
+    for copy in inputs[:3] + weight_copies:
         copy.wait()
     outputs[0].start()
 
@@ -62,7 +72,7 @@
 
     lax.fori_loop(0, 5, project_keys, 0)
     queries = nn(tok_s[0:256, :], w_s[:, 0:256]) * 0.125
-    inputs[1].wait()
+    inputs[3].wait()
     grads = nn(g_s[...], w_s[:, 768:1024])
     lane = lax.broadcasted_iota(jnp.int32, (256, 128), 1)
     for head in range(4):
@@ -112,15 +122,15 @@
 
     x_rows = 64 // nx
     y_cols = 1024 // ny
-    inputs[2].wait()
-    inputs[3].wait()
-
-    def part_copy(step):
-        where = pl.ds(2 * step, 2)
-        return pltpu.make_async_copy(part_s.at[:, where], results[1].at[:, where], part_sem.at[step])
-
-    def grad_rows(step, carry):
-        rows = pl.ds(pl.multiple_of(step * 128, 128), 128)
+    for copy in inputs[4:]:
+        copy.wait()
+
+    def part_copy(low):
+        where = pl.ds(8 * low, 8)
+        return pltpu.make_async_copy(part_s.at[:, where], results[1].at[:, where], part_sem.at[low])
+
+    def grad_rows(low, quad, carry):
+        rows = pl.ds(pl.multiple_of((2 * quad + low) * 128, 128), 128)
         lhs = tokt_s[rows, :]
         att_all = jnp.concatenate([att_s[0], att_s[1]], axis=0)
         block = jnp.concatenate(
@@ -129,18 +139,19 @@
         for side in range(2):
             for x in range(nx):
                 for y in range(ny):
-                    part_s[x * ny + y, 2 * step + side] = block[
+                    part_s[x * ny + y, (2 * low + side) * 4 + quad] = block[
                         side * 64 + x * x_rows:side * 64 + (x + 1) * x_rows, y * y_cols:(y + 1) * y_cols]
-        part_copy(step).start()
         return carry
 
-    lax.fori_loop(0, 8, grad_rows, 0)
+    for low in range(2):
+        lax.fori_loop(0, 4, functools.partial(grad_rows, low), 0)
+        part_copy(low).start()
     lown_s[...] = nt(att_s[core], w_s[:, 768:1024])
     lsend_s[...] = nt(att_s[1 - core], w_s[:, 768:1024]).astype(BF)
     outputs[2].start()
     outputs[3].start()
-    for step in range(8):
-        part_copy(step).wait()
+    for low in range(2):
+        part_copy(low).wait()
     for index in (0, 2, 3, 4, 5, 6, 7):
         outputs[index].wait()
 
@@ -176,10 +187,10 @@
             pltpu.VMEM((256, 256), F32),
             pltpu.VMEM((256, 256), F32),
             pltpu.VMEM((2, 128, 256), BF),
-            pltpu.SemaphoreType.DMA((4,)),
             pltpu.SemaphoreType.DMA((8,)),
             pltpu.SemaphoreType.DMA((8,)),
             pltpu.SemaphoreType.DMA((8,)),
+            pltpu.SemaphoreType.DMA((2,)),
         ],
         compiler_params=pltpu.CompilerParams(vmem_limit_bytes=60 * 1024 * 1024),
         cost_estimate=pl.CostEstimate(flops=3_500_000_000, bytes_accessed=14_000_000, transcendentals=700_000),
@@ -232,38 +243,41 @@
             return jnp.where(first, jnp.concatenate([mine, other], axis), jnp.concatenate([other, mine], axis))
 
         both = ("dp", "seq")
-        shard = stacked.reshape(64, 4, 2, 256)
-        keep = lax.dynamic_index_in_dim(shard, core, 2, False).reshape(64, 1024)
-        give = lax.dynamic_index_in_dim(shard, 1 - core, 2, False).reshape(64, 1024)
+        def shard_half(which):
+            return lax.dynamic_slice(stacked, (0, 0, which * 256), (64, 4, 256)).reshape(64, 1024)
+
+        keep, give = shard_half(core), shard_half(1 - core)
         shard_got = swap_core(give)
         w0 = ordered(keep, shard_got, 0)
         w1 = lax.ppermute(w0, both, swap_even)
         even = (zl + core) & 1 == 0
         n1 = jnp.where(even, jnp.concatenate([w0, w1], 0), jnp.concatenate([w1, w0], 0))
-        n2 = lax.ppermute(n1, both, swap_odd)
-        n3 = lax.ppermute(n2, both, swap_even)
-        n4 = lax.ppermute(n3, both, swap_odd)
 
         own = jnp.concatenate([tokens[0], grad_out[0]], axis=0)
-        own, _ = lax.optimization_barrier((own, shard_got))
         got = swap_core(own)
         chip_tokens = ordered(own[0:128], got[0:128], 0)
         chip_grads = ordered(own[128:256], got[128:256], 0)
         matrix = jnp.asarray(coarse_matrix, BF)
         half_tokens = lax.dynamic_slice(chip_tokens, (0, core * 512), (256, 512))
         coarse = nn(matrix, half_tokens).astype(BF)
+        n1, coarse = lax.optimization_barrier((n1, coarse))
         c1, c2, c3 = coarse[0:128], coarse[128:192], coarse[192:224]
+        n2 = lax.ppermute(n1, both, swap_odd)
         t3 = lax.ppermute(c3, "seq", chip_swap(2))
+        n2, t3 = lax.optimization_barrier((n2, t3))
+        n3 = lax.ppermute(n2, both, swap_even)
         second = lax.ppermute(jnp.concatenate([c2, t3], 0), "seq", chip_swap(1))
+        n3, second = lax.optimization_barrier((n3, second))
+        n4 = lax.ppermute(n3, both, swap_odd)
         held = jnp.concatenate([second[0:64], t3, second[64:96]], 0)
         third = lax.ppermute(jnp.concatenate([c1, held], 0), "seq", chip_swap(0))
         half_set = jnp.concatenate([held, third], 0)
-        rest = ordered(half_set, swap_core(half_set), 1)
-        token_set = jnp.concatenate([chip_tokens, rest], 0)
+        other_set = swap_core(half_set)
 
         position = jnp.stack([zl, core]).astype(jnp.int32)
         (weight, part, layer_own, layer_send, dquery, grad_own, grad_keep, grad_send) = run_layer(
-            nx, ny, position, token_set, token_set.T, chip_grads, chip_grads.T,
+            nx, ny, position, chip_tokens, chip_tokens.T, half_set, half_set.T, other_set, other_set.T,
+            chip_grads, chip_grads.T,
             n1, n2, n3, n4)
 
         if nxy > 1:
@@ -272,7 +286,7 @@
             pieces = part
         plane_sum = jnp.sum(pieces.astype(F32), axis=0).astype(BF)
         rows, cols = 64 // nx, 1024 // ny
-        by_chip = plane_sum.reshape(4, 4, rows, cols).transpose(1, 0, 2, 3)
+        by_chip = plane_sum.reshape(4, 4, rows, cols)
         by_chip = lax.all_to_all(by_chip, "seq", 0, 0, axis_index_groups=quad_groups, tiled=True)
         quad_sum = jnp.sum(by_chip.astype(F32).reshape(2, 2, 4, rows, cols), axis=0).astype(BF)
         by_quad = quad_sum.transpose(1, 0, 2, 3)

time: 178 us -> 184 us (1.034)
  starting transfers between devices: 82.7 us -> 87.9 us
    ppermute x1, starting transfers between devices: 9.44 us -> 1.92 us  [per_device(): second = lax.ppermute(jnp.concatenate([c2, t3], 0), 'seq', chip_swap(1))]
    all_to_all x1, starting transfers between devices: 6.52 us -> 12.8 us  [per_device(): lax.all_to_all(jnp.concatenate([by_quad] * nzh, axis=0), both, 0, 0, axis...]
    ppermute x1, starting transfers between devices: 1.92 us -> 8.03 us  [per_device(): n3 = lax.ppermute(n2, both, swap_even)]
    ppermute x1, waiting for transfers between devices: 4.95 us -> 8.73 us  [per_device(): t3 = lax.ppermute(c3, 'seq', chip_swap(2))]
    ppermute x1, starting transfers between devices: 7.27 us -> 3.91 us  [per_device(): b1 = lax.ppermute(grad_send, 'seq', chip_swap(0))]
    ppermute x1, waiting for transfers between devices: 3.34 us -> 0.01 us  [per_device(): n4 = lax.ppermute(n3, both, swap_odd)]
    ppermute x1, starting transfers between devices: 3.87 us -> 7.2 us  [per_device(): lax.ppermute((joined[64:96] + b2[64:96].astype(F32)).astype(BF), 'seq', c...]
    ppermute x1, waiting for transfers between devices: 3.63 us -> 1.12 us  [per_device(): n3 = lax.ppermute(n2, both, swap_even)]
  transfers between devices with their start and end apart: 19 -> 19, of which waited for: 13 -> 11; matrix products, arithmetic and copies ran while one was open for 8% -> 8% of each run, Pallas kernels for 0% -> 0%
where the time goes in v4:
time: 184 us; the launch traced here: 183 us
  starting transfers between devices  87.9 us (48%)
  waiting for transfers between devices  61.6 us (33%)
  Pallas kernels  13 us (7%)
  local copies, waits for them, and re-layouts  10.8 us (6%)
  other arithmetic  5.47 us (3%)
  matrix products  2.91 us (2%)
    pallas_call x1, Pallas kernels, run_layer(): pl.pallas_call(functools.partial(layer_kernel, nx, ny), out_shape=tuple((...  13 us
    all_to_all x1, starting transfers between devices, per_device(): lax.all_to_all(jnp.concatenate([by_quad] * nzh, axis=0), both, 0, 0, axis...  12.8 us
    all_to_all x1, waiting for transfers between devices, per_device(): lax.all_to_all(jnp.concatenate([by_quad] * nzh, axis=0), both, 0, 0, axis...  11.9 us
    ppermute x5, starting transfers between devices, swap_core(): return lax.ppermute(value, 'seq', core_pairs)  10.2 us
    ppermute x1, waiting for transfers between devices, per_device(): t3 = lax.ppermute(c3, 'seq', chip_swap(2))  8.73 us
    ppermute x1, starting transfers between devices, per_device(): n3 = lax.ppermute(n2, both, swap_even)  8.03 us
    ppermute x1, starting transfers between devices, per_device(): t3 = lax.ppermute(c3, 'seq', chip_swap(2))  7.53 us
    ppermute x1, starting transfers between devices, per_device(): w1 = lax.ppermute(w0, both, swap_even)  7.39 us
  transfers between devices with their start and end apart: 19, of which 11 were waited for; matrix products, arithmetic and copies ran while one was open for 8% of the time, Pallas kernels for 0%

profile of v4, /device:TPU:32, one launch (start us, length us, event | category | flops | bytes accessed | tf_op | source)
XLA Modules:
  0.0 182.9 jit_solution(4613632302565457862)
XLA Ops:
  6.0 2.5 %collective-permute-start = (bf16[256,1024]{0,1:T(8,128)(2,1)S(1)}, bf16[256,1024]{0,1:T(8,128)(2,1)S(1)}, u32[]{:S(2)}, u32[]{:S(2)}) collective-permute-start(bf16[256,1024]{0,1:T(8,128)(2,1)S(1)} %pad_maximum_fusion.1), channel_id=1, source_target_pairs={{0,1},{1,0},{2,3},{3,2},{4,5},{5,4},{6,7},{7,6},{8,9},{9,8},{10,11... | collective-permute-start | bytes 1572872 | tf_op jit(solution)/shard_map/ppermute | solution.py:234
  8.6 7.4 %collective-permute-start.2 = (bf16[128,1024]{1,0:T(8,128)(2,1)S(1)}, bf16[128,1024]{1,0:T(8,128)(2,1)S(1)}, u32[]{:S(2)}, u32[]{:S(2)}) collective-permute-start(bf16[128,1024]{1,0:T(8,128)(2,1)S(1)} %maximum_select_fusion.1), channel_id=1, source_target_pairs={{2,0},{271,1},{18,16},{287,17},{34,32},{303,33},{50,48},{319,49},{... | collective-permute-start | bytes 786440 | tf_op jit(solution)/shard_map/ppermute | solution.py:252
  16.0 4.3 %collective-permute-done.2 = bf16[128,1024]{1,0:T(8,128)(2,1)S(1)} collective-permute-done((bf16[128,1024]{1,0:T(8,128)(2,1)S(1)}, bf16[128,1024]{1,0:T(8,128)(2,1)S(1)}, u32[]{:S(2)}, u32[]{:S(2)}) %collective-permute-start.2) | collective-permute-done | bytes 262176 | tf_op jit(solution)/shard_map/ppermute | solution.py:252
  23.2 7.5 %collective-permute-start.4 = (bf16[32,512]{0,1:T(8,128)(2,1)S(1)}, bf16[32,512]{0,1:T(8,128)(2,1)S(1)}, u32[]{:S(2)}, u32[]{:S(2)}) collective-permute-start(bf16[32,512]{0,1:T(8,128)(2,1)S(1)} %slice.48), channel_id=1, source_target_pairs={{0,8},{1,9},{2,10},{3,11},{4,12},{5,13},{6,14},{7,15},{8,0},{9,1},... | collective-permute-start | bytes 98312 | tf_op jit(solution)/shard_map/ppermute | solution.py:266
  30.8 8.7 %collective-permute-done.4 = bf16[32,512]{0,1:T(8,128)(2,1)S(1)} collective-permute-done((bf16[32,512]{0,1:T(8,128)(2,1)S(1)}, bf16[32,512]{0,1:T(8,128)(2,1)S(1)}, u32[]{:S(2)}, u32[]{:S(2)}) %collective-permute-start.4) | collective-permute-done | bytes 32800 | tf_op jit(solution)/shard_map/ppermute | solution.py:266
  39.5 8.0 %collective-permute-start.5 = (bf16[256,1024]{1,0:T(8,128)(2,1)S(1)}, bf16[256,1024]{1,0:T(8,128)(2,1)}, u32[]{:S(2)}, u32[]{:S(2)}) collective-permute-start(bf16[256,1024]{1,0:T(8,128)(2,1)S(1)} %collective-permute-done.3.refs_9_), channel_id=1, source_target_pairs={{2,0},{271,1},{18,16},{287,17},{34,32},{303,33},{50,48},{319,49},{... | collective-permute-start | bytes 1572872 | tf_op jit(solution)/shard_map/ppermute | solution.py:268
  49.6 6.3 %collective-permute-done.6 = bf16[96,512]{0,1:T(8,128)(2,1)S(1)} collective-permute-done((bf16[96,512]{0,1:T(8,128)(2,1)S(1)}, bf16[96,512]{0,1:T(8,128)(2,1)S(1)}, u32[]{:S(2)}, u32[]{:S(2)}) %collective-permute-start.6) | collective-permute-done | bytes 98336 | tf_op jit(solution)/shard_map/ppermute | solution.py:269
  57.3 4.5 %collective-permute-start.7 = (bf16[256,512]{0,1:T(8,128)(2,1)S(1)}, bf16[256,512]{0,1:T(8,128)(2,1)S(1)}, u32[]{:S(2)}, u32[]{:S(2)}) collective-permute-start(bf16[256,512]{0,1:T(8,128)(2,1)S(1)} %pad_maximum_fusion.4), channel_id=1, source_target_pairs={{0,2},{1,3},{2,0},{3,1},{4,6},{5,7},{6,4},{7,5},{8,10},{9,11},{10,... | collective-permute-start | bytes 786440 | tf_op jit(solution)/shard_map/ppermute | solution.py:273
  63.7 5.3 %collective-permute-done.7 = bf16[256,512]{0,1:T(8,128)(2,1)S(1)} collective-permute-done((bf16[256,512]{0,1:T(8,128)(2,1)S(1)}, bf16[256,512]{0,1:T(8,128)(2,1)S(1)}, u32[]{:S(2)}, u32[]{:S(2)}) %collective-permute-start.7) | collective-permute-done | bytes 262176 | tf_op jit(solution)/shard_map/ppermute | solution.py:273
  76.9 13.0 %shard_map.76 = (bf16[1024,1024]{1,0:T(8,128)(2,1)}, bf16[16,16,16,256]{3,2,1,0:T(8,128)(2,1)}, f32[128,1024]{1,0:T(8,128)}, bf16[128,1024]{1,0:T(8,128)(2,1)}, ...) custom-call(s32[2]{0:T(128)} %pad_add_fusion.pos_ref, ...), custom_call_target="tpu_custom_call" | custom-call | flops 3500000000 | bytes 14000000 | tf_op jit(solution)/shard_map/pallas_call | solution.py:172
  89.9 7.0 %all-to-all-start = ((bf16[16,16,16,256]{3,2,1,0:T(8,128)(2,1)}), bf16[16,16,16,256]{3,2,1,0:T(8,128)(2,1)S(1)}, u32[]{:S(2)}, u32[]{:S(2)}) async-start(bf16[16,16,16,256]{3,2,1,0:T(8,128)(2,1)} %get-tuple-element.30), calls=%async_computation | async-start | bytes 4194304 | tf_op jit(solution)/shard_map/all_to_all | solution.py:284
  97.0 3.9 %collective-permute-start.11 = (bf16[256,512]{1,0:T(8,128)(2,1)S(1)}, bf16[256,512]{1,0:T(8,128)(2,1)S(1)}, u32[]{:S(2)}, u32[]{:S(2)}) collective-permute-start(bf16[256,512]{1,0:T(8,128)(2,1)S(1)} %copy-done.12), channel_id=1, source_target_pairs={{0,2},{1,3},{2,0},{3,1},{4,6},{5,7},{6,4},{7,5},{8,10},{9,11},{10,... | collective-permute-start | bytes 786440 | tf_op jit(solution)/shard_map/ppermute | solution.py:306
  100.9 6.7 %collective-permute-done.11 = bf16[256,512]{1,0:T(8,128)(2,1)S(1)} collective-permute-done((bf16[256,512]{1,0:T(8,128)(2,1)S(1)}, bf16[256,512]{1,0:T(8,128)(2,1)S(1)}, u32[]{:S(2)}, u32[]{:S(2)}) %collective-permute-start.11) | collective-permute-done | bytes 262176 | tf_op jit(solution)/shard_map/ppermute | solution.py:306
  107.7 2.7 %collective-permute-start.12 = (bf16[96,512]{1,0:T(8,128)(2,1)S(1)}, bf16[96,512]{1,0:T(8,128)(2,1)S(1)}, u32[]{:S(2)}, u32[]{:S(2)}) collective-permute-start(bf16[96,512]{1,0:T(8,128)(2,1)S(1)} %pad_maximum_fusion.7), channel_id=1, source_target_pairs={{0,4},{1,5},{2,6},{3,7},{4,0},{5,1},{6,2},{7,3},{8,12},{9,13},{10,... | collective-permute-start | bytes 294920 | tf_op jit(solution)/shard_map/ppermute | solution.py:308
  112.3 2.8 %collective-permute-done.12 = bf16[96,512]{1,0:T(8,128)(2,1)S(1)} collective-permute-done((bf16[96,512]{1,0:T(8,128)(2,1)S(1)}, bf16[96,512]{1,0:T(8,128)(2,1)S(1)}, u32[]{:S(2)}, u32[]{:S(2)}) %collective-permute-start.12) | collective-permute-done | bytes 98336 | tf_op jit(solution)/shard_map/ppermute | solution.py:308
  115.1 7.2 %collective-permute-start.13 = (bf16[32,512]{1,0:T(8,128)(2,1)S(1)}, bf16[32,512]{1,0:T(8,128)(2,1)S(1)}, u32[]{:S(2)}, u32[]{:S(2)}) collective-permute-start(bf16[32,512]{1,0:T(8,128)(2,1)S(1)} %fusion.13), channel_id=1, source_target_pairs={{0,8},{1,9},{2,10},{3,11},{4,12},{5,13},{6,14},{7,15},{8,0},{9,1},... | collective-permute-start | bytes 98312 | tf_op jit(solution)/shard_map/ppermute | solution.py:309
  122.5 5.1 %all-to-all-done = bf16[16,16,16,256]{3,2,1,0:T(8,128)(2,1)S(1)} async-done(((bf16[16,16,16,256]{3,2,1,0:T(8,128)(2,1)}), bf16[16,16,16,256]{3,2,1,0:T(8,128)(2,1)S(1)}, u32[]{:S(2)}, u32[]{:S(2)}) %all-to-all-start) | async-done | bytes 2097184 | tf_op jit(solution)/shard_map/all_to_all | solution.py:284
  128.5 5.4 %all-to-all-start.1 = ((bf16[4,4,16,256]{3,2,1,0:T(8,128)(2,1)}), bf16[4,4,16,256]{3,2,1,0:T(8,128)(2,1)S(1)}, u32[]{:S(2)}, u32[]{:S(2)}) async-start(bf16[4,4,16,256]{3,2,1,0:T(8,128)(2,1)} %bitcast.12), calls=%async_computation.1 | async-start | bytes 262144 | tf_op jit(solution)/shard_map/all_to_all | solution.py:290
  134.4 2.5 %all-to-all-done.1 = bf16[4,4,16,256]{3,2,1,0:T(8,128)(2,1)S(1)} async-done(((bf16[4,4,16,256]{3,2,1,0:T(8,128)(2,1)}), bf16[4,4,16,256]{3,2,1,0:T(8,128)(2,1)S(1)}, u32[]{:S(2)}, u32[]{:S(2)}) %all-to-all-start.1) | async-done | bytes 131104 | tf_op jit(solution)/shard_map/all_to_all | solution.py:290
  137.7 12.8 %all-to-all-start.2 = ((bf16[8,2,16,256]{3,2,1,0:T(8,128)(2,1)}), bf16[8,2,16,256]{3,2,1,0:T(8,128)(2,1)S(1)}, u32[]{:S(2)}, u32[]{:S(2)}) async-start(bf16[8,2,16,256]{3,2,1,0:T(8,128)(2,1)} %copy.69), calls=%async_computation.2 | async-start | bytes 262144 | tf_op jit(solution)/shard_map/all_to_all | solution.py:293
  150.6 2.1 %fusion = f32[256,1024]{1,0:T(8,128)S(1)} fusion(bf16[1024,1024]{1,0:T(8,128)(2,1)} %get-tuple-element.29, bf16[256,512]{1,0:T(8,128)(2,1)S(1)} %add_convert_fusion.1, bf16[256,256]{1,0:T(8,128)(2,1)S(1)} %copy-done.13), kind=kOutput, calls=%fused_computation | convolution fusion | flops 403439616 | bytes 3014656 | tf_op jit(solution)/shard_map/dot_general | solution.py:25
  154.6 11.9 %all-to-all-done.2 = bf16[8,2,16,256]{3,2,1,0:T(8,128)(2,1)S(1)} async-done(((bf16[8,2,16,256]{3,2,1,0:T(8,128)(2,1)}), bf16[8,2,16,256]{3,2,1,0:T(8,128)(2,1)S(1)}, u32[]{:S(2)}, u32[]{:S(2)}) %all-to-all-start.2) | async-done | bytes 131104 | tf_op jit(solution)/shard_map/all_to_all | solution.py:293
  167.3 5.3 %all-to-all-start.3 = ((bf16[16,2,16,256]{3,2,1,0:T(8,128)(2,1)}), bf16[16,2,16,256]{3,2,1,0:T(8,128)(2,1)S(1)}, u32[]{:S(2)}, u32[]{:S(2)}) async-start(bf16[16,2,16,256]{3,2,1,0:T(8,128)(2,1)} %broadcast_in_dim.14), calls=%async_computation.3 | async-start | bytes 524288 | tf_op jit(solution)/shard_map/all_to_all | solution.py:298
  174.2 6.9 %all-to-all-done.3 = bf16[16,2,16,256]{3,2,1,0:T(8,128)(2,1)S(1)} async-done(((bf16[16,2,16,256]{3,2,1,0:T(8,128)(2,1)}), bf16[16,2,16,256]{3,2,1,0:T(8,128)(2,1)S(1)}, u32[]{:S(2)}, u32[]{:S(2)}) %all-to-all-start.3) | async-done | bytes 262176 | tf_op jit(solution)/shard_map/all_to_all | solution.py:298
  (91 shorter events, 31.7 us)
Async XLA Ops:
  1.7 6.8 %collective-permute-start.1 = (bf16[64,1024]{1,0:T(8,128)(2,1)S(1)}, bf16[64,1024]{1,0:T(8,128)(2,1)S(1)}, u32[]{:S(2)}, u32[]{:S(2)}) collective-permute-start(bf16[64,1024]{1,0:T(8,128)(2,1)S(1)} %bitcast.53), channel_id=1, source_target_pairs={{0,1},{1,0},{2,3},{3,2},{4,5},{5,4},{6,7},{7,6},{8,9},{9,8},{10,11... | collective-permute-start | bytes 393224 | tf_op jit(solution)/shard_map/ppermute | solution.py:234
  6.0 14.5 %collective-permute-start = (bf16[256,1024]{0,1:T(8,128)(2,1)S(1)}, bf16[256,1024]{0,1:T(8,128)(2,1)S(1)}, u32[]{:S(2)}, u32[]{:S(2)}) collective-permute-start(bf16[256,1024]{0,1:T(8,128)(2,1)S(1)} %pad_maximum_fusion.1), channel_id=1, source_target_pairs={{0,1},{1,0},{2,3},{3,2},{4,5},{5,4},{6,7},{7,6},{8,9},{9,8},{10,11... | collective-permute-start | bytes 1572872 | tf_op jit(solution)/shard_map/ppermute | solution.py:234
  8.6 11.7 %collective-permute-start.2 = (bf16[128,1024]{1,0:T(8,128)(2,1)S(1)}, bf16[128,1024]{1,0:T(8,128)(2,1)S(1)}, u32[]{:S(2)}, u32[]{:S(2)}) collective-permute-start(bf16[128,1024]{1,0:T(8,128)(2,1)S(1)} %maximum_select_fusion.1), channel_id=1, source_target_pairs={{2,0},{271,1},{18,16},{287,17},{34,32},{303,33},{50,48},{319,49},{... | collective-permute-start | bytes 786440 | tf_op jit(solution)/shard_map/ppermute | solution.py:252
  20.5 29.1 %copy-start.4 = (bf16[256,1024]{1,0:T(8,128)(2,1)}, bf16[256,1024]{1,0:T(8,128)(2,1)S(1)}, u32[]{:S(2)}) copy-start(bf16[256,1024]{1,0:T(8,128)(2,1)S(1)} %maximum_select_fusion.refs_8_) | copy-start | bytes 1572868
  20.8 51.0 %copy-start = (bf16[256,1024]{0,1:T(8,128)(2,1)}, bf16[256,1024]{0,1:T(8,128)(2,1)S(1)}, u32[]{:S(2)}) copy-start(bf16[256,1024]{0,1:T(8,128)(2,1)S(1)} %fusion.4) | copy-start | bytes 1572868
  21.2 18.3 %collective-permute-start.3 = (bf16[256,1024]{1,0:T(8,128)(2,1)S(1)}, bf16[256,1024]{1,0:T(8,128)(2,1)S(1)}, u32[]{:S(2)}, u32[]{:S(2)}) collective-permute-start(bf16[256,1024]{1,0:T(8,128)(2,1)S(1)} %maximum_select_fusion.refs_8_), channel_id=1, source_target_pairs={{270,0},{3,1},{286,16},{19,17},{302,32},{35,33},{318,48},{51,49},{... | collective-permute-start | bytes 1572872 | tf_op jit(solution)/shard_map/ppermute | solution.py:265
  23.2 16.3 %collective-permute-start.4 = (bf16[32,512]{0,1:T(8,128)(2,1)S(1)}, bf16[32,512]{0,1:T(8,128)(2,1)S(1)}, u32[]{:S(2)}, u32[]{:S(2)}) collective-permute-start(bf16[32,512]{0,1:T(8,128)(2,1)S(1)} %slice.48), channel_id=1, source_target_pairs={{0,8},{1,9},{2,10},{3,11},{4,12},{5,13},{6,14},{7,15},{8,0},{9,1},... | collective-permute-start | bytes 98312 | tf_op jit(solution)/shard_map/ppermute | solution.py:266
  39.5 33.5 %copy-start.11 = (bf16[256,1024]{1,0:T(8,128)(2,1)}, bf16[256,1024]{1,0:T(8,128)(2,1)S(1)}, u32[]{:S(2)}) copy-start(bf16[256,1024]{1,0:T(8,128)(2,1)S(1)} %collective-permute-done.3.refs_9_) | copy-start | bytes 1572868
  39.5 17.5 %collective-permute-start.5 = (bf16[256,1024]{1,0:T(8,128)(2,1)S(1)}, bf16[256,1024]{1,0:T(8,128)(2,1)}, u32[]{:S(2)}, u32[]{:S(2)}) collective-permute-start(bf16[256,1024]{1,0:T(8,128)(2,1)S(1)} %collective-permute-done.3.refs_9_), channel_id=1, source_target_pairs={{2,0},{271,1},{18,16},{287,17},{34,32},{303,33},{50,48},{319,49},{... | collective-permute-start | bytes 1572872 | tf_op jit(solution)/shard_map/ppermute | solution.py:268
  47.7 8.2 %collective-permute-start.6 = (bf16[96,512]{0,1:T(8,128)(2,1)S(1)}, bf16[96,512]{0,1:T(8,128)(2,1)S(1)}, u32[]{:S(2)}, u32[]{:S(2)}) collective-permute-start(bf16[96,512]{0,1:T(8,128)(2,1)S(1)} %pad_maximum_fusion.5), channel_id=1, source_target_pairs={{0,4},{1,5},{2,6},{3,7},{4,0},{5,1},{6,2},{7,3},{8,12},{9,13},{10,... | collective-permute-start | bytes 294920 | tf_op jit(solution)/shard_map/ppermute | solution.py:269
  57.3 11.7 %collective-permute-start.7 = (bf16[256,512]{0,1:T(8,128)(2,1)S(1)}, bf16[256,512]{0,1:T(8,128)(2,1)S(1)}, u32[]{:S(2)}, u32[]{:S(2)}) collective-permute-start(bf16[256,512]{0,1:T(8,128)(2,1)S(1)} %pad_maximum_fusion.4), channel_id=1, source_target_pairs={{0,2},{1,3},{2,0},{3,1},{4,6},{5,7},{6,4},{7,5},{8,10},{9,11},{10,... | collective-permute-start | bytes 786440 | tf_op jit(solution)/shard_map/ppermute | solution.py:273
  61.8 15.1 %collective-permute-start.9 = (bf16[256,1024]{1,0:T(8,128)(2,1)}, bf16[256,1024]{1,0:T(8,128)(2,1)}, u32[]{:S(2)}, u32[]{:S(2)}) collective-permute-start(bf16[256,1024]{1,0:T(8,128)(2,1)} %collective-permute-done.5.refs_10_), channel_id=1, source_target_pairs={{270,0},{3,1},{286,16},{19,17},{302,32},{35,33},{318,48},{51,49},{... | collective-permute-start | bytes 1572872 | tf_op jit(solution)/shard_map/ppermute | solution.py:271
  69.2 6.7 %collective-permute-start.8 = (bf16[384,512]{0,1:T(8,128)(2,1)S(1)}, bf16[384,512]{0,1:T(8,128)(2,1)S(1)}, u32[]{:S(2)}, u32[]{:S(2)}) collective-permute-start(bf16[384,512]{0,1:T(8,128)(2,1)S(1)} %pad_maximum_fusion.3), channel_id=1, source_target_pairs={{0,1},{1,0},{2,3},{3,2},{4,5},{5,4},{6,7},{7,6},{8,9},{9,8},{10,11... | collective-permute-start | bytes 1179656 | tf_op jit(solution)/shard_map/ppermute | solution.py:234
  89.9 32.4 %copy-start.10 = (bf16[256,64]{1,0:T(8,128)(2,1)S(1)}, bf16[256,64]{1,0:T(8,128)(2,1)}, u32[]{:S(2)}) copy-start(bf16[256,64]{1,0:T(8,128)(2,1)} %constant.32) | copy-start | bytes 98308
  89.9 37.7 %all-to-all-start = ((bf16[16,16,16,256]{3,2,1,0:T(8,128)(2,1)}), bf16[16,16,16,256]{3,2,1,0:T(8,128)(2,1)S(1)}, u32[]{:S(2)}, u32[]{:S(2)}) async-start(bf16[16,16,16,256]{3,2,1,0:T(8,128)(2,1)} %get-tuple-element.30), calls=%async_computation | async-start | bytes 4194304 | tf_op jit(solution)/shard_map/all_to_all | solution.py:284
  97.0 10.6 %collective-permute-start.11 = (bf16[256,512]{1,0:T(8,128)(2,1)S(1)}, bf16[256,512]{1,0:T(8,128)(2,1)S(1)}, u32[]{:S(2)}, u32[]{:S(2)}) collective-permute-start(bf16[256,512]{1,0:T(8,128)(2,1)S(1)} %copy-done.12), channel_id=1, source_target_pairs={{0,2},{1,3},{2,0},{3,1},{4,6},{5,7},{6,4},{7,5},{8,10},{9,11},{10,... | collective-permute-start | bytes 786440 | tf_op jit(solution)/shard_map/ppermute | solution.py:306
  107.6 26.5 %copy-start.8 = (bf16[256,128]{1,0:T(8,128)(2,1)S(1)}, bf16[256,128]{1,0:T(8,128)(2,1)}, u32[]{:S(2)}) copy-start(bf16[256,128]{1,0:T(8,128)(2,1)} %constant.31) | copy-start | bytes 196612
  107.7 7.4 %collective-permute-start.12 = (bf16[96,512]{1,0:T(8,128)(2,1)S(1)}, bf16[96,512]{1,0:T(8,128)(2,1)S(1)}, u32[]{:S(2)}, u32[]{:S(2)}) collective-permute-start(bf16[96,512]{1,0:T(8,128)(2,1)S(1)} %pad_maximum_fusion.7), channel_id=1, source_target_pairs={{0,4},{1,5},{2,6},{3,7},{4,0},{5,1},{6,2},{7,3},{8,12},{9,13},{10,... | collective-permute-start | bytes 294920 | tf_op jit(solution)/shard_map/ppermute | solution.py:308
  110.4 62.2 %collective-permute-start.10 = (bf16[128,1024]{1,0:T(8,128)(2,1)}, bf16[128,1024]{1,0:T(8,128)(2,1)S(1)}, u32[]{:S(2)}, u32[]{:S(2)}) collective-permute-start(bf16[128,1024]{1,0:T(8,128)(2,1)} %get-tuple-element.24), channel_id=1, source_target_pairs={{0,1},{1,0},{2,3},{3,2},{4,5},{5,4},{6,7},{7,6},{8,9},{9,8},{10,11... | collective-permute-start | bytes 786440 | tf_op jit(solution)/shard_map/ppermute | solution.py:234
  115.1 18.9 %collective-permute-start.13 = (bf16[32,512]{1,0:T(8,128)(2,1)S(1)}, bf16[32,512]{1,0:T(8,128)(2,1)S(1)}, u32[]{:S(2)}, u32[]{:S(2)}) collective-permute-start(bf16[32,512]{1,0:T(8,128)(2,1)S(1)} %fusion.13), channel_id=1, source_target_pairs={{0,8},{1,9},{2,10},{3,11},{4,12},{5,13},{6,14},{7,15},{8,0},{9,1},... | collective-permute-start | bytes 98312 | tf_op jit(solution)/shard_map/ppermute | solution.py:309
  128.5 8.4 %all-to-all-start.1 = ((bf16[4,4,16,256]{3,2,1,0:T(8,128)(2,1)}), bf16[4,4,16,256]{3,2,1,0:T(8,128)(2,1)S(1)}, u32[]{:S(2)}, u32[]{:S(2)}) async-start(bf16[4,4,16,256]{3,2,1,0:T(8,128)(2,1)} %bitcast.12), calls=%async_computation.1 | async-start | bytes 262144 | tf_op jit(solution)/shard_map/all_to_all | solution.py:290
  137.7 28.9 %all-to-all-start.2 = ((bf16[8,2,16,256]{3,2,1,0:T(8,128)(2,1)}), bf16[8,2,16,256]{3,2,1,0:T(8,128)(2,1)S(1)}, u32[]{:S(2)}, u32[]{:S(2)}) async-start(bf16[8,2,16,256]{3,2,1,0:T(8,128)(2,1)} %copy.69), calls=%async_computation.2 | async-start | bytes 262144 | tf_op jit(solution)/shard_map/all_to_all | solution.py:293
  152.7 20.7 %collective-permute-start.14 = (bf16[128,1024]{1,0:T(8,128)(2,1)S(1)}, bf16[128,1024]{1,0:T(8,128)(2,1)S(1)}, u32[]{:S(2)}, u32[]{:S(2)}) collective-permute-start(bf16[128,1024]{1,0:T(8,128)(2,1)S(1)} %dynamic-slice_convert_fusion), channel_id=1, source_target_pairs={{0,1},{1,0},{2,3},{3,2},{4,5},{5,4},{6,7},{7,6},{8,9},{9,8},{10,11... | collective-permute-start | bytes 786440 | tf_op jit(solution)/shard_map/ppermute | solution.py:234
  167.3 13.8 %all-to-all-start.3 = ((bf16[16,2,16,256]{3,2,1,0:T(8,128)(2,1)}), bf16[16,2,16,256]{3,2,1,0:T(8,128)(2,1)S(1)}, u32[]{:S(2)}, u32[]{:S(2)}) async-start(bf16[16,2,16,256]{3,2,1,0:T(8,128)(2,1)} %broadcast_in_dim.14), calls=%async_computation.3 | async-start | bytes 524288 | tf_op jit(solution)/shard_map/all_to_all | solution.py:298
  (9 other events, 131.2 us)

commit v5 on v4

--- a/solution.py
+++ b/solution.py
@@ -249,9 +249,6 @@
         keep, give = shard_half(core), shard_half(1 - core)
         shard_got = swap_core(give)
         w0 = ordered(keep, shard_got, 0)
-        w1 = lax.ppermute(w0, both, swap_even)
-        even = (zl + core) & 1 == 0
-        n1 = jnp.where(even, jnp.concatenate([w0, w1], 0), jnp.concatenate([w1, w0], 0))
 
         own = jnp.concatenate([tokens[0], grad_out[0]], axis=0)
         got = swap_core(own)
@@ -260,18 +257,21 @@
         matrix = jnp.asarray(coarse_matrix, BF)
         half_tokens = lax.dynamic_slice(chip_tokens, (0, core * 512), (256, 512))
         coarse = nn(matrix, half_tokens).astype(BF)
-        n1, coarse = lax.optimization_barrier((n1, coarse))
         c1, c2, c3 = coarse[0:128], coarse[128:192], coarse[192:224]
+
+        even = (zl + core) & 1 == 0
+        t3 = lax.ppermute(c3, "seq", chip_swap(2))
+        second = lax.ppermute(jnp.concatenate([c2, t3], 0), "seq", chip_swap(1))
+        held = jnp.concatenate([second[0:64], t3, second[64:96]], 0)
+        w0, held, to_third = lax.optimization_barrier((w0, held, jnp.concatenate([c1, held], 0)))
+        third = lax.ppermute(to_third, "seq", chip_swap(0))
+        w1 = lax.ppermute(w0, both, swap_even)
+        half_set = jnp.concatenate([held, third], 0)
+        w1, half_set = lax.optimization_barrier((w1, half_set))
+        n1 = jnp.where(even, jnp.concatenate([w0, w1], 0), jnp.concatenate([w1, w0], 0))
         n2 = lax.ppermute(n1, both, swap_odd)
-        t3 = lax.ppermute(c3, "seq", chip_swap(2))
-        n2, t3 = lax.optimization_barrier((n2, t3))
         n3 = lax.ppermute(n2, both, swap_even)
-        second = lax.ppermute(jnp.concatenate([c2, t3], 0), "seq", chip_swap(1))
-        n3, second = lax.optimization_barrier((n3, second))
         n4 = lax.ppermute(n3, both, swap_odd)
-        held = jnp.concatenate([second[0:64], t3, second[64:96]], 0)
-        third = lax.ppermute(jnp.concatenate([c1, held], 0), "seq", chip_swap(0))
-        half_set = jnp.concatenate([held, third], 0)
         other_set = swap_core(half_set)
 
         position = jnp.stack([zl, core]).astype(jnp.int32)

time: 184 us -> 187 us (1.016)
  the two profiles are of different devices: /device:TPU:32 before, /device:TPU:1 now
where the time goes in v5:
time: 187 us; the launch traced here: 183 us
  starting transfers between devices  81.2 us (43%)
  waiting for transfers between devices  70.4 us (38%)
  Pallas kernels  13 us (7%)
  local copies, waits for them, and re-layouts  9.92 us (5%)
  other arithmetic  4.45 us (2%)
  matrix products  2.92 us (2%)
    ppermute x5, starting transfers between devices, swap_core(): return lax.ppermute(value, 'seq', core_pairs)  28.4 us
    pallas_call x1, Pallas kernels, run_layer(): pl.pallas_call(functools.partial(layer_kernel, nx, ny), out_shape=tuple((...  13 us
    ppermute x1, waiting for transfers between devices, per_device(): t3 = lax.ppermute(c3, 'seq', chip_swap(2))  11 us
    ppermute x1, waiting for transfers between devices, per_device(): n2 = lax.ppermute(n1, both, swap_odd)  8.29 us
    all_to_all x1, waiting for transfers between devices, per_device(): lax.all_to_all(jnp.concatenate([by_quad] * nzh, axis=0), both, 0, 0, axis...  7.67 us
    ppermute x1, waiting for transfers between devices, per_device(): second = lax.ppermute(jnp.concatenate([c2, t3], 0), 'seq', chip_swap(1))  7.54 us
    all_to_all x1, starting transfers between devices, per_device(): lax.all_to_all(by_chip, 'seq', 0, 0, axis_index_groups=quad_groups, tiled...  7.34 us
    all_to_all x1, starting transfers between devices, per_device(): lax.all_to_all(part, 'dp', 0, 0, axis_index_groups=plane_groups, tiled=True)  6.9 us
  transfers between devices with their start and end apart: 19, of which 13 were waited for; matrix products, arithmetic and copies ran while one was open for 6% of the time, Pallas kernels for 0%

profile of v5, /device:TPU:1, one launch (start us, length us, event | category | flops | bytes accessed | tf_op | source)
XLA Modules:
  0.0 183.1 jit_solution(17581200573518335581)
XLA Ops:
  3.0 8.8 %collective-permute-start = (bf16[256,1024]{0,1:T(8,128)(2,1)S(1)}, bf16[256,1024]{0,1:T(8,128)(2,1)S(1)}, u32[]{:S(2)}, u32[]{:S(2)}) collective-permute-start(bf16[256,1024]{0,1:T(8,128)(2,1)S(1)} %pad_maximum_fusion.1), channel_id=1, source_target_pairs={{0,1},{1,0},{2,3},{3,2},{4,5},{5,4},{6,7},{7,6},{8,9},{9,8},{10,11... | collective-permute-start | bytes 1572872 | tf_op jit(solution)/shard_map/ppermute | solution.py:234
  14.1 3.4 %collective-permute-start.2 = (bf16[32,512]{0,1:T(8,128)(2,1)S(1)}, bf16[32,512]{0,1:T(8,128)(2,1)S(1)}, u32[]{:S(2)}, u32[]{:S(2)}) collective-permute-start(bf16[32,512]{0,1:T(8,128)(2,1)S(1)} %slice.67), channel_id=1, source_target_pairs={{0,8},{1,9},{2,10},{3,11},{4,12},{5,13},{6,14},{7,15},{8,0},{9,1},... | collective-permute-start | bytes 98312 | tf_op jit(solution)/shard_map/ppermute | solution.py:263
  17.7 2.6 %collective-permute-start.1 = (bf16[64,1024]{1,0:T(8,128)(2,1)S(1)}, bf16[64,1024]{1,0:T(8,128)(2,1)S(1)}, u32[]{:S(2)}, u32[]{:S(2)}) collective-permute-start(bf16[64,1024]{1,0:T(8,128)(2,1)S(1)} %bitcast.52), channel_id=1, source_target_pairs={{0,1},{1,0},{2,3},{3,2},{4,5},{5,4},{6,7},{7,6},{8,9},{9,8},{10,11... | collective-permute-start | bytes 393224 | tf_op jit(solution)/shard_map/ppermute | solution.py:234
  20.3 11.0 %collective-permute-done.2 = bf16[32,512]{0,1:T(8,128)(2,1)S(1)} collective-permute-done((bf16[32,512]{0,1:T(8,128)(2,1)S(1)}, bf16[32,512]{0,1:T(8,128)(2,1)S(1)}, u32[]{:S(2)}, u32[]{:S(2)}) %collective-permute-start.2) | collective-permute-done | bytes 32800 | tf_op jit(solution)/shard_map/ppermute | solution.py:263
  33.4 7.5 %collective-permute-done.3 = bf16[96,512]{0,1:T(8,128)(2,1)S(1)} collective-permute-done((bf16[96,512]{0,1:T(8,128)(2,1)S(1)}, bf16[96,512]{0,1:T(8,128)(2,1)S(1)}, u32[]{:S(2)}, u32[]{:S(2)}) %collective-permute-start.3) | collective-permute-done | bytes 98336 | tf_op jit(solution)/shard_map/ppermute | solution.py:264
  43.3 6.1 %collective-permute-start.4 = (bf16[128,1024]{1,0:T(8,128)(2,1)S(1)}, bf16[128,1024]{1,0:T(8,128)(2,1)S(1)}, u32[]{:S(2)}, u32[]{:S(2)}) collective-permute-start(bf16[128,1024]{1,0:T(8,128)(2,1)S(1)} %maximum_select_fusion.1), channel_id=1, source_target_pairs={{2,0},{271,1},{18,16},{287,17},{34,32},{303,33},{50,48},{319,49},{... | collective-permute-start | bytes 786440 | tf_op jit(solution)/shard_map/ppermute | solution.py:268
  50.7 2.5 %collective-permute-done.4 = bf16[128,1024]{1,0:T(8,128)(2,1)S(1)} collective-permute-done((bf16[128,1024]{1,0:T(8,128)(2,1)S(1)}, bf16[128,1024]{1,0:T(8,128)(2,1)S(1)}, u32[]{:S(2)}, u32[]{:S(2)}) %collective-permute-start.4) | collective-permute-done | bytes 262176 | tf_op jit(solution)/shard_map/ppermute | solution.py:268
  55.2 8.3 %collective-permute-done.7.refs_9_ = bf16[256,1024]{1,0:T(8,128)(2,1)S(1)} collective-permute-done((bf16[256,1024]{1,0:T(8,128)(2,1)S(1)}, bf16[256,1024]{1,0:T(8,128)(2,1)S(1)}, u32[]{:S(2)}, u32[]{:S(2)}) %collective-permute-start.7) | collective-permute-done | bytes 524320 | tf_op jit(solution)/shard_map/ppermute | solution.py:272
  63.5 4.6 %collective-permute-start.8 = (bf16[256,1024]{1,0:T(8,128)(2,1)S(1)}, bf16[256,1024]{1,0:T(8,128)(2,1)}, u32[]{:S(2)}, u32[]{:S(2)}) collective-permute-start(bf16[256,1024]{1,0:T(8,128)(2,1)S(1)} %collective-permute-done.7.refs_9_), channel_id=1, source_target_pairs={{2,0},{271,1},{18,16},{287,17},{34,32},{303,33},{50,48},{319,49},{... | collective-permute-start | bytes 1572872 | tf_op jit(solution)/shard_map/ppermute | solution.py:273
  68.1 6.7 %collective-permute-done.8.refs_10_ = bf16[256,1024]{1,0:T(8,128)(2,1)} collective-permute-done((bf16[256,1024]{1,0:T(8,128)(2,1)S(1)}, bf16[256,1024]{1,0:T(8,128)(2,1)}, u32[]{:S(2)}, u32[]{:S(2)}) %collective-permute-start.8) | collective-permute-done | bytes 524320 | tf_op jit(solution)/shard_map/ppermute | solution.py:273
  76.7 10.0 %collective-permute-start.6 = (bf16[384,512]{0,1:T(8,128)(2,1)S(1)}, bf16[384,512]{0,1:T(8,128)(2,1)S(1)}, u32[]{:S(2)}, u32[]{:S(2)}) collective-permute-start(bf16[384,512]{0,1:T(8,128)(2,1)S(1)} %pad_maximum_fusion.3), channel_id=1, source_target_pairs={{0,1},{1,0},{2,3},{3,2},{4,5},{5,4},{6,7},{7,6},{8,9},{9,8},{10,11... | collective-permute-start | bytes 1179656 | tf_op jit(solution)/shard_map/ppermute | solution.py:234
  91.5 13.0 %shard_map.76 = (bf16[1024,1024]{1,0:T(8,128)(2,1)}, bf16[16,16,16,256]{3,2,1,0:T(8,128)(2,1)}, f32[128,1024]{1,0:T(8,128)}, bf16[128,1024]{1,0:T(8,128)(2,1)}, ...) custom-call(s32[2]{0:T(128)} %pad_add_fusion.pos_ref, ...), custom_call_target="tpu_custom_call" | custom-call | flops 3500000000 | bytes 14000000 | tf_op jit(solution)/shard_map/pallas_call | solution.py:172
  104.5 6.9 %all-to-all-start = ((bf16[16,16,16,256]{3,2,1,0:T(8,128)(2,1)}), bf16[16,16,16,256]{3,2,1,0:T(8,128)(2,1)S(1)}, u32[]{:S(2)}, u32[]{:S(2)}) async-start(bf16[16,16,16,256]{3,2,1,0:T(8,128)(2,1)} %get-tuple-element.28), calls=%async_computation | async-start | bytes 4194304 | tf_op jit(solution)/shard_map/all_to_all | solution.py:284
  113.4 6.7 %collective-permute-done.11 = bf16[256,512]{1,0:T(8,128)(2,1)S(1)} collective-permute-done((bf16[256,512]{1,0:T(8,128)(2,1)S(1)}, bf16[256,512]{1,0:T(8,128)(2,1)S(1)}, u32[]{:S(2)}, u32[]{:S(2)}) %collective-permute-start.11) | collective-permute-done | bytes 262176 | tf_op jit(solution)/shard_map/ppermute | solution.py:306
  122.1 3.8 %collective-permute-start.10 = (bf16[128,1024]{1,0:T(8,128)(2,1)}, bf16[128,1024]{1,0:T(8,128)(2,1)S(1)}, u32[]{:S(2)}, u32[]{:S(2)}) collective-permute-start(bf16[128,1024]{1,0:T(8,128)(2,1)} %get-tuple-element.22), channel_id=1, source_target_pairs={{0,1},{1,0},{2,3},{3,2},{4,5},{5,4},{6,7},{7,6},{8,9},{9,8},{10,11... | collective-permute-start | bytes 786440 | tf_op jit(solution)/shard_map/ppermute | solution.py:234
  127.8 4.1 %collective-permute-start.13 = (bf16[32,512]{1,0:T(8,128)(2,1)S(1)}, bf16[32,512]{1,0:T(8,128)(2,1)S(1)}, u32[]{:S(2)}, u32[]{:S(2)}) collective-permute-start(bf16[32,512]{1,0:T(8,128)(2,1)S(1)} %fusion.13), channel_id=1, source_target_pairs={{0,8},{1,9},{2,10},{3,11},{4,12},{5,13},{6,14},{7,15},{8,0},{9,1},... | collective-permute-start | bytes 98312 | tf_op jit(solution)/shard_map/ppermute | solution.py:309
  132.1 6.6 %all-to-all-done = bf16[16,16,16,256]{3,2,1,0:T(8,128)(2,1)S(1)} async-done(((bf16[16,16,16,256]{3,2,1,0:T(8,128)(2,1)}), bf16[16,16,16,256]{3,2,1,0:T(8,128)(2,1)S(1)}, u32[]{:S(2)}, u32[]{:S(2)}) %all-to-all-start) | async-done | bytes 2097184 | tf_op jit(solution)/shard_map/all_to_all | solution.py:284
  139.7 7.3 %all-to-all-start.1 = ((bf16[4,4,16,256]{3,2,1,0:T(8,128)(2,1)}), bf16[4,4,16,256]{3,2,1,0:T(8,128)(2,1)S(1)}, u32[]{:S(2)}, u32[]{:S(2)}) async-start(bf16[4,4,16,256]{3,2,1,0:T(8,128)(2,1)} %bitcast.12), calls=%async_computation.1 | async-start | bytes 262144 | tf_op jit(solution)/shard_map/all_to_all | solution.py:290
  147.5 3.2 %all-to-all-done.1 = bf16[4,4,16,256]{3,2,1,0:T(8,128)(2,1)S(1)} async-done(((bf16[4,4,16,256]{3,2,1,0:T(8,128)(2,1)}), bf16[4,4,16,256]{3,2,1,0:T(8,128)(2,1)S(1)}, u32[]{:S(2)}, u32[]{:S(2)}) %all-to-all-start.1) | async-done | bytes 131104 | tf_op jit(solution)/shard_map/all_to_all | solution.py:290
  151.4 5.2 %all-to-all-start.2 = ((bf16[8,2,16,256]{3,2,1,0:T(8,128)(2,1)}), bf16[8,2,16,256]{3,2,1,0:T(8,128)(2,1)S(1)}, u32[]{:S(2)}, u32[]{:S(2)}) async-start(bf16[8,2,16,256]{3,2,1,0:T(8,128)(2,1)} %copy.69), calls=%async_computation.2 | async-start | bytes 262144 | tf_op jit(solution)/shard_map/all_to_all | solution.py:293
  158.8 3.2 %collective-permute-start.14 = (bf16[128,1024]{1,0:T(8,128)(2,1)S(1)}, bf16[128,1024]{1,0:T(8,128)(2,1)S(1)}, u32[]{:S(2)}, u32[]{:S(2)}) collective-permute-start(bf16[128,1024]{1,0:T(8,128)(2,1)S(1)} %dynamic-slice_convert_fusion), channel_id=1, source_target_pairs={{0,1},{1,0},{2,3},{3,2},{4,5},{5,4},{6,7},{7,6},{8,9},{9,8},{10,11... | collective-permute-start | bytes 786440 | tf_op jit(solution)/shard_map/ppermute | solution.py:234
  162.1 7.7 %all-to-all-done.2 = bf16[8,2,16,256]{3,2,1,0:T(8,128)(2,1)S(1)} async-done(((bf16[8,2,16,256]{3,2,1,0:T(8,128)(2,1)}), bf16[8,2,16,256]{3,2,1,0:T(8,128)(2,1)S(1)}, u32[]{:S(2)}, u32[]{:S(2)}) %all-to-all-start.2) | async-done | bytes 131104 | tf_op jit(solution)/shard_map/all_to_all | solution.py:293
  170.5 3.5 %all-to-all-start.3 = ((bf16[16,2,16,256]{3,2,1,0:T(8,128)(2,1)}), bf16[16,2,16,256]{3,2,1,0:T(8,128)(2,1)S(1)}, u32[]{:S(2)}, u32[]{:S(2)}) async-start(bf16[16,2,16,256]{3,2,1,0:T(8,128)(2,1)} %broadcast_in_dim.14), calls=%async_computation.3 | async-start | bytes 524288 | tf_op jit(solution)/shard_map/all_to_all | solution.py:298
  175.6 5.7 %all-to-all-done.3 = bf16[16,2,16,256]{3,2,1,0:T(8,128)(2,1)S(1)} async-done(((bf16[16,2,16,256]{3,2,1,0:T(8,128)(2,1)}), bf16[16,2,16,256]{3,2,1,0:T(8,128)(2,1)S(1)}, u32[]{:S(2)}, u32[]{:S(2)}) %all-to-all-start.3) | async-done | bytes 262176 | tf_op jit(solution)/shard_map/all_to_all | solution.py:298
  (95 shorter events, 33.3 us)
Async XLA Ops:
  3.0 10.3 %collective-permute-start = (bf16[256,1024]{0,1:T(8,128)(2,1)S(1)}, bf16[256,1024]{0,1:T(8,128)(2,1)S(1)}, u32[]{:S(2)}, u32[]{:S(2)}) collective-permute-start(bf16[256,1024]{0,1:T(8,128)(2,1)S(1)} %pad_maximum_fusion.1), channel_id=1, source_target_pairs={{0,1},{1,0},{2,3},{3,2},{4,5},{5,4},{6,7},{7,6},{8,9},{9,8},{10,11... | collective-permute-start | bytes 1572872 | tf_op jit(solution)/shard_map/ppermute | solution.py:234
  13.6 73.8 %copy-start = (bf16[256,1024]{0,1:T(8,128)(2,1)}, bf16[256,1024]{0,1:T(8,128)(2,1)S(1)}, u32[]{:S(2)}) copy-start(bf16[256,1024]{0,1:T(8,128)(2,1)S(1)} %fusion.4) | copy-start | bytes 1572868
  14.1 17.2 %collective-permute-start.2 = (bf16[32,512]{0,1:T(8,128)(2,1)S(1)}, bf16[32,512]{0,1:T(8,128)(2,1)S(1)}, u32[]{:S(2)}, u32[]{:S(2)}) collective-permute-start(bf16[32,512]{0,1:T(8,128)(2,1)S(1)} %slice.67), channel_id=1, source_target_pairs={{0,8},{1,9},{2,10},{3,11},{4,12},{5,13},{6,14},{7,15},{8,0},{9,1},... | collective-permute-start | bytes 98312 | tf_op jit(solution)/shard_map/ppermute | solution.py:263
  17.7 15.6 %collective-permute-start.1 = (bf16[64,1024]{1,0:T(8,128)(2,1)S(1)}, bf16[64,1024]{1,0:T(8,128)(2,1)S(1)}, u32[]{:S(2)}, u32[]{:S(2)}) collective-permute-start(bf16[64,1024]{1,0:T(8,128)(2,1)S(1)} %bitcast.52), channel_id=1, source_target_pairs={{0,1},{1,0},{2,3},{3,2},{4,5},{5,4},{6,7},{7,6},{8,9},{9,8},{10,11... | collective-permute-start | bytes 393224 | tf_op jit(solution)/shard_map/ppermute | solution.py:234
  31.4 9.6 %collective-permute-start.3 = (bf16[96,512]{0,1:T(8,128)(2,1)S(1)}, bf16[96,512]{0,1:T(8,128)(2,1)S(1)}, u32[]{:S(2)}, u32[]{:S(2)}) collective-permute-start(bf16[96,512]{0,1:T(8,128)(2,1)S(1)} %pad_maximum_fusion.5), channel_id=1, source_target_pairs={{0,4},{1,5},{2,6},{3,7},{4,0},{5,1},{6,2},{7,3},{8,12},{9,13},{10,... | collective-permute-start | bytes 294920 | tf_op jit(solution)/shard_map/ppermute | solution.py:264
  41.4 9.3 %collective-permute-start.5 = (bf16[256,512]{0,1:T(8,128)(2,1)S(1)}, bf16[256,512]{0,1:T(8,128)(2,1)S(1)}, u32[]{:S(2)}, u32[]{:S(2)}) collective-permute-start(bf16[256,512]{0,1:T(8,128)(2,1)S(1)} %pad_maximum_fusion.4), channel_id=1, source_target_pairs={{0,2},{1,3},{2,0},{3,1},{4,6},{5,7},{6,4},{7,5},{8,10},{9,11},{10,... | collective-permute-start | bytes 786440 | tf_op jit(solution)/shard_map/ppermute | solution.py:267
  43.3 9.9 %collective-permute-start.4 = (bf16[128,1024]{1,0:T(8,128)(2,1)S(1)}, bf16[128,1024]{1,0:T(8,128)(2,1)S(1)}, u32[]{:S(2)}, u32[]{:S(2)}) collective-permute-start(bf16[128,1024]{1,0:T(8,128)(2,1)S(1)} %maximum_select_fusion.1), channel_id=1, source_target_pairs={{2,0},{271,1},{18,16},{287,17},{34,32},{303,33},{50,48},{319,49},{... | collective-permute-start | bytes 786440 | tf_op jit(solution)/shard_map/ppermute | solution.py:268
  50.7 38.9 %copy-start.2 = (bf16[384,512]{0,1:T(8,128)(2,1)}, bf16[384,512]{0,1:T(8,128)(2,1)S(1)}, u32[]{:S(2)}) copy-start(bf16[384,512]{0,1:T(8,128)(2,1)S(1)} %pad_maximum_fusion.3) | copy-start | bytes 1179652
  53.3 38.2 %copy-start.5 = (bf16[256,1024]{1,0:T(8,128)(2,1)}, bf16[256,1024]{1,0:T(8,128)(2,1)S(1)}, u32[]{:S(2)}) copy-start(bf16[256,1024]{1,0:T(8,128)(2,1)S(1)} %maximum_select_fusion.refs_8_) | copy-start | bytes 1572868
  53.3 10.2 %collective-permute-start.7 = (bf16[256,1024]{1,0:T(8,128)(2,1)S(1)}, bf16[256,1024]{1,0:T(8,128)(2,1)S(1)}, u32[]{:S(2)}, u32[]{:S(2)}) collective-permute-start(bf16[256,1024]{1,0:T(8,128)(2,1)S(1)} %maximum_select_fusion.refs_8_), channel_id=1, source_target_pairs={{270,0},{3,1},{286,16},{19,17},{302,32},{35,33},{318,48},{51,49},{... | collective-permute-start | bytes 1572872 | tf_op jit(solution)/shard_map/ppermute | solution.py:272
  63.5 27.9 %copy-start.13 = (bf16[256,1024]{1,0:T(8,128)(2,1)}, bf16[256,1024]{1,0:T(8,128)(2,1)S(1)}, u32[]{:S(2)}) copy-start(bf16[256,1024]{1,0:T(8,128)(2,1)S(1)} %collective-permute-done.7.refs_9_) | copy-start | bytes 1572868
  63.5 11.2 %collective-permute-start.8 = (bf16[256,1024]{1,0:T(8,128)(2,1)S(1)}, bf16[256,1024]{1,0:T(8,128)(2,1)}, u32[]{:S(2)}, u32[]{:S(2)}) collective-permute-start(bf16[256,1024]{1,0:T(8,128)(2,1)S(1)} %collective-permute-done.7.refs_9_), channel_id=1, source_target_pairs={{2,0},{271,1},{18,16},{287,17},{34,32},{303,33},{50,48},{319,49},{... | collective-permute-start | bytes 1572872 | tf_op jit(solution)/shard_map/ppermute | solution.py:273
  74.8 16.7 %collective-permute-start.9 = (bf16[256,1024]{1,0:T(8,128)(2,1)}, bf16[256,1024]{1,0:T(8,128)(2,1)}, u32[]{:S(2)}, u32[]{:S(2)}) collective-permute-start(bf16[256,1024]{1,0:T(8,128)(2,1)} %collective-permute-done.8.refs_10_), channel_id=1, source_target_pairs={{270,0},{3,1},{286,16},{19,17},{302,32},{35,33},{318,48},{51,49},{... | collective-permute-start | bytes 1572872 | tf_op jit(solution)/shard_map/ppermute | solution.py:274
  76.7 13.8 %collective-permute-start.6 = (bf16[384,512]{0,1:T(8,128)(2,1)S(1)}, bf16[384,512]{0,1:T(8,128)(2,1)S(1)}, u32[]{:S(2)}, u32[]{:S(2)}) collective-permute-start(bf16[384,512]{0,1:T(8,128)(2,1)S(1)} %pad_maximum_fusion.3), channel_id=1, source_target_pairs={{0,1},{1,0},{2,3},{3,2},{4,5},{5,4},{6,7},{7,6},{8,9},{9,8},{10,11... | collective-permute-start | bytes 1179656 | tf_op jit(solution)/shard_map/ppermute | solution.py:234
  104.5 27.4 %copy-start.12 = (bf16[256,64]{1,0:T(8,128)(2,1)S(1)}, bf16[256,64]{1,0:T(8,128)(2,1)}, u32[]{:S(2)}) copy-start(bf16[256,64]{1,0:T(8,128)(2,1)} %constant.32) | copy-start | bytes 98308
  104.5 34.3 %all-to-all-start = ((bf16[16,16,16,256]{3,2,1,0:T(8,128)(2,1)}), bf16[16,16,16,256]{3,2,1,0:T(8,128)(2,1)S(1)}, u32[]{:S(2)}, u32[]{:S(2)}) async-start(bf16[16,16,16,256]{3,2,1,0:T(8,128)(2,1)} %get-tuple-element.28), calls=%async_computation | async-start | bytes 4194304 | tf_op jit(solution)/shard_map/all_to_all | solution.py:284
  111.4 8.7 %collective-permute-start.11 = (bf16[256,512]{1,0:T(8,128)(2,1)S(1)}, bf16[256,512]{1,0:T(8,128)(2,1)S(1)}, u32[]{:S(2)}, u32[]{:S(2)}) collective-permute-start(bf16[256,512]{1,0:T(8,128)(2,1)S(1)} %copy-done.14), channel_id=1, source_target_pairs={{0,2},{1,3},{2,0},{3,1},{4,6},{5,7},{6,4},{7,5},{8,10},{9,11},{10,... | collective-permute-start | bytes 786440 | tf_op jit(solution)/shard_map/ppermute | solution.py:306
  120.2 7.6 %collective-permute-start.12 = (bf16[96,512]{1,0:T(8,128)(2,1)S(1)}, bf16[96,512]{1,0:T(8,128)(2,1)S(1)}, u32[]{:S(2)}, u32[]{:S(2)}) collective-permute-start(bf16[96,512]{1,0:T(8,128)(2,1)S(1)} %pad_maximum_fusion.8), channel_id=1, source_target_pairs={{0,4},{1,5},{2,6},{3,7},{4,0},{5,1},{6,2},{7,3},{8,12},{9,13},{10,... | collective-permute-start | bytes 294920 | tf_op jit(solution)/shard_map/ppermute | solution.py:308
  122.1 51.9 %collective-permute-start.10 = (bf16[128,1024]{1,0:T(8,128)(2,1)}, bf16[128,1024]{1,0:T(8,128)(2,1)S(1)}, u32[]{:S(2)}, u32[]{:S(2)}) collective-permute-start(bf16[128,1024]{1,0:T(8,128)(2,1)} %get-tuple-element.22), channel_id=1, source_target_pairs={{0,1},{1,0},{2,3},{3,2},{4,5},{5,4},{6,7},{7,6},{8,9},{9,8},{10,11... | collective-permute-start | bytes 786440 | tf_op jit(solution)/shard_map/ppermute | solution.py:234
  127.8 19.2 %collective-permute-start.13 = (bf16[32,512]{1,0:T(8,128)(2,1)S(1)}, bf16[32,512]{1,0:T(8,128)(2,1)S(1)}, u32[]{:S(2)}, u32[]{:S(2)}) collective-permute-start(bf16[32,512]{1,0:T(8,128)(2,1)S(1)} %fusion.13), channel_id=1, source_target_pairs={{0,8},{1,9},{2,10},{3,11},{4,12},{5,13},{6,14},{7,15},{8,0},{9,1},... | collective-permute-start | bytes 98312 | tf_op jit(solution)/shard_map/ppermute | solution.py:309
  139.7 10.9 %all-to-all-start.1 = ((bf16[4,4,16,256]{3,2,1,0:T(8,128)(2,1)}), bf16[4,4,16,256]{3,2,1,0:T(8,128)(2,1)S(1)}, u32[]{:S(2)}, u32[]{:S(2)}) async-start(bf16[4,4,16,256]{3,2,1,0:T(8,128)(2,1)} %bitcast.12), calls=%async_computation.1 | async-start | bytes 262144 | tf_op jit(solution)/shard_map/all_to_all | solution.py:290
  151.4 18.3 %all-to-all-start.2 = ((bf16[8,2,16,256]{3,2,1,0:T(8,128)(2,1)}), bf16[8,2,16,256]{3,2,1,0:T(8,128)(2,1)S(1)}, u32[]{:S(2)}, u32[]{:S(2)}) async-start(bf16[8,2,16,256]{3,2,1,0:T(8,128)(2,1)} %copy.69), calls=%async_computation.2 | async-start | bytes 262144 | tf_op jit(solution)/shard_map/all_to_all | solution.py:293
  158.8 16.0 %collective-permute-start.14 = (bf16[128,1024]{1,0:T(8,128)(2,1)S(1)}, bf16[128,1024]{1,0:T(8,128)(2,1)S(1)}, u32[]{:S(2)}, u32[]{:S(2)}) collective-permute-start(bf16[128,1024]{1,0:T(8,128)(2,1)S(1)} %dynamic-slice_convert_fusion), channel_id=1, source_target_pairs={{0,1},{1,0},{2,3},{3,2},{4,5},{5,4},{6,7},{7,6},{8,9},{9,8},{10,11... | collective-permute-start | bytes 786440 | tf_op jit(solution)/shard_map/ppermute | solution.py:234
  170.5 10.8 %all-to-all-start.3 = ((bf16[16,2,16,256]{3,2,1,0:T(8,128)(2,1)}), bf16[16,2,16,256]{3,2,1,0:T(8,128)(2,1)S(1)}, u32[]{:S(2)}, u32[]{:S(2)}) async-start(bf16[16,2,16,256]{3,2,1,0:T(8,128)(2,1)} %broadcast_in_dim.14), calls=%async_computation.3 | async-start | bytes 524288 | tf_op jit(solution)/shard_map/all_to_all | solution.py:298
  (11 other events, 151.7 us)

commit v6 on v5

--- a/solution.py
+++ b/solution.py
@@ -224,9 +224,8 @@
                 for z in range(ring) for xy in range(nxy) for core in range(2)]
 
     swap_even, swap_odd = swaps(0), swaps(1)
-    quad_groups = [[4 * quad + i for i in range(4)] for quad in range(seq_count // 4)]
-    line_groups = [[(zh * nxy + xy) * seq_count + 4 * quad + i for zh in range(nzh) for quad in range(4)]
-                   for xy in range(nxy) for i in range(4)]
+    line_groups = [[(zh * nxy + xy) * seq_count + 4 * quad + i for zh in range(nzh) for i in range(4) for quad in range(4)]
+                   for xy in range(nxy)]
     plane_groups = [[zh * nxy + xy for xy in range(nxy)] for zh in range(nzh)]
     coarse_matrix = coarsening()
 
@@ -260,17 +259,18 @@
         c1, c2, c3 = coarse[0:128], coarse[128:192], coarse[192:224]
 
         even = (zl + core) & 1 == 0
+        w0, c3 = lax.optimization_barrier((w0, c3))
         t3 = lax.ppermute(c3, "seq", chip_swap(2))
-        second = lax.ppermute(jnp.concatenate([c2, t3], 0), "seq", chip_swap(1))
+        w1 = lax.ppermute(w0, both, swap_even)
+        n1 = jnp.where(even, jnp.concatenate([w0, w1], 0), jnp.concatenate([w1, w0], 0))
+        n1, to_second, t3 = lax.optimization_barrier((n1, jnp.concatenate([c2, t3], 0), t3))
+        second = lax.ppermute(to_second, "seq", chip_swap(1))
+        n2 = lax.ppermute(n1, both, swap_odd)
         held = jnp.concatenate([second[0:64], t3, second[64:96]], 0)
-        w0, held, to_third = lax.optimization_barrier((w0, held, jnp.concatenate([c1, held], 0)))
+        n2, to_third, held = lax.optimization_barrier((n2, jnp.concatenate([c1, held], 0), held))
         third = lax.ppermute(to_third, "seq", chip_swap(0))
-        w1 = lax.ppermute(w0, both, swap_even)
-        half_set = jnp.concatenate([held, third], 0)
-        w1, half_set = lax.optimization_barrier((w1, half_set))
-        n1 = jnp.where(even, jnp.concatenate([w0, w1], 0), jnp.concatenate([w1, w0], 0))
-        n2 = lax.ppermute(n1, both, swap_odd)
         n3 = lax.ppermute(n2, both, swap_even)
+        n3, half_set = lax.optimization_barrier((n3, jnp.concatenate([held, third], 0)))
         n4 = lax.ppermute(n3, both, swap_odd)
         other_set = swap_core(half_set)
 
@@ -286,13 +286,9 @@
             pieces = part
         plane_sum = jnp.sum(pieces.astype(F32), axis=0).astype(BF)
         rows, cols = 64 // nx, 1024 // ny
-        by_chip = plane_sum.reshape(4, 4, rows, cols)
-        by_chip = lax.all_to_all(by_chip, "seq", 0, 0, axis_index_groups=quad_groups, tiled=True)
-        quad_sum = jnp.sum(by_chip.astype(F32).reshape(2, 2, 4, rows, cols), axis=0).astype(BF)
-        by_quad = quad_sum.transpose(1, 0, 2, 3)
-        by_quad = lax.all_to_all(jnp.concatenate([by_quad] * nzh, axis=0), both, 0, 0,
-                                 axis_index_groups=line_groups, tiled=True)
-        line_sum = jnp.sum(by_quad.astype(F32), axis=0).astype(BF)
+        copies = jnp.broadcast_to(plane_sum[None], (nzh, 16, rows, cols)).reshape(nzh * 16, rows, cols)
+        columns = lax.all_to_all(copies, both, 0, 0, axis_index_groups=line_groups, tiled=True)
+        line_sum = jnp.sum(columns.astype(F32).reshape(nzh * 2, 2, 4, rows, cols), axis=(0, 2)).astype(BF)
         spread = jnp.broadcast_to(line_sum[None], (nxy, 2, rows, cols))
         if nxy > 1:
             spread = lax.all_to_all(spread, "dp", 0, 0, axis_index_groups=plane_groups, tiled=True)

time: 187 us -> 178 us (0.952); the launches traced: 183 us -> 177 us
  starting transfers between devices: 81.2 us -> 77.7 us
    ppermute x1, waiting for transfers between devices: 8.29 us -> 0.01 us  [per_device(): n2 = lax.ppermute(n1, both, swap_odd)]
    ppermute x1, waiting for transfers between devices: 1.2 us -> 8.36 us  [per_device(): third = lax.ppermute(to_third, 'seq', chip_swap(0))]
    ppermute x1, waiting for transfers between devices: 6.66 us -> 0.01 us  [per_device(): n3 = lax.ppermute(n2, both, swap_even)]
    all_to_all x2 -> x1, waiting for transfers between devices: 10.8 us -> 17.4 us  [per_device(): lax.all_to_all(copies, both, 0, 0, axis_index_groups=line_groups, tiled=T...]
    ppermute x1, waiting for transfers between devices: 2.47 us -> 0.01 us  [per_device(): w1 = lax.ppermute(w0, both, swap_even)]
    all_to_all x2 -> x1, starting transfers between devices: 12.5 us -> 10.5 us  [per_device(): lax.all_to_all(copies, both, 0, 0, axis_index_groups=line_groups, tiled=T...]
    ppermute x1, waiting for transfers between devices: 11 us -> 13 us  [per_device(): t3 = lax.ppermute(c3, 'seq', chip_swap(2))]
    unnamed x38 -> x40, local copies, waits for them, and re-layouts: 4.09 us -> 5.1 us
  transfers between devices with their start and end apart: 19 -> 18, of which waited for: 13 -> 9; matrix products, arithmetic and copies ran while one was open for 6% -> 6% of each run, Pallas kernels for 0% -> 0%
where the time goes in v6:
time: 178 us; the launch traced here: 177 us
  starting transfers between devices  77.7 us (44%)
  waiting for transfers between devices  68.7 us (39%)
  Pallas kernels  13 us (7%)
  local copies, waits for them, and re-layouts  11 us (6%)
  other arithmetic  3.73 us (2%)
    ppermute x5, starting transfers between devices, swap_core(): return lax.ppermute(value, 'seq', core_pairs)  26.6 us
    all_to_all x1, waiting for transfers between devices, per_device(): lax.all_to_all(copies, both, 0, 0, axis_index_groups=line_groups, tiled=T...  17.4 us
    ppermute x1, waiting for transfers between devices, per_device(): t3 = lax.ppermute(c3, 'seq', chip_swap(2))  13 us
    pallas_call x1, Pallas kernels, run_layer(): pl.pallas_call(functools.partial(layer_kernel, nx, ny), out_shape=tuple((...  13 us
    all_to_all x1, starting transfers between devices, per_device(): lax.all_to_all(copies, both, 0, 0, axis_index_groups=line_groups, tiled=T...  10.5 us
    ppermute x1, waiting for transfers between devices, per_device(): third = lax.ppermute(to_third, 'seq', chip_swap(0))  8.36 us
    ppermute x1, waiting for transfers between devices, per_device(): second = lax.ppermute(to_second, 'seq', chip_swap(1))  7.85 us
    all_to_all x1, starting transfers between devices, per_device(): lax.all_to_all(part, 'dp', 0, 0, axis_index_groups=plane_groups, tiled=True)  6.89 us
  transfers between devices with their start and end apart: 18, of which 9 were waited for; matrix products, arithmetic and copies ran while one was open for 6% of the time, Pallas kernels for 0%

profile of v6, /device:TPU:1, one launch (start us, length us, event | category | flops | bytes accessed | tf_op | source)
XLA Modules:
  0.0 176.9 jit_solution(12659662088907827909)
XLA Ops:
  3.0 8.9 %collective-permute-start = (bf16[256,1024]{0,1:T(8,128)(2,1)S(1)}, bf16[256,1024]{0,1:T(8,128)(2,1)S(1)}, u32[]{:S(2)}, u32[]{:S(2)}) collective-permute-start(bf16[256,1024]{0,1:T(8,128)(2,1)S(1)} %pad_maximum_fusion.1), channel_id=1, source_target_pairs={{0,1},{1,0},{2,3},{3,2},{4,5},{5,4},{6,7},{7,6},{8,9},{9,8},{10,11... | collective-permute-start | bytes 1572872 | tf_op jit(solution)/shard_map/ppermute | solution.py:233
  12.1 1.9 %collective-permute-start.1 = (bf16[64,1024]{1,0:T(8,128)(2,1)S(1)}, bf16[64,1024]{1,0:T(8,128)(2,1)S(1)}, u32[]{:S(2)}, u32[]{:S(2)}) collective-permute-start(bf16[64,1024]{1,0:T(8,128)(2,1)S(1)} %bitcast.50), channel_id=1, source_target_pairs={{0,1},{1,0},{2,3},{3,2},{4,5},{5,4},{6,7},{7,6},{8,9},{9,8},{10,11... | collective-permute-start | bytes 393224 | tf_op jit(solution)/shard_map/ppermute | solution.py:233
  16.2 5.8 %collective-permute-start.2 = (bf16[128,1024]{1,0:T(8,128)(2,1)S(1)}, bf16[128,1024]{1,0:T(8,128)(2,1)S(1)}, u32[]{:S(2)}, u32[]{:S(2)}) collective-permute-start(bf16[128,1024]{1,0:T(8,128)(2,1)S(1)} %maximum_select_fusion.1), channel_id=1, source_target_pairs={{2,0},{271,1},{18,16},{287,17},{34,32},{303,33},{50,48},{319,49},{... | collective-permute-start | bytes 786440 | tf_op jit(solution)/shard_map/ppermute | solution.py:264
  21.9 1.9 %collective-permute-start.3 = (bf16[32,512]{0,1:T(8,128)(2,1)S(1)}, bf16[32,512]{0,1:T(8,128)(2,1)S(1)}, u32[]{:S(2)}, u32[]{:S(2)}) collective-permute-start(bf16[32,512]{0,1:T(8,128)(2,1)S(1)} %slice.66), channel_id=1, source_target_pairs={{0,8},{1,9},{2,10},{3,11},{4,12},{5,13},{6,14},{7,15},{8,0},{9,1},... | collective-permute-start | bytes 98312 | tf_op jit(solution)/shard_map/ppermute | solution.py:263
  23.9 13.0 %collective-permute-done.3 = bf16[32,512]{0,1:T(8,128)(2,1)S(1)} collective-permute-done((bf16[32,512]{0,1:T(8,128)(2,1)S(1)}, bf16[32,512]{0,1:T(8,128)(2,1)S(1)}, u32[]{:S(2)}, u32[]{:S(2)}) %collective-permute-start.3) | collective-permute-done | bytes 32800 | tf_op jit(solution)/shard_map/ppermute | solution.py:263
  37.2 1.9 %collective-permute-start.4 = (bf16[256,1024]{1,0:T(8,128)(2,1)S(1)}, bf16[256,1024]{1,0:T(8,128)(2,1)S(1)}, u32[]{:S(2)}, u32[]{:S(2)}) collective-permute-start(bf16[256,1024]{1,0:T(8,128)(2,1)S(1)} %maximum_select_fusion.refs_8_), channel_id=1, source_target_pairs={{270,0},{3,1},{286,16},{19,17},{302,32},{35,33},{318,48},{51,49},{... | collective-permute-start | bytes 1572872 | tf_op jit(solution)/shard_map/ppermute | solution.py:268
  39.1 2.5 %collective-permute-start.5 = (bf16[96,512]{0,1:T(8,128)(2,1)S(1)}, bf16[96,512]{0,1:T(8,128)(2,1)S(1)}, u32[]{:S(2)}, u32[]{:S(2)}) collective-permute-start(bf16[96,512]{0,1:T(8,128)(2,1)S(1)} %pad_maximum_fusion.5), channel_id=1, source_target_pairs={{0,4},{1,5},{2,6},{3,7},{4,0},{5,1},{6,2},{7,3},{8,12},{9,13},{10,... | collective-permute-start | bytes 294920 | tf_op jit(solution)/shard_map/ppermute | solution.py:267
  41.7 7.8 %collective-permute-done.5 = bf16[96,512]{0,1:T(8,128)(2,1)S(1)} collective-permute-done((bf16[96,512]{0,1:T(8,128)(2,1)S(1)}, bf16[96,512]{0,1:T(8,128)(2,1)S(1)}, u32[]{:S(2)}, u32[]{:S(2)}) %collective-permute-start.5) | collective-permute-done | bytes 98336 | tf_op jit(solution)/shard_map/ppermute | solution.py:267
  49.9 6.1 %collective-permute-start.6 = (bf16[256,1024]{1,0:T(8,128)(2,1)S(1)}, bf16[256,1024]{1,0:T(8,128)(2,1)}, u32[]{:S(2)}, u32[]{:S(2)}) collective-permute-start(bf16[256,1024]{1,0:T(8,128)(2,1)S(1)} %collective-permute-done.4.refs_9_), channel_id=1, source_target_pairs={{2,0},{271,1},{18,16},{287,17},{34,32},{303,33},{50,48},{319,49},{... | collective-permute-start | bytes 1572872 | tf_op jit(solution)/shard_map/ppermute | solution.py:272
  58.0 8.4 %collective-permute-done.7 = bf16[256,512]{0,1:T(8,128)(2,1)S(1)} collective-permute-done((bf16[256,512]{0,1:T(8,128)(2,1)S(1)}, bf16[256,512]{0,1:T(8,128)(2,1)S(1)}, u32[]{:S(2)}, u32[]{:S(2)}) %collective-permute-start.7) | collective-permute-done | bytes 262176 | tf_op jit(solution)/shard_map/ppermute | solution.py:271
  66.5 1.9 %collective-permute-start.9 = (bf16[256,1024]{1,0:T(8,128)(2,1)}, bf16[256,1024]{1,0:T(8,128)(2,1)}, u32[]{:S(2)}, u32[]{:S(2)}) collective-permute-start(bf16[256,1024]{1,0:T(8,128)(2,1)} %collective-permute-done.6.refs_10_), channel_id=1, source_target_pairs={{270,0},{3,1},{286,16},{19,17},{302,32},{35,33},{318,48},{51,49},{... | collective-permute-start | bytes 1572872 | tf_op jit(solution)/shard_map/ppermute | solution.py:274
  68.4 9.8 %collective-permute-start.8 = (bf16[384,512]{0,1:T(8,128)(2,1)S(1)}, bf16[384,512]{0,1:T(8,128)(2,1)S(1)}, u32[]{:S(2)}, u32[]{:S(2)}) collective-permute-start(bf16[384,512]{0,1:T(8,128)(2,1)S(1)} %pad_maximum_fusion.3), channel_id=1, source_target_pairs={{0,1},{1,0},{2,3},{3,2},{4,5},{5,4},{6,7},{7,6},{8,9},{9,8},{10,11... | collective-permute-start | bytes 1179656 | tf_op jit(solution)/shard_map/ppermute | solution.py:233
  82.9 13.0 %shard_map.76 = (bf16[1024,1024]{1,0:T(8,128)(2,1)}, bf16[16,16,16,256]{3,2,1,0:T(8,128)(2,1)}, f32[128,1024]{1,0:T(8,128)}, bf16[128,1024]{1,0:T(8,128)(2,1)}, ...) custom-call(s32[2]{0:T(128)} %pad_add_fusion.pos_ref, ...), custom_call_target="tpu_custom_call" | custom-call | flops 3500000000 | bytes 14000000 | tf_op jit(solution)/shard_map/pallas_call | solution.py:172
  96.0 6.9 %all-to-all-start = ((bf16[16,16,16,256]{3,2,1,0:T(8,128)(2,1)}), bf16[16,16,16,256]{3,2,1,0:T(8,128)(2,1)S(1)}, u32[]{:S(2)}, u32[]{:S(2)}) async-start(bf16[16,16,16,256]{3,2,1,0:T(8,128)(2,1)} %get-tuple-element.38), calls=%async_computation | async-start | bytes 4194304 | tf_op jit(solution)/shard_map/all_to_all | solution.py:284
  102.9 1.9 %collective-permute-start.11 = (bf16[256,512]{1,0:T(8,128)(2,1)S(1)}, bf16[256,512]{1,0:T(8,128)(2,1)S(1)}, u32[]{:S(2)}, u32[]{:S(2)}) collective-permute-start(bf16[256,512]{1,0:T(8,128)(2,1)S(1)} %copy-done.14), channel_id=1, source_target_pairs={{0,2},{1,3},{2,0},{3,1},{4,6},{5,7},{6,4},{7,5},{8,10},{9,11},{10,... | collective-permute-start | bytes 786440 | tf_op jit(solution)/shard_map/ppermute | solution.py:302
  104.8 6.7 %collective-permute-done.11 = bf16[256,512]{1,0:T(8,128)(2,1)S(1)} collective-permute-done((bf16[256,512]{1,0:T(8,128)(2,1)S(1)}, bf16[256,512]{1,0:T(8,128)(2,1)S(1)}, u32[]{:S(2)}, u32[]{:S(2)}) %collective-permute-start.11) | collective-permute-done | bytes 262176 | tf_op jit(solution)/shard_map/ppermute | solution.py:302
  113.5 3.9 %collective-permute-start.10 = (bf16[128,1024]{1,0:T(8,128)(2,1)}, bf16[128,1024]{1,0:T(8,128)(2,1)S(1)}, u32[]{:S(2)}, u32[]{:S(2)}) collective-permute-start(bf16[128,1024]{1,0:T(8,128)(2,1)} %get-tuple-element.32), channel_id=1, source_target_pairs={{0,1},{1,0},{2,3},{3,2},{4,5},{5,4},{6,7},{7,6},{8,9},{9,8},{10,11... | collective-permute-start | bytes 786440 | tf_op jit(solution)/shard_map/ppermute | solution.py:233
  119.2 4.2 %collective-permute-start.13 = (bf16[32,512]{1,0:T(8,128)(2,1)S(1)}, bf16[32,512]{1,0:T(8,128)(2,1)S(1)}, u32[]{:S(2)}, u32[]{:S(2)}) collective-permute-start(bf16[32,512]{1,0:T(8,128)(2,1)S(1)} %fusion.13), channel_id=1, source_target_pairs={{0,8},{1,9},{2,10},{3,11},{4,12},{5,13},{6,14},{7,15},{8,0},{9,1},... | collective-permute-start | bytes 98312 | tf_op jit(solution)/shard_map/ppermute | solution.py:305
  123.7 6.3 %all-to-all-done = bf16[16,16,16,256]{3,2,1,0:T(8,128)(2,1)S(1)} async-done(((bf16[16,16,16,256]{3,2,1,0:T(8,128)(2,1)}), bf16[16,16,16,256]{3,2,1,0:T(8,128)(2,1)S(1)}, u32[]{:S(2)}, u32[]{:S(2)}) %all-to-all-start) | async-done | bytes 2097184 | tf_op jit(solution)/shard_map/all_to_all | solution.py:284
  131.0 10.5 %all-to-all-start.1 = ((bf16[32,16,256]{2,1,0:T(8,128)(2,1)}), bf16[32,16,256]{2,1,0:T(8,128)(2,1)S(1)}, u32[]{:S(2)}, u32[]{:S(2)}) async-start(bf16[32,16,256]{2,1,0:T(8,128)(2,1)} %bitcast.12), calls=%async_computation.1 | async-start | bytes 524288 | tf_op jit(solution)/shard_map/all_to_all | solution.py:290
  143.8 2.1 %collective-permute-start.14 = (bf16[128,1024]{1,0:T(8,128)(2,1)S(1)}, bf16[128,1024]{1,0:T(8,128)(2,1)S(1)}, u32[]{:S(2)}, u32[]{:S(2)}) collective-permute-start(bf16[128,1024]{1,0:T(8,128)(2,1)S(1)} %dynamic-slice_convert_fusion), channel_id=1, source_target_pairs={{0,1},{1,0},{2,3},{3,2},{4,5},{5,4},{6,7},{7,6},{8,9},{9,8},{10,11... | collective-permute-start | bytes 786440 | tf_op jit(solution)/shard_map/ppermute | solution.py:233
  145.9 17.4 %all-to-all-done.1 = bf16[32,16,256]{2,1,0:T(8,128)(2,1)S(1)} async-done(((bf16[32,16,256]{2,1,0:T(8,128)(2,1)}), bf16[32,16,256]{2,1,0:T(8,128)(2,1)S(1)}, u32[]{:S(2)}, u32[]{:S(2)}) %all-to-all-start.1) | async-done | bytes 262176 | tf_op jit(solution)/shard_map/all_to_all | solution.py:290
  164.1 3.5 %all-to-all-start.2 = ((bf16[16,2,16,256]{3,2,1,0:T(8,128)(2,1)}), bf16[16,2,16,256]{3,2,1,0:T(8,128)(2,1)S(1)}, u32[]{:S(2)}, u32[]{:S(2)}) async-start(bf16[16,2,16,256]{3,2,1,0:T(8,128)(2,1)} %broadcast_in_dim.21), calls=%async_computation.2 | async-start | bytes 524288 | tf_op jit(solution)/shard_map/all_to_all | solution.py:294
  169.2 5.9 %all-to-all-done.2 = bf16[16,2,16,256]{3,2,1,0:T(8,128)(2,1)S(1)} async-done(((bf16[16,2,16,256]{3,2,1,0:T(8,128)(2,1)}), bf16[16,2,16,256]{3,2,1,0:T(8,128)(2,1)S(1)}, u32[]{:S(2)}, u32[]{:S(2)}) %all-to-all-start.2) | async-done | bytes 262176 | tf_op jit(solution)/shard_map/all_to_all | solution.py:294
  (93 shorter events, 23.2 us)
Async XLA Ops:
  3.0 12.4 %collective-permute-start = (bf16[256,1024]{0,1:T(8,128)(2,1)S(1)}, bf16[256,1024]{0,1:T(8,128)(2,1)S(1)}, u32[]{:S(2)}, u32[]{:S(2)}) collective-permute-start(bf16[256,1024]{0,1:T(8,128)(2,1)S(1)} %pad_maximum_fusion.1), channel_id=1, source_target_pairs={{0,1},{1,0},{2,3},{3,2},{4,5},{5,4},{6,7},{7,6},{8,9},{9,8},{10,11... | collective-permute-start | bytes 1572872 | tf_op jit(solution)/shard_map/ppermute | solution.py:233
  12.1 3.2 %collective-permute-start.1 = (bf16[64,1024]{1,0:T(8,128)(2,1)S(1)}, bf16[64,1024]{1,0:T(8,128)(2,1)S(1)}, u32[]{:S(2)}, u32[]{:S(2)}) collective-permute-start(bf16[64,1024]{1,0:T(8,128)(2,1)S(1)} %bitcast.50), channel_id=1, source_target_pairs={{0,1},{1,0},{2,3},{3,2},{4,5},{5,4},{6,7},{7,6},{8,9},{9,8},{10,11... | collective-permute-start | bytes 393224 | tf_op jit(solution)/shard_map/ppermute | solution.py:233
  15.6 63.1 %copy-start = (bf16[256,1024]{0,1:T(8,128)(2,1)}, bf16[256,1024]{0,1:T(8,128)(2,1)S(1)}, u32[]{:S(2)}) copy-start(bf16[256,1024]{0,1:T(8,128)(2,1)S(1)} %fusion.4) | copy-start | bytes 1572868
  16.2 20.8 %collective-permute-start.2 = (bf16[128,1024]{1,0:T(8,128)(2,1)S(1)}, bf16[128,1024]{1,0:T(8,128)(2,1)S(1)}, u32[]{:S(2)}, u32[]{:S(2)}) collective-permute-start(bf16[128,1024]{1,0:T(8,128)(2,1)S(1)} %maximum_select_fusion.1), channel_id=1, source_target_pairs={{2,0},{271,1},{18,16},{287,17},{34,32},{303,33},{50,48},{319,49},{... | collective-permute-start | bytes 786440 | tf_op jit(solution)/shard_map/ppermute | solution.py:264
  21.9 15.0 %collective-permute-start.3 = (bf16[32,512]{0,1:T(8,128)(2,1)S(1)}, bf16[32,512]{0,1:T(8,128)(2,1)S(1)}, u32[]{:S(2)}, u32[]{:S(2)}) collective-permute-start(bf16[32,512]{0,1:T(8,128)(2,1)S(1)} %slice.66), channel_id=1, source_target_pairs={{0,8},{1,9},{2,10},{3,11},{4,12},{5,13},{6,14},{7,15},{8,0},{9,1},... | collective-permute-start | bytes 98312 | tf_op jit(solution)/shard_map/ppermute | solution.py:263
  37.2 42.8 %copy-start.5 = (bf16[256,1024]{1,0:T(8,128)(2,1)}, bf16[256,1024]{1,0:T(8,128)(2,1)S(1)}, u32[]{:S(2)}) copy-start(bf16[256,1024]{1,0:T(8,128)(2,1)S(1)} %maximum_select_fusion.refs_8_) | copy-start | bytes 1572868
  37.2 12.7 %collective-permute-start.4 = (bf16[256,1024]{1,0:T(8,128)(2,1)S(1)}, bf16[256,1024]{1,0:T(8,128)(2,1)S(1)}, u32[]{:S(2)}, u32[]{:S(2)}) collective-permute-start(bf16[256,1024]{1,0:T(8,128)(2,1)S(1)} %maximum_select_fusion.refs_8_), channel_id=1, source_target_pairs={{270,0},{3,1},{286,16},{19,17},{302,32},{35,33},{318,48},{51,49},{... | collective-permute-start | bytes 1572872 | tf_op jit(solution)/shard_map/ppermute | solution.py:268
  39.1 10.4 %collective-permute-start.5 = (bf16[96,512]{0,1:T(8,128)(2,1)S(1)}, bf16[96,512]{0,1:T(8,128)(2,1)S(1)}, u32[]{:S(2)}, u32[]{:S(2)}) collective-permute-start(bf16[96,512]{0,1:T(8,128)(2,1)S(1)} %pad_maximum_fusion.5), channel_id=1, source_target_pairs={{0,4},{1,5},{2,6},{3,7},{4,0},{5,1},{6,2},{7,3},{8,12},{9,13},{10,... | collective-permute-start | bytes 294920 | tf_op jit(solution)/shard_map/ppermute | solution.py:267
  49.9 32.0 %copy-start.13 = (bf16[256,1024]{1,0:T(8,128)(2,1)}, bf16[256,1024]{1,0:T(8,128)(2,1)S(1)}, u32[]{:S(2)}) copy-start(bf16[256,1024]{1,0:T(8,128)(2,1)S(1)} %collective-permute-done.4.refs_9_) | copy-start | bytes 1572868
  49.9 16.5 %collective-permute-start.6 = (bf16[256,1024]{1,0:T(8,128)(2,1)S(1)}, bf16[256,1024]{1,0:T(8,128)(2,1)}, u32[]{:S(2)}, u32[]{:S(2)}) collective-permute-start(bf16[256,1024]{1,0:T(8,128)(2,1)S(1)} %collective-permute-done.4.refs_9_), channel_id=1, source_target_pairs={{2,0},{271,1},{18,16},{287,17},{34,32},{303,33},{50,48},{319,49},{... | collective-permute-start | bytes 1572872 | tf_op jit(solution)/shard_map/ppermute | solution.py:272
  56.1 10.3 %collective-permute-start.7 = (bf16[256,512]{0,1:T(8,128)(2,1)S(1)}, bf16[256,512]{0,1:T(8,128)(2,1)S(1)}, u32[]{:S(2)}, u32[]{:S(2)}) collective-permute-start(bf16[256,512]{0,1:T(8,128)(2,1)S(1)} %pad_maximum_fusion.4), channel_id=1, source_target_pairs={{0,2},{1,3},{2,0},{3,1},{4,6},{5,7},{6,4},{7,5},{8,10},{9,11},{10,... | collective-permute-start | bytes 786440 | tf_op jit(solution)/shard_map/ppermute | solution.py:271
  66.5 16.5 %collective-permute-start.9 = (bf16[256,1024]{1,0:T(8,128)(2,1)}, bf16[256,1024]{1,0:T(8,128)(2,1)}, u32[]{:S(2)}, u32[]{:S(2)}) collective-permute-start(bf16[256,1024]{1,0:T(8,128)(2,1)} %collective-permute-done.6.refs_10_), channel_id=1, source_target_pairs={{270,0},{3,1},{286,16},{19,17},{302,32},{35,33},{318,48},{51,49},{... | collective-permute-start | bytes 1572872 | tf_op jit(solution)/shard_map/ppermute | solution.py:274
  68.4 13.6 %collective-permute-start.8 = (bf16[384,512]{0,1:T(8,128)(2,1)S(1)}, bf16[384,512]{0,1:T(8,128)(2,1)S(1)}, u32[]{:S(2)}, u32[]{:S(2)}) collective-permute-start(bf16[384,512]{0,1:T(8,128)(2,1)S(1)} %pad_maximum_fusion.3), channel_id=1, source_target_pairs={{0,1},{1,0},{2,3},{3,2},{4,5},{5,4},{6,7},{7,6},{8,9},{9,8},{10,11... | collective-permute-start | bytes 1179656 | tf_op jit(solution)/shard_map/ppermute | solution.py:233
  95.9 27.5 %copy-start.12 = (bf16[256,64]{1,0:T(8,128)(2,1)S(1)}, bf16[256,64]{1,0:T(8,128)(2,1)}, u32[]{:S(2)}) copy-start(bf16[256,64]{1,0:T(8,128)(2,1)} %constant.31) | copy-start | bytes 98308
  96.0 34.0 %all-to-all-start = ((bf16[16,16,16,256]{3,2,1,0:T(8,128)(2,1)}), bf16[16,16,16,256]{3,2,1,0:T(8,128)(2,1)S(1)}, u32[]{:S(2)}, u32[]{:S(2)}) async-start(bf16[16,16,16,256]{3,2,1,0:T(8,128)(2,1)} %get-tuple-element.38), calls=%async_computation | async-start | bytes 4194304 | tf_op jit(solution)/shard_map/all_to_all | solution.py:284
  102.9 8.6 %collective-permute-start.11 = (bf16[256,512]{1,0:T(8,128)(2,1)S(1)}, bf16[256,512]{1,0:T(8,128)(2,1)S(1)}, u32[]{:S(2)}, u32[]{:S(2)}) collective-permute-start(bf16[256,512]{1,0:T(8,128)(2,1)S(1)} %copy-done.14), channel_id=1, source_target_pairs={{0,2},{1,3},{2,0},{3,1},{4,6},{5,7},{6,4},{7,5},{8,10},{9,11},{10,... | collective-permute-start | bytes 786440 | tf_op jit(solution)/shard_map/ppermute | solution.py:302
  111.6 30.0 %copy-start.11 = (bf16[256,32]{1,0:T(8,128)(2,1)S(1)}, bf16[256,32]{1,0:T(8,128)(2,1)}, u32[]{:S(2)}) copy-start(bf16[256,32]{1,0:T(8,128)(2,1)} %constant.32) | copy-start | bytes 49156
  111.6 7.6 %collective-permute-start.12 = (bf16[96,512]{1,0:T(8,128)(2,1)S(1)}, bf16[96,512]{1,0:T(8,128)(2,1)S(1)}, u32[]{:S(2)}, u32[]{:S(2)}) collective-permute-start(bf16[96,512]{1,0:T(8,128)(2,1)S(1)} %pad_maximum_fusion.7), channel_id=1, source_target_pairs={{0,4},{1,5},{2,6},{3,7},{4,0},{5,1},{6,2},{7,3},{8,12},{9,13},{10,... | collective-permute-start | bytes 294920 | tf_op jit(solution)/shard_map/ppermute | solution.py:304
  113.5 54.1 %collective-permute-start.10 = (bf16[128,1024]{1,0:T(8,128)(2,1)}, bf16[128,1024]{1,0:T(8,128)(2,1)S(1)}, u32[]{:S(2)}, u32[]{:S(2)}) collective-permute-start(bf16[128,1024]{1,0:T(8,128)(2,1)} %get-tuple-element.32), channel_id=1, source_target_pairs={{0,1},{1,0},{2,3},{3,2},{4,5},{5,4},{6,7},{7,6},{8,9},{9,8},{10,11... | collective-permute-start | bytes 786440 | tf_op jit(solution)/shard_map/ppermute | solution.py:233
  119.2 22.3 %collective-permute-start.13 = (bf16[32,512]{1,0:T(8,128)(2,1)S(1)}, bf16[32,512]{1,0:T(8,128)(2,1)S(1)}, u32[]{:S(2)}, u32[]{:S(2)}) collective-permute-start(bf16[32,512]{1,0:T(8,128)(2,1)S(1)} %fusion.13), channel_id=1, source_target_pairs={{0,8},{1,9},{2,10},{3,11},{4,12},{5,13},{6,14},{7,15},{8,0},{9,1},... | collective-permute-start | bytes 98312 | tf_op jit(solution)/shard_map/ppermute | solution.py:305
  131.0 32.3 %all-to-all-start.1 = ((bf16[32,16,256]{2,1,0:T(8,128)(2,1)}), bf16[32,16,256]{2,1,0:T(8,128)(2,1)S(1)}, u32[]{:S(2)}, u32[]{:S(2)}) async-start(bf16[32,16,256]{2,1,0:T(8,128)(2,1)} %bitcast.12), calls=%async_computation.1 | async-start | bytes 524288 | tf_op jit(solution)/shard_map/all_to_all | solution.py:290
  143.1 24.5 %copy-start.3 = (f32[128,1024]{1,0:T(8,128)S(1)}, f32[128,1024]{1,0:T(8,128)}, u32[]{:S(2)}) copy-start(f32[128,1024]{1,0:T(8,128)} %get-tuple-element.31) | copy-start | bytes 1572868
  143.8 24.6 %collective-permute-start.14 = (bf16[128,1024]{1,0:T(8,128)(2,1)S(1)}, bf16[128,1024]{1,0:T(8,128)(2,1)S(1)}, u32[]{:S(2)}, u32[]{:S(2)}) collective-permute-start(bf16[128,1024]{1,0:T(8,128)(2,1)S(1)} %dynamic-slice_convert_fusion), channel_id=1, source_target_pairs={{0,1},{1,0},{2,3},{3,2},{4,5},{5,4},{6,7},{7,6},{8,9},{9,8},{10,11... | collective-permute-start | bytes 786440 | tf_op jit(solution)/shard_map/ppermute | solution.py:233
  164.1 11.0 %all-to-all-start.2 = ((bf16[16,2,16,256]{3,2,1,0:T(8,128)(2,1)}), bf16[16,2,16,256]{3,2,1,0:T(8,128)(2,1)S(1)}, u32[]{:S(2)}, u32[]{:S(2)}) async-start(bf16[16,2,16,256]{3,2,1,0:T(8,128)(2,1)} %broadcast_in_dim.21), calls=%async_computation.2 | async-start | bytes 524288 | tf_op jit(solution)/shard_map/all_to_all | solution.py:294
  (11 other events, 113.8 us)

commit v7 on v6

--- a/solution.py
+++ b/solution.py
@@ -27,11 +27,12 @@
 
 def layer_kernel(nx, ny, pos_ref, *refs):
     sources, refs = refs[:12], refs[12:]
-    results, refs = refs[:8], refs[8:]
-    staged, refs = refs[:8], refs[8:]
+    results, refs = refs[:9], refs[9:]
+    staged, refs = refs[:9], refs[9:]
     (tok_s, tokt_s, g_s, gt_s, kv_s, kvt_s, qm_s, gm_s, gkv_s, attt_s, dqt_s, att_s, in_sem, w_sem, out_sem, part_sem) = refs
     own, ownt, mine, minet, other, othert, g, gt, n1, n2, n3, n4 = sources
-    w_s, part_s, lown_s, lsend_s, dq_s, gown_s, gkeep_s, gsend_s = staged
+    w_s, lown_s, lsend_s, dq_s, gown_s, gkeep_s, gsend_s = staged[:1] + staged[3:]
+    part_s, part_out = staged[1:3], results[1:3]
     zl = pos_ref[0]
     core = pos_ref[1]
     even = lax.rem(zl + core, 2) == 0
@@ -58,7 +59,7 @@
     inputs = [pltpu.make_async_copy(src, dst, in_sem.at[i]) for i, (src, dst) in enumerate(pairs)]
     for copy in inputs[:3] + weight_copies + inputs[3:]:
         copy.start()
-    outputs = {i: pltpu.make_async_copy(staged[i], results[i], out_sem.at[i]) for i in (0, 2, 3, 4, 5, 6, 7)}
+    outputs = {i: pltpu.make_async_copy(staged[i], results[i], out_sem.at[i]) for i in (0, 3, 4, 5, 6, 7, 8)}
     for copy in inputs[:3] + weight_copies:
         copy.wait()
     outputs[0].start()
@@ -117,17 +118,18 @@
     attended = attt_s[...].T.astype(BF)
     att_s[0] = attended[0:128]
     att_s[1] = attended[128:256]
-    for index in (4, 5, 6, 7):
+    for index in (5, 6, 7, 8):
         outputs[index].start()
 
     x_rows = 64 // nx
-    y_cols = 1024 // ny
+    y_cols = 512 // ny
     for copy in inputs[4:]:
         copy.wait()
 
-    def part_copy(low):
+    def part_copies(low):
         where = pl.ds(8 * low, 8)
-        return pltpu.make_async_copy(part_s.at[:, where], results[1].at[:, where], part_sem.at[low])
+        return [pltpu.make_async_copy(part_s[half].at[:, where], part_out[half].at[:, where], part_sem.at[low, half])
+                for half in range(2)]
 
     def grad_rows(low, quad, carry):
         rows = pl.ds(pl.multiple_of((2 * quad + low) * 128, 128), 128)
@@ -139,20 +141,24 @@
         for side in range(2):
             for x in range(nx):
                 for y in range(ny):
-                    part_s[x * ny + y, (2 * low + side) * 4 + quad] = block[
-                        side * 64 + x * x_rows:side * 64 + (x + 1) * x_rows, y * y_cols:(y + 1) * y_cols]
+                    for half in range(2):
+                        col = (2 * y + half) * y_cols
+                        part_s[half][x * ny + y, (2 * low + side) * 4 + quad] = block[
+                            side * 64 + x * x_rows:side * 64 + (x + 1) * x_rows, col:col + y_cols]
         return carry
 
     for low in range(2):
         lax.fori_loop(0, 4, functools.partial(grad_rows, low), 0)
-        part_copy(low).start()
+        for copy in part_copies(low):
+            copy.start()
     lown_s[...] = nt(att_s[core], w_s[:, 768:1024])
     lsend_s[...] = nt(att_s[1 - core], w_s[:, 768:1024]).astype(BF)
-    outputs[2].start()
     outputs[3].start()
+    outputs[4].start()
     for low in range(2):
-        part_copy(low).wait()
-    for index in (0, 2, 3, 4, 5, 6, 7):
+        for copy in part_copies(low):
+            copy.wait()
+    for index in (0, 3, 4, 5, 6, 7, 8):
         outputs[index].wait()
 
 
@@ -161,7 +167,8 @@
     smem = pl.BlockSpec(memory_space=pltpu.SMEM)
     results = (
         ((1024, 1024), BF),
-        ((nx * ny, 16, 64 // nx, 1024 // ny), BF),
+        ((nx * ny, 16, 64 // nx, 512 // ny), BF),
+        ((nx * ny, 16, 64 // nx, 512 // ny), BF),
         ((128, 1024), F32),
         ((128, 1024), BF),
         ((256, 256), BF),
@@ -189,8 +196,8 @@
             pltpu.VMEM((2, 128, 256), BF),
             pltpu.SemaphoreType.DMA((8,)),
             pltpu.SemaphoreType.DMA((8,)),
-            pltpu.SemaphoreType.DMA((8,)),
-            pltpu.SemaphoreType.DMA((2,)),
+            pltpu.SemaphoreType.DMA((9,)),
+            pltpu.SemaphoreType.DMA((2, 2)),
         ],
         compiler_params=pltpu.CompilerParams(vmem_limit_bytes=60 * 1024 * 1024),
         cost_estimate=pl.CostEstimate(flops=3_500_000_000, bytes_accessed=14_000_000, transcendentals=700_000),
@@ -275,20 +282,22 @@
         other_set = swap_core(half_set)
 
         position = jnp.stack([zl, core]).astype(jnp.int32)
-        (weight, part, layer_own, layer_send, dquery, grad_own, grad_keep, grad_send) = run_layer(
+        (weight, part_a, part_b, layer_own, layer_send, dquery, grad_own, grad_keep, grad_send) = run_layer(
             nx, ny, position, chip_tokens, chip_tokens.T, half_set, half_set.T, other_set, other_set.T,
             chip_grads, chip_grads.T,
             n1, n2, n3, n4)
 
-        if nxy > 1:
-            pieces = lax.all_to_all(part, "dp", 0, 0, axis_index_groups=plane_groups, tiled=True)
-        else:
-            pieces = part
-        plane_sum = jnp.sum(pieces.astype(F32), axis=0).astype(BF)
         rows, cols = 64 // nx, 1024 // ny
-        copies = jnp.broadcast_to(plane_sum[None], (nzh, 16, rows, cols)).reshape(nzh * 16, rows, cols)
-        columns = lax.all_to_all(copies, both, 0, 0, axis_index_groups=line_groups, tiled=True)
-        line_sum = jnp.sum(columns.astype(F32).reshape(nzh * 2, 2, 4, rows, cols), axis=(0, 2)).astype(BF)
+
+        def reduced(part):
+            if nxy > 1:
+                part = lax.all_to_all(part, "dp", 0, 0, axis_index_groups=plane_groups, tiled=True)
+            plane_sum = jnp.sum(part.astype(F32), axis=0).astype(BF)
+            copies = jnp.broadcast_to(plane_sum[None], (nzh,) + plane_sum.shape).reshape(nzh * 16, rows, cols // 2)
+            columns = lax.all_to_all(copies, both, 0, 0, axis_index_groups=line_groups, tiled=True)
+            return jnp.sum(columns.astype(F32).reshape(nzh * 2, 2, 4, rows, cols // 2), axis=(0, 2)).astype(BF)
+
+        line_sum = jnp.concatenate([reduced(part_a), reduced(part_b)], axis=-1)
         spread = jnp.broadcast_to(line_sum[None], (nxy, 2, rows, cols))
         if nxy > 1:
             spread = lax.all_to_all(spread, "dp", 0, 0, axis_index_groups=plane_groups, tiled=True)

time: 178 us -> 201 us (1.13)
  waiting for transfers between devices: 68.7 us -> 79.3 us
  starting transfers between devices: 77.7 us -> 86.1 us
  matrix products: 1.48 us -> 5.48 us
    all_to_all x2 -> x4, waiting for transfers between devices: 23.7 us -> 42.9 us  [the longest x2 25.1 us: reduced(): lax.all_to_all(copies, both, 0, 0, axis_index_groups=line_groups, tiled=T...]
    all_to_all x2 -> x4, starting transfers between devices: 17.4 us -> 25.6 us  [the longest x2 14.7 us: reduced(): lax.all_to_all(copies, both, 0, 0, axis_index_groups=line_groups, tiled=T...]
    ppermute x1, waiting for transfers between devices: 6.72 us -> 0.01 us  [per_device(): b1 = lax.ppermute(grad_send, 'seq', chip_swap(0))]
    dot_general x4, matrix products: 0.86 us -> 3.42 us  [nn(): lax.dot_general(a, b, (((1,), (0,)), ((), ())), preferred_element_type=F32)]
    ppermute x1, starting transfers between devices: 4.21 us -> 1.92 us  [per_device(): lax.ppermute((joined[64:96] + b2[64:96].astype(F32)).astype(BF), 'seq', c...]
    unnamed x40 -> x32, local copies, waits for them, and re-layouts: 5.1 us -> 4.08 us
  transfers between devices with their start and end apart: 18 -> 20, of which waited for: 9 -> 9; matrix products, arithmetic and copies ran while one was open for 6% -> 7% of each run, Pallas kernels for 0% -> 0%
where the time goes in v7:
time: 201 us; the launch traced here: 200 us
  starting transfers between devices  86.1 us (43%)
  waiting for transfers between devices  79.3 us (39%)
  Pallas kernels  13 us (6%)
  local copies, waits for them, and re-layouts  10.6 us (5%)
  matrix products  5.48 us (3%)
  other arithmetic  3.8 us (2%)
    ppermute x5, starting transfers between devices, swap_core(): return lax.ppermute(value, 'seq', core_pairs)  27.6 us
    all_to_all x2, waiting for transfers between devices, reduced(): lax.all_to_all(copies, both, 0, 0, axis_index_groups=line_groups, tiled=T...  25.1 us
    all_to_all x2, waiting for transfers between devices, reduced(): lax.all_to_all(part, 'dp', 0, 0, axis_index_groups=plane_groups, tiled=True)  17.8 us
    all_to_all x2, starting transfers between devices, reduced(): lax.all_to_all(copies, both, 0, 0, axis_index_groups=line_groups, tiled=T...  14.7 us
    ppermute x1, waiting for transfers between devices, per_device(): t3 = lax.ppermute(c3, 'seq', chip_swap(2))  13 us
    pallas_call x1, Pallas kernels, run_layer(): pl.pallas_call(functools.partial(layer_kernel, nx, ny), out_shape=tuple((...  13 us
    all_to_all x2, starting transfers between devices, reduced(): lax.all_to_all(part, 'dp', 0, 0, axis_index_groups=plane_groups, tiled=True)  10.8 us
    ppermute x1, waiting for transfers between devices, per_device(): third = lax.ppermute(to_third, 'seq', chip_swap(0))  8.36 us
  transfers between devices with their start and end apart: 20, of which 9 were waited for; matrix products, arithmetic and copies ran while one was open for 7% of the time, Pallas kernels for 0%

profile of v7, /device:TPU:1, one launch (start us, length us, event | category | flops | bytes accessed | tf_op | source)
XLA Modules:
  0.0 199.5 jit_solution(4148971028047500752)
XLA Ops:
  3.0 8.9 %collective-permute-start = (bf16[256,1024]{0,1:T(8,128)(2,1)S(1)}, bf16[256,1024]{0,1:T(8,128)(2,1)S(1)}, u32[]{:S(2)}, u32[]{:S(2)}) collective-permute-start(bf16[256,1024]{0,1:T(8,128)(2,1)S(1)} %pad_maximum_fusion.1), channel_id=1, source_target_pairs={{0,1},{1,0},{2,3},{3,2},{4,5},{5,4},{6,7},{7,6},{8,9},{9,8},{10,11... | collective-permute-start | bytes 1572872 | tf_op jit(solution)/shard_map/ppermute | solution.py:240
  16.2 5.8 %collective-permute-start.2 = (bf16[128,1024]{1,0:T(8,128)(2,1)S(1)}, bf16[128,1024]{1,0:T(8,128)(2,1)S(1)}, u32[]{:S(2)}, u32[]{:S(2)}) collective-permute-start(bf16[128,1024]{1,0:T(8,128)(2,1)S(1)} %maximum_select_fusion.1), channel_id=1, source_target_pairs={{2,0},{271,1},{18,16},{287,17},{34,32},{303,33},{50,48},{319,49},{... | collective-permute-start | bytes 786440 | tf_op jit(solution)/shard_map/ppermute | solution.py:271
  23.9 13.0 %collective-permute-done.3 = bf16[32,512]{0,1:T(8,128)(2,1)S(1)} collective-permute-done((bf16[32,512]{0,1:T(8,128)(2,1)S(1)}, bf16[32,512]{0,1:T(8,128)(2,1)S(1)}, u32[]{:S(2)}, u32[]{:S(2)}) %collective-permute-start.3) | collective-permute-done | bytes 32800 | tf_op jit(solution)/shard_map/ppermute | solution.py:270
  39.1 2.5 %collective-permute-start.5 = (bf16[96,512]{0,1:T(8,128)(2,1)S(1)}, bf16[96,512]{0,1:T(8,128)(2,1)S(1)}, u32[]{:S(2)}, u32[]{:S(2)}) collective-permute-start(bf16[96,512]{0,1:T(8,128)(2,1)S(1)} %pad_maximum_fusion.5), channel_id=1, source_target_pairs={{0,4},{1,5},{2,6},{3,7},{4,0},{5,1},{6,2},{7,3},{8,12},{9,13},{10,... | collective-permute-start | bytes 294920 | tf_op jit(solution)/shard_map/ppermute | solution.py:274
  41.7 7.8 %collective-permute-done.5 = bf16[96,512]{0,1:T(8,128)(2,1)S(1)} collective-permute-done((bf16[96,512]{0,1:T(8,128)(2,1)S(1)}, bf16[96,512]{0,1:T(8,128)(2,1)S(1)}, u32[]{:S(2)}, u32[]{:S(2)}) %collective-permute-start.5) | collective-permute-done | bytes 98336 | tf_op jit(solution)/shard_map/ppermute | solution.py:274
  49.9 6.1 %collective-permute-start.6 = (bf16[256,1024]{1,0:T(8,128)(2,1)S(1)}, bf16[256,1024]{1,0:T(8,128)(2,1)}, u32[]{:S(2)}, u32[]{:S(2)}) collective-permute-start(bf16[256,1024]{1,0:T(8,128)(2,1)S(1)} %collective-permute-done.4.refs_9_), channel_id=1, source_target_pairs={{2,0},{271,1},{18,16},{287,17},{34,32},{303,33},{50,48},{319,49},{... | collective-permute-start | bytes 1572872 | tf_op jit(solution)/shard_map/ppermute | solution.py:279
  58.0 8.4 %collective-permute-done.7 = bf16[256,512]{0,1:T(8,128)(2,1)S(1)} collective-permute-done((bf16[256,512]{0,1:T(8,128)(2,1)S(1)}, bf16[256,512]{0,1:T(8,128)(2,1)S(1)}, u32[]{:S(2)}, u32[]{:S(2)}) %collective-permute-start.7) | collective-permute-done | bytes 262176 | tf_op jit(solution)/shard_map/ppermute | solution.py:278
  66.5 1.9 collective-permute-start.9
  68.4 9.8 %collective-permute-start.8 = (bf16[384,512]{0,1:T(8,128)(2,1)S(1)}, bf16[384,512]{0,1:T(8,128)(2,1)S(1)}, u32[]{:S(2)}, u32[]{:S(2)}) collective-permute-start(bf16[384,512]{0,1:T(8,128)(2,1)S(1)} %pad_maximum_fusion.3), channel_id=1, source_target_pairs={{0,1},{1,0},{2,3},{3,2},{4,5},{5,4},{6,7},{7,6},{8,9},{9,8},{10,11... | collective-permute-start | bytes 1179656 | tf_op jit(solution)/shard_map/ppermute | solution.py:240
  83.0 13.0 %shard_map.76 = (bf16[1024,1024]{1,0:T(8,128)(2,1)}, bf16[16,16,16,128]{3,2,1,0:T(8,128)(2,1)}, bf16[16,16,16,128]{3,2,1,0:T(8,128)(2,1)}, f32[128,1024]{1,0:T(8...) custom-call(s32[2]{0:T(128)} %pad_add_fusion.pos_ref, ...), custom_call_target="tpu_custom_call" | custom-call | flops 3500000000 | bytes 14000000 | tf_op jit(solution)/shard_map/pallas_call | solution.py:179
  96.0 6.9 %all-to-all-start.2 = ((bf16[16,16,16,128]{3,2,1,0:T(8,128)(2,1)}), bf16[16,16,16,128]{3,2,1,0:T(8,128)(2,1)S(1)}, u32[]{:S(2)}, u32[]{:S(2)}) async-start(bf16[16,16,16,128]{3,2,1,0:T(8,128)(2,1)} %get-tuple-element.40), calls=%async_computation.2 | async-start | bytes 2097152 | tf_op jit(solution)/shard_map/all_to_all | solution.py:294
  104.9 13.5 %all-to-all-done.2 = bf16[16,16,16,128]{3,2,1,0:T(8,128)(2,1)S(1)} async-done(((bf16[16,16,16,128]{3,2,1,0:T(8,128)(2,1)}), bf16[16,16,16,128]{3,2,1,0:T(8,128)(2,1)S(1)}, u32[]{:S(2)}, u32[]{:S(2)}) %all-to-all-start.2) | async-done | bytes 1048608 | tf_op jit(solution)/shard_map/all_to_all | solution.py:294
  118.4 3.9 %all-to-all-start = ((bf16[16,16,16,128]{3,2,1,0:T(8,128)(2,1)}), bf16[16,16,16,128]{3,2,1,0:T(8,128)(2,1)S(1)}, u32[]{:S(2)}, u32[]{:S(2)}) async-start(bf16[16,16,16,128]{3,2,1,0:T(8,128)(2,1)} %get-tuple-element.39), calls=%async_computation | async-start | bytes 2097152 | tf_op jit(solution)/shard_map/all_to_all | solution.py:294
  122.4 1.9 collective-permute-start.12
  124.4 4.8 %collective-permute-start.10 = (bf16[128,1024]{1,0:T(8,128)(2,1)}, bf16[128,1024]{1,0:T(8,128)(2,1)S(1)}, u32[]{:S(2)}, u32[]{:S(2)}) collective-permute-start(bf16[128,1024]{1,0:T(8,128)(2,1)} %get-tuple-element.33), channel_id=1, source_target_pairs={{0,1},{1,0},{2,3},{3,2},{4,5},{5,4},{6,7},{7,6},{8,9},{9,8},{10,11... | collective-permute-start | bytes 786440 | tf_op jit(solution)/shard_map/ppermute | solution.py:240
  132.3 4.3 %all-to-all-done = bf16[16,16,16,128]{3,2,1,0:T(8,128)(2,1)S(1)} async-done(((bf16[16,16,16,128]{3,2,1,0:T(8,128)(2,1)}), bf16[16,16,16,128]{3,2,1,0:T(8,128)(2,1)S(1)}, u32[]{:S(2)}, u32[]{:S(2)}) %all-to-all-start) | async-done | bytes 1048608 | tf_op jit(solution)/shard_map/all_to_all | solution.py:294
  137.3 10.2 %all-to-all-start.3 = ((bf16[32,16,128]{2,1,0:T(8,128)(2,1)}), bf16[32,16,128]{2,1,0:T(8,128)(2,1)S(1)}, u32[]{:S(2)}, u32[]{:S(2)}) async-start(bf16[32,16,128]{2,1,0:T(8,128)(2,1)} %bitcast.14), calls=%async_computation.3 | async-start | bytes 262144 | tf_op jit(solution)/shard_map/all_to_all | solution.py:297
  149.8 13.8 %all-to-all-done.3 = bf16[32,16,128]{2,1,0:T(8,128)(2,1)S(1)} async-done(((bf16[32,16,128]{2,1,0:T(8,128)(2,1)}), bf16[32,16,128]{2,1,0:T(8,128)(2,1)S(1)}, u32[]{:S(2)}, u32[]{:S(2)}) %all-to-all-start.3) | async-done | bytes 131104 | tf_op jit(solution)/shard_map/all_to_all | solution.py:297
  164.2 4.6 %all-to-all-start.1 = ((bf16[32,16,128]{2,1,0:T(8,128)(2,1)}), bf16[32,16,128]{2,1,0:T(8,128)(2,1)S(1)}, u32[]{:S(2)}, u32[]{:S(2)}) async-start(bf16[32,16,128]{2,1,0:T(8,128)(2,1)} %bitcast.12), calls=%async_computation.1 | async-start | bytes 262144 | tf_op jit(solution)/shard_map/all_to_all | solution.py:297
  168.9 2.1 %fusion = f32[256,1024]{1,0:T(8,128)S(1)} fusion(bf16[1024,1024]{1,0:T(8,128)(2,1)} %get-tuple-element.38, bf16[256,512]{1,0:T(8,128)(2,1)S(1)} %add_convert_fusion.1, bf16[256,256]{1,0:T(8,128)(2,1)S(1)} %copy-done.12), kind=kOutput, calls=%fused_computation | convolution fusion | flops 403439616 | bytes 3014656 | tf_op jit(solution)/shard_map/dot_general | solution.py:25
  171.0 2.2 %collective-permute-start.14 = (bf16[128,1024]{1,0:T(8,128)(2,1)S(1)}, bf16[128,1024]{1,0:T(8,128)(2,1)S(1)}, u32[]{:S(2)}, u32[]{:S(2)}) collective-permute-start(bf16[128,1024]{1,0:T(8,128)(2,1)S(1)} %dynamic-slice_convert_fusion), channel_id=1, source_target_pairs={{0,1},{1,0},{2,3},{3,2},{4,5},{5,4},{6,7},{7,6},{8,9},{9,8},{10,11... | collective-permute-start | bytes 786440 | tf_op jit(solution)/shard_map/ppermute | solution.py:240
  173.3 11.4 %all-to-all-done.1 = bf16[32,16,128]{2,1,0:T(8,128)(2,1)S(1)} async-done(((bf16[32,16,128]{2,1,0:T(8,128)(2,1)}), bf16[32,16,128]{2,1,0:T(8,128)(2,1)S(1)}, u32[]{:S(2)}, u32[]{:S(2)}) %all-to-all-start.1) | async-done | bytes 131104 | tf_op jit(solution)/shard_map/all_to_all | solution.py:297
  185.4 5.0 %all-to-all-start.4 = ((bf16[16,2,16,256]{3,2,1,0:T(8,128)(2,1)}), bf16[16,2,16,256]{3,2,1,0:T(8,128)(2,1)S(1)}, u32[]{:S(2)}, u32[]{:S(2)}) async-start(bf16[16,2,16,256]{3,2,1,0:T(8,128)(2,1)} %broadcast_in_dim.28), calls=%async_computation.4 | async-start | bytes 524288 | tf_op jit(solution)/shard_map/all_to_all | solution.py:303
  192.0 5.8 %all-to-all-done.4 = bf16[16,2,16,256]{3,2,1,0:T(8,128)(2,1)S(1)} async-done(((bf16[16,2,16,256]{3,2,1,0:T(8,128)(2,1)}), bf16[16,2,16,256]{3,2,1,0:T(8,128)(2,1)S(1)}, u32[]{:S(2)}, u32[]{:S(2)}) %all-to-all-start.4) | async-done | bytes 262176 | tf_op jit(solution)/shard_map/all_to_all | solution.py:303
  (93 shorter events, 30.6 us)
Async XLA Ops:
  3.0 12.4 %collective-permute-start = (bf16[256,1024]{0,1:T(8,128)(2,1)S(1)}, bf16[256,1024]{0,1:T(8,128)(2,1)S(1)}, u32[]{:S(2)}, u32[]{:S(2)}) collective-permute-start(bf16[256,1024]{0,1:T(8,128)(2,1)S(1)} %pad_maximum_fusion.1), channel_id=1, source_target_pairs={{0,1},{1,0},{2,3},{3,2},{4,5},{5,4},{6,7},{7,6},{8,9},{9,8},{10,11... | collective-permute-start | bytes 1572872 | tf_op jit(solution)/shard_map/ppermute | solution.py:240
  12.1 3.2 %collective-permute-start.1 = (bf16[64,1024]{1,0:T(8,128)(2,1)S(1)}, bf16[64,1024]{1,0:T(8,128)(2,1)S(1)}, u32[]{:S(2)}, u32[]{:S(2)}) collective-permute-start(bf16[64,1024]{1,0:T(8,128)(2,1)S(1)} %bitcast.53), channel_id=1, source_target_pairs={{0,1},{1,0},{2,3},{3,2},{4,5},{5,4},{6,7},{7,6},{8,9},{9,8},{10,11... | collective-permute-start | bytes 393224 | tf_op jit(solution)/shard_map/ppermute | solution.py:240
  15.6 63.2 %copy-start = (bf16[256,1024]{0,1:T(8,128)(2,1)}, bf16[256,1024]{0,1:T(8,128)(2,1)S(1)}, u32[]{:S(2)}) copy-start(bf16[256,1024]{0,1:T(8,128)(2,1)S(1)} %fusion.4) | copy-start | bytes 1572868
  16.2 20.8 %collective-permute-start.2 = (bf16[128,1024]{1,0:T(8,128)(2,1)S(1)}, bf16[128,1024]{1,0:T(8,128)(2,1)S(1)}, u32[]{:S(2)}, u32[]{:S(2)}) collective-permute-start(bf16[128,1024]{1,0:T(8,128)(2,1)S(1)} %maximum_select_fusion.1), channel_id=1, source_target_pairs={{2,0},{271,1},{18,16},{287,17},{34,32},{303,33},{50,48},{319,49},{... | collective-permute-start | bytes 786440 | tf_op jit(solution)/shard_map/ppermute | solution.py:271
  21.9 15.0 %collective-permute-start.3 = (bf16[32,512]{0,1:T(8,128)(2,1)S(1)}, bf16[32,512]{0,1:T(8,128)(2,1)S(1)}, u32[]{:S(2)}, u32[]{:S(2)}) collective-permute-start(bf16[32,512]{0,1:T(8,128)(2,1)S(1)} %slice.66), channel_id=1, source_target_pairs={{0,8},{1,9},{2,10},{3,11},{4,12},{5,13},{6,14},{7,15},{8,0},{9,1},... | collective-permute-start | bytes 98312 | tf_op jit(solution)/shard_map/ppermute | solution.py:270
  37.2 42.9 %copy-start.5 = (bf16[256,1024]{1,0:T(8,128)(2,1)}, bf16[256,1024]{1,0:T(8,128)(2,1)S(1)}, u32[]{:S(2)}) copy-start(bf16[256,1024]{1,0:T(8,128)(2,1)S(1)} %maximum_select_fusion.refs_8_) | copy-start | bytes 1572868
  37.2 12.7 %collective-permute-start.4 = (bf16[256,1024]{1,0:T(8,128)(2,1)S(1)}, bf16[256,1024]{1,0:T(8,128)(2,1)S(1)}, u32[]{:S(2)}, u32[]{:S(2)}) collective-permute-start(bf16[256,1024]{1,0:T(8,128)(2,1)S(1)} %maximum_select_fusion.refs_8_), channel_id=1, source_target_pairs={{270,0},{3,1},{286,16},{19,17},{302,32},{35,33},{318,48},{51,49},{... | collective-permute-start | bytes 1572872 | tf_op jit(solution)/shard_map/ppermute | solution.py:275
  39.1 10.4 %collective-permute-start.5 = (bf16[96,512]{0,1:T(8,128)(2,1)S(1)}, bf16[96,512]{0,1:T(8,128)(2,1)S(1)}, u32[]{:S(2)}, u32[]{:S(2)}) collective-permute-start(bf16[96,512]{0,1:T(8,128)(2,1)S(1)} %pad_maximum_fusion.5), channel_id=1, source_target_pairs={{0,4},{1,5},{2,6},{3,7},{4,0},{5,1},{6,2},{7,3},{8,12},{9,13},{10,... | collective-permute-start | bytes 294920 | tf_op jit(solution)/shard_map/ppermute | solution.py:274
  49.9 32.1 %copy-start.10 = (bf16[256,1024]{1,0:T(8,128)(2,1)}, bf16[256,1024]{1,0:T(8,128)(2,1)S(1)}, u32[]{:S(2)}) copy-start(bf16[256,1024]{1,0:T(8,128)(2,1)S(1)} %collective-permute-done.4.refs_9_) | copy-start | bytes 1572868
  49.9 16.5 %collective-permute-start.6 = (bf16[256,1024]{1,0:T(8,128)(2,1)S(1)}, bf16[256,1024]{1,0:T(8,128)(2,1)}, u32[]{:S(2)}, u32[]{:S(2)}) collective-permute-start(bf16[256,1024]{1,0:T(8,128)(2,1)S(1)} %collective-permute-done.4.refs_9_), channel_id=1, source_target_pairs={{2,0},{271,1},{18,16},{287,17},{34,32},{303,33},{50,48},{319,49},{... | collective-permute-start | bytes 1572872 | tf_op jit(solution)/shard_map/ppermute | solution.py:279
  56.1 10.3 %collective-permute-start.7 = (bf16[256,512]{0,1:T(8,128)(2,1)S(1)}, bf16[256,512]{0,1:T(8,128)(2,1)S(1)}, u32[]{:S(2)}, u32[]{:S(2)}) collective-permute-start(bf16[256,512]{0,1:T(8,128)(2,1)S(1)} %pad_maximum_fusion.4), channel_id=1, source_target_pairs={{0,2},{1,3},{2,0},{3,1},{4,6},{5,7},{6,4},{7,5},{8,10},{9,11},{10,... | collective-permute-start | bytes 786440 | tf_op jit(solution)/shard_map/ppermute | solution.py:278
  66.5 16.5 %collective-permute-start.9 = (bf16[256,1024]{1,0:T(8,128)(2,1)}, bf16[256,1024]{1,0:T(8,128)(2,1)}, u32[]{:S(2)}, u32[]{:S(2)}) collective-permute-start(bf16[256,1024]{1,0:T(8,128)(2,1)} %collective-permute-done.6.refs_10_), channel_id=1, source_target_pairs={{270,0},{3,1},{286,16},{19,17},{302,32},{35,33},{318,48},{51,49},{... | collective-permute-start | bytes 1572872 | tf_op jit(solution)/shard_map/ppermute | solution.py:281
  68.4 13.6 %collective-permute-start.8 = (bf16[384,512]{0,1:T(8,128)(2,1)S(1)}, bf16[384,512]{0,1:T(8,128)(2,1)S(1)}, u32[]{:S(2)}, u32[]{:S(2)}) collective-permute-start(bf16[384,512]{0,1:T(8,128)(2,1)S(1)} %pad_maximum_fusion.3), channel_id=1, source_target_pairs={{0,1},{1,0},{2,3},{3,2},{4,5},{5,4},{6,7},{7,6},{8,9},{9,8},{10,11... | collective-permute-start | bytes 1179656 | tf_op jit(solution)/shard_map/ppermute | solution.py:240
  96.0 22.4 %all-to-all-start.2 = ((bf16[16,16,16,128]{3,2,1,0:T(8,128)(2,1)}), bf16[16,16,16,128]{3,2,1,0:T(8,128)(2,1)S(1)}, u32[]{:S(2)}, u32[]{:S(2)}) async-start(bf16[16,16,16,128]{3,2,1,0:T(8,128)(2,1)} %get-tuple-element.40), calls=%async_computation.2 | async-start | bytes 2097152 | tf_op jit(solution)/shard_map/all_to_all | solution.py:294
  102.9 19.4 %collective-permute-start.11 = (bf16[256,512]{1,0:T(8,128)(2,1)S(1)}, bf16[256,512]{1,0:T(8,128)(2,1)S(1)}, u32[]{:S(2)}, u32[]{:S(2)}) collective-permute-start(bf16[256,512]{1,0:T(8,128)(2,1)S(1)} %copy-done.11), channel_id=1, source_target_pairs={{0,2},{1,3},{2,0},{3,1},{4,6},{5,7},{6,4},{7,5},{8,10},{9,11},{10,... | collective-permute-start | bytes 786440 | tf_op jit(solution)/shard_map/ppermute | solution.py:311
  118.4 18.2 %all-to-all-start = ((bf16[16,16,16,128]{3,2,1,0:T(8,128)(2,1)}), bf16[16,16,16,128]{3,2,1,0:T(8,128)(2,1)S(1)}, u32[]{:S(2)}, u32[]{:S(2)}) async-start(bf16[16,16,16,128]{3,2,1,0:T(8,128)(2,1)} %get-tuple-element.39), calls=%async_computation | async-start | bytes 2097152 | tf_op jit(solution)/shard_map/all_to_all | solution.py:294
  122.4 6.7 %collective-permute-start.12 = (bf16[96,512]{1,0:T(8,128)(2,1)S(1)}, bf16[96,512]{1,0:T(8,128)(2,1)S(1)}, u32[]{:S(2)}, u32[]{:S(2)}) collective-permute-start(bf16[96,512]{1,0:T(8,128)(2,1)S(1)} %pad_maximum_fusion.7), channel_id=1, source_target_pairs={{0,4},{1,5},{2,6},{3,7},{4,0},{5,1},{6,2},{7,3},{8,12},{9,13},{10,... | collective-permute-start | bytes 294920 | tf_op jit(solution)/shard_map/ppermute | solution.py:313
  124.4 66.0 %collective-permute-start.10 = (bf16[128,1024]{1,0:T(8,128)(2,1)}, bf16[128,1024]{1,0:T(8,128)(2,1)S(1)}, u32[]{:S(2)}, u32[]{:S(2)}) collective-permute-start(bf16[128,1024]{1,0:T(8,128)(2,1)} %get-tuple-element.33), channel_id=1, source_target_pairs={{0,1},{1,0},{2,3},{3,2},{4,5},{5,4},{6,7},{7,6},{8,9},{9,8},{10,11... | collective-permute-start | bytes 786440 | tf_op jit(solution)/shard_map/ppermute | solution.py:240
  129.2 18.3 %collective-permute-start.13 = (bf16[32,512]{1,0:T(8,128)(2,1)S(1)}, bf16[32,512]{1,0:T(8,128)(2,1)S(1)}, u32[]{:S(2)}, u32[]{:S(2)}) collective-permute-start(bf16[32,512]{1,0:T(8,128)(2,1)S(1)} %fusion.13), channel_id=1, source_target_pairs={{0,8},{1,9},{2,10},{3,11},{4,12},{5,13},{6,14},{7,15},{8,0},{9,1},... | collective-permute-start | bytes 98312 | tf_op jit(solution)/shard_map/ppermute | solution.py:314
  137.3 31.5 %copy-start.4 = (f32[256,512]{1,0:T(8,128)S(1)}, f32[256,512]{1,0:T(8,128)}, u32[]{:S(2)}) copy-start(f32[256,512]{1,0:T(8,128)} %get-tuple-element.35) | copy-start | bytes 1572868
  137.3 26.2 %all-to-all-start.3 = ((bf16[32,16,128]{2,1,0:T(8,128)(2,1)}), bf16[32,16,128]{2,1,0:T(8,128)(2,1)S(1)}, u32[]{:S(2)}, u32[]{:S(2)}) async-start(bf16[32,16,128]{2,1,0:T(8,128)(2,1)} %bitcast.14), calls=%async_computation.3 | async-start | bytes 262144 | tf_op jit(solution)/shard_map/all_to_all | solution.py:297
  164.2 20.4 %all-to-all-start.1 = ((bf16[32,16,128]{2,1,0:T(8,128)(2,1)}), bf16[32,16,128]{2,1,0:T(8,128)(2,1)S(1)}, u32[]{:S(2)}, u32[]{:S(2)}) async-start(bf16[32,16,128]{2,1,0:T(8,128)(2,1)} %bitcast.12), calls=%async_computation.1 | async-start | bytes 262144 | tf_op jit(solution)/shard_map/all_to_all | solution.py:297
  171.0 20.2 %collective-permute-start.14 = (bf16[128,1024]{1,0:T(8,128)(2,1)S(1)}, bf16[128,1024]{1,0:T(8,128)(2,1)S(1)}, u32[]{:S(2)}, u32[]{:S(2)}) collective-permute-start(bf16[128,1024]{1,0:T(8,128)(2,1)S(1)} %dynamic-slice_convert_fusion), channel_id=1, source_target_pairs={{0,1},{1,0},{2,3},{3,2},{4,5},{5,4},{6,7},{7,6},{8,9},{9,8},{10,11... | collective-permute-start | bytes 786440 | tf_op jit(solution)/shard_map/ppermute | solution.py:240
  185.4 12.3 %all-to-all-start.4 = ((bf16[16,2,16,256]{3,2,1,0:T(8,128)(2,1)}), bf16[16,2,16,256]{3,2,1,0:T(8,128)(2,1)S(1)}, u32[]{:S(2)}, u32[]{:S(2)}) async-start(bf16[16,2,16,256]{3,2,1,0:T(8,128)(2,1)} %broadcast_in_dim.28), calls=%async_computation.4 | async-start | bytes 524288 | tf_op jit(solution)/shard_map/all_to_all | solution.py:303
  (9 other events, 119.5 us)

commit v8 on v6

--- a/solution.py
+++ b/solution.py
@@ -14,8 +14,10 @@
 BF = jnp.bfloat16
 F32 = jnp.float32
 
-ROW_LEVELS = ((0, 256, 0), (256, 320, 2), (320, 384, 3), (384, 512, 1), (512, 576, 2), (576, 640, 3))
-
+ROW_LEVELS = ((0, 256, 0), (256, 288, 2), (288, 320, 3), (320, 384, 1), (384, 416, 2), (416, 448, 3),
+              (448, 480, 2), (480, 512, 3), (512, 576, 1), (576, 608, 2), (608, 640, 3))
+KEPT = ((0, 32, 0), (32, 16, 64), (48, 16, 96))
+SENT = ((64, 64, 0), (128, 32, 128), (160, 16, 192), (176, 16, 224))
 
 def nn(a, b):
     return lax.dot_general(a, b, (((1,), (0,)), ((), ())), preferred_element_type=F32)
@@ -26,11 +28,11 @@
 
 
 def layer_kernel(nx, ny, pos_ref, *refs):
-    sources, refs = refs[:12], refs[12:]
+    sources, refs = refs[:10], refs[10:]
     results, refs = refs[:8], refs[8:]
     staged, refs = refs[:8], refs[8:]
     (tok_s, tokt_s, g_s, gt_s, kv_s, kvt_s, qm_s, gm_s, gkv_s, attt_s, dqt_s, att_s, in_sem, w_sem, out_sem, part_sem) = refs
-    own, ownt, mine, minet, other, othert, g, gt, n1, n2, n3, n4 = sources
+    own, ownt, rest, restt, g, gt, n1, n2, n3, n4 = sources
     w_s, part_s, lown_s, lsend_s, dq_s, gown_s, gkeep_s, gsend_s = staged
     zl = pos_ref[0]
     core = pos_ref[1]
@@ -43,23 +45,19 @@
             row = pl.multiple_of(lax.rem(start + k + 8, 8) * 128, 128)
             moves.append((piece.at[pl.ds(128 * k, 128), :], w_s.at[pl.ds(row, 128), :]))
     weight_copies = [pltpu.make_async_copy(src, dst, w_sem.at[i]) for i, (src, dst) in enumerate(moves)]
-    here = pl.ds(pl.multiple_of(core * 512, 512), 512)
-    there = pl.ds(pl.multiple_of((1 - core) * 512, 512), 512)
     pairs = (
         (own, tok_s.at[pl.ds(0, 256), :]),
-        (mine, tok_s.at[pl.ds(256, 384), here]),
-        (other, tok_s.at[pl.ds(256, 384), there]),
+        (rest, tok_s.at[pl.ds(256, 384), :]),
         (g, g_s),
         (ownt, tokt_s.at[:, pl.ds(0, 256)]),
-        (minet, tokt_s.at[here, pl.ds(256, 384)]),
-        (othert, tokt_s.at[there, pl.ds(256, 384)]),
+        (restt, tokt_s.at[:, pl.ds(256, 384)]),
         (gt, gt_s),
     )
     inputs = [pltpu.make_async_copy(src, dst, in_sem.at[i]) for i, (src, dst) in enumerate(pairs)]
-    for copy in inputs[:3] + weight_copies + inputs[3:]:
+    for copy in inputs[:2] + weight_copies + inputs[2:]:
         copy.start()
     outputs = {i: pltpu.make_async_copy(staged[i], results[i], out_sem.at[i]) for i in (0, 2, 3, 4, 5, 6, 7)}
-    for copy in inputs[:3] + weight_copies:
+    for copy in inputs[:2] + weight_copies:
         copy.wait()
     outputs[0].start()
 
@@ -72,7 +70,7 @@
 
     lax.fori_loop(0, 5, project_keys, 0)
     queries = nn(tok_s[0:256, :], w_s[:, 0:256]) * 0.125
-    inputs[3].wait()
+    inputs[2].wait()
     grads = nn(g_s[...], w_s[:, 768:1024])
     lane = lax.broadcasted_iota(jnp.int32, (256, 128), 1)
     for head in range(4):
@@ -109,10 +107,16 @@
         for col, grad in ((kcol, key_grad), (vcol, value_grad)):
             where = slice(col, col + 128)
             gown_s[:, where] = grad[0:256]
-            gkeep_s[:, where] = grad[256:384]
+            for part in range(2):
+                for start, count, to in KEPT:
+                    first = 256 + 192 * part + start
+                    gkeep_s[to + count * part:to + count * part + count, where] = grad[first:first + count]
             gkv_s[:, where] = grad.astype(BF)
 
-    gsend_s[...] = gkv_s[384:640, :]
+    for part in range(2):
+        for start, count, to in SENT:
+            first = 256 + 192 * part + start
+            gsend_s[to + count * part:to + count * part + count, :] = gkv_s[first:first + count, :]
     dq_s[...] = dqt_s[...].T.astype(BF)
     attended = attt_s[...].T.astype(BF)
     att_s[0] = attended[0:128]
@@ -122,7 +126,7 @@
 
     x_rows = 64 // nx
     y_cols = 1024 // ny
-    for copy in inputs[4:]:
+    for copy in inputs[3:]:
         copy.wait()
 
     def part_copy(low):
@@ -197,13 +201,13 @@
     )(*operands)
 
 
-def coarsening():
-    matrix = np.zeros((224, 256), np.float32)
+def coarsening(count):
+    matrix = np.zeros((count * 7 // 8, count), np.float32)
     base = 0
     for level in (1, 2, 3):
-        for row in range(256 >> level):
+        for row in range(count >> level):
             matrix[base + row, row << level:(row + 1) << level] = 0.5 ** level
-        base += 256 >> level
+        base += count >> level
     return matrix
 
 
@@ -227,7 +231,7 @@
     line_groups = [[(zh * nxy + xy) * seq_count + 4 * quad + i for zh in range(nzh) for i in range(4) for quad in range(4)]
                    for xy in range(nxy)]
     plane_groups = [[zh * nxy + xy for xy in range(nxy)] for zh in range(nzh)]
-    coarse_matrix = coarsening()
+    coarse_matrix = coarsening(256)
 
     def swap_core(value):
         return lax.ppermute(value, "seq", core_pairs)
@@ -253,30 +257,29 @@
         got = swap_core(own)
         chip_tokens = ordered(own[0:128], got[0:128], 0)
         chip_grads = ordered(own[128:256], got[128:256], 0)
-        matrix = jnp.asarray(coarse_matrix, BF)
-        half_tokens = lax.dynamic_slice(chip_tokens, (0, core * 512), (256, 512))
-        coarse = nn(matrix, half_tokens).astype(BF)
-        c1, c2, c3 = coarse[0:128], coarse[128:192], coarse[192:224]
+        coarse = nn(jnp.asarray(coarsening(128), BF), tokens[0]).astype(BF)
+        c1, c2, c3 = coarse[0:64], coarse[64:96], coarse[96:112]
 
         even = (zl + core) & 1 == 0
-        w0, c3 = lax.optimization_barrier((w0, c3))
         t3 = lax.ppermute(c3, "seq", chip_swap(2))
+        w0, to_second, t3 = lax.optimization_barrier((w0, jnp.concatenate([c2, t3], 0), t3))
+        second = lax.ppermute(to_second, "seq", chip_swap(1))
         w1 = lax.ppermute(w0, both, swap_even)
+        held = jnp.concatenate([second[0:32], t3, second[32:48]], 0)
+        w1, to_third, held = lax.optimization_barrier((w1, jnp.concatenate([c1, held], 0), held))
+        third = lax.ppermute(to_third, "seq", chip_swap(0))
         n1 = jnp.where(even, jnp.concatenate([w0, w1], 0), jnp.concatenate([w1, w0], 0))
-        n1, to_second, t3 = lax.optimization_barrier((n1, jnp.concatenate([c2, t3], 0), t3))
-        second = lax.ppermute(to_second, "seq", chip_swap(1))
         n2 = lax.ppermute(n1, both, swap_odd)
-        held = jnp.concatenate([second[0:64], t3, second[64:96]], 0)
-        n2, to_third, held = lax.optimization_barrier((n2, jnp.concatenate([c1, held], 0), held))
-        third = lax.ppermute(to_third, "seq", chip_swap(0))
+        n2, half_set = lax.optimization_barrier((n2, jnp.concatenate([held, third], 0)))
+        other_set = swap_core(half_set)
         n3 = lax.ppermute(n2, both, swap_even)
-        n3, half_set = lax.optimization_barrier((n3, jnp.concatenate([held, third], 0)))
+        n3, rest, chip_tokens, chip_grads = lax.optimization_barrier(
+            (n3, ordered(half_set, other_set, 0), chip_tokens, chip_grads))
         n4 = lax.ppermute(n3, both, swap_odd)
-        other_set = swap_core(half_set)
 
         position = jnp.stack([zl, core]).astype(jnp.int32)
         (weight, part, layer_own, layer_send, dquery, grad_own, grad_keep, grad_send) = run_layer(
-            nx, ny, position, chip_tokens, chip_tokens.T, half_set, half_set.T, other_set, other_set.T,
+            nx, ny, position, chip_tokens, chip_tokens.T, rest, rest.T,
             chip_grads, chip_grads.T,
             n1, n2, n3, n4)
 

time: 178 us -> 192 us (1.079)
  waiting for transfers between devices: 68.7 us -> 75.9 us
  starting transfers between devices: 77.7 us -> 83.5 us
    ppermute x1, waiting for transfers between devices: 0.01 us -> 8.22 us  [per_device(): n3 = lax.ppermute(n2, both, swap_even)]
    ppermute x1, starting transfers between devices: 1.92 us -> 9.65 us  [per_device(): t3 = lax.ppermute(c3, 'seq', chip_swap(2))]
    ppermute x5, starting transfers between devices: 26.6 us -> 20.8 us  [swap_core(): return lax.ppermute(value, 'seq', core_pairs)]
    ppermute x1, waiting for transfers between devices: 7.85 us -> 2.47 us  [per_device(): second = lax.ppermute(to_second, 'seq', chip_swap(1))]
    ppermute x1, starting transfers between devices: 5.75 us -> 10.5 us  [per_device(): w1 = lax.ppermute(w0, both, swap_even)]
    ppermute x1, waiting for transfers between devices: 0.01 us -> 4.74 us  [per_device(): n4 = lax.ppermute(n3, both, swap_odd)]
    ppermute x1, waiting for transfers between devices: 13 us -> 17.7 us  [per_device(): t3 = lax.ppermute(c3, 'seq', chip_swap(2))]
    ppermute x1, starting transfers between devices: 6.15 us -> 1.92 us  [per_device(): n3 = lax.ppermute(n2, both, swap_even)]
  transfers between devices with their start and end apart: 18 -> 18, of which waited for: 9 -> 11; matrix products, arithmetic and copies ran while one was open for 6% -> 6% of each run, Pallas kernels for 0% -> 0%
where the time goes in v8:
time: 192 us
  starting transfers between devices  83.5 us (43%)
  waiting for transfers between devices  75.9 us (40%)
  Pallas kernels  12.9 us (7%)
  local copies, waits for them, and re-layouts  10.8 us (6%)
  other arithmetic  4.71 us (2%)
  matrix products  2.45 us (1%)
    ppermute x5, starting transfers between devices, swap_core(): return lax.ppermute(value, 'seq', core_pairs)  20.8 us
    ppermute x1, waiting for transfers between devices, per_device(): t3 = lax.ppermute(c3, 'seq', chip_swap(2))  17.7 us
    all_to_all x1, waiting for transfers between devices, per_device(): lax.all_to_all(copies, both, 0, 0, axis_index_groups=line_groups, tiled=T...  16.8 us
    pallas_call x1, Pallas kernels, run_layer(): pl.pallas_call(functools.partial(layer_kernel, nx, ny), out_shape=tuple((...  12.9 us
    all_to_all x1, starting transfers between devices, per_device(): lax.all_to_all(copies, both, 0, 0, axis_index_groups=line_groups, tiled=T...  11.1 us
    ppermute x1, starting transfers between devices, per_device(): w1 = lax.ppermute(w0, both, swap_even)  10.5 us
    ppermute x1, starting transfers between devices, per_device(): t3 = lax.ppermute(c3, 'seq', chip_swap(2))  9.65 us
    ppermute x1, waiting for transfers between devices, per_device(): n3 = lax.ppermute(n2, both, swap_even)  8.22 us
  transfers between devices with their start and end apart: 18, of which 11 were waited for; matrix products, arithmetic and copies ran while one was open for 6% of the time, Pallas kernels for 0%

profile of v8, /device:TPU:1, one launch (start us, length us, event | category | flops | bytes accessed | tf_op | source)
XLA Modules:
  0.0 191.6 jit_solution(5808767077381013736)
XLA Ops:
  2.0 9.6 %collective-permute-start.1 = (bf16[16,1024]{0,1:T(8,128)(2,1)S(1)}, bf16[16,1024]{0,1:T(8,128)(2,1)S(1)}, u32[]{:S(2)}, u32[]{:S(2)}) collective-permute-start(bf16[16,1024]{0,1:T(8,128)(2,1)S(1)} %slice.66), channel_id=1, source_target_pairs={{0,8},{1,9},{2,10},{3,11},{4,12},{5,13},{6,14},{7,15},{8,0},{9,1},... | collective-permute-start | bytes 98312 | tf_op jit(solution)/shard_map/ppermute | solution.py:264
  12.8 3.0 %collective-permute-start = (bf16[64,1024]{1,0:T(8,128)(2,1)S(1)}, bf16[64,1024]{1,0:T(8,128)(2,1)S(1)}, u32[]{:S(2)}, u32[]{:S(2)}) collective-permute-start(bf16[64,1024]{1,0:T(8,128)(2,1)S(1)} %bitcast.49), channel_id=1, source_target_pairs={{0,1},{1,0},{2,3},{3,2},{4,5},{5,4},{6,7},{7,6},{8,9},{9,8},{10,11... | collective-permute-start | bytes 393224 | tf_op jit(solution)/shard_map/ppermute | solution.py:237
  16.1 17.7 %collective-permute-done.1 = bf16[16,1024]{0,1:T(8,128)(2,1)S(1)} collective-permute-done((bf16[16,1024]{0,1:T(8,128)(2,1)S(1)}, bf16[16,1024]{0,1:T(8,128)(2,1)S(1)}, u32[]{:S(2)}, u32[]{:S(2)}) %collective-permute-start.1) | collective-permute-done | bytes 32800 | tf_op jit(solution)/shard_map/ppermute | solution.py:264
  36.2 10.5 %collective-permute-start.2 = (bf16[128,1024]{1,0:T(8,128)(2,1)S(1)}, bf16[128,1024]{1,0:T(8,128)(2,1)S(1)}, u32[]{:S(2)}, u32[]{:S(2)}) collective-permute-start(bf16[128,1024]{1,0:T(8,128)(2,1)S(1)} %maximum_select_fusion.2), channel_id=1, source_target_pairs={{2,0},{271,1},{18,16},{287,17},{34,32},{303,33},{50,48},{319,49},{... | collective-permute-start | bytes 786440 | tf_op jit(solution)/shard_map/ppermute | solution.py:267
  47.1 2.5 %collective-permute-done.3 = bf16[48,1024]{0,1:T(8,128)(2,1)S(1)} collective-permute-done((bf16[48,1024]{0,1:T(8,128)(2,1)S(1)}, bf16[48,1024]{0,1:T(8,128)(2,1)S(1)}, u32[]{:S(2)}, u32[]{:S(2)}) %collective-permute-start.3) | collective-permute-done | bytes 98336 | tf_op jit(solution)/shard_map/ppermute | solution.py:266
  50.7 5.1 %collective-permute-start.4 = (bf16[256,1024]{1,0:T(8,128)(2,1)S(1)}, bf16[256,1024]{1,0:T(8,128)(2,1)S(1)}, u32[]{:S(2)}, u32[]{:S(2)}) collective-permute-start(bf16[256,1024]{1,0:T(8,128)(2,1)S(1)} %maximum_select_fusion.1.refs_6_), channel_id=1, source_target_pairs={{270,0},{3,1},{286,16},{19,17},{302,32},{35,33},{318,48},{51,49},{... | collective-permute-start | bytes 1572872 | tf_op jit(solution)/shard_map/ppermute | solution.py:272
  55.9 7.6 %collective-permute-start.8 = (bf16[256,1024]{0,1:T(8,128)(2,1)S(1)}, bf16[256,1024]{0,1:T(8,128)(2,1)S(1)}, u32[]{:S(2)}, u32[]{:S(2)}) collective-permute-start(bf16[256,1024]{0,1:T(8,128)(2,1)S(1)} %pad_maximum_fusion.1), channel_id=1, source_target_pairs={{0,1},{1,0},{2,3},{3,2},{4,5},{5,4},{6,7},{7,6},{8,9},{9,8},{10,11... | collective-permute-start | bytes 1572872 | tf_op jit(solution)/shard_map/ppermute | solution.py:237
  63.5 1.9 %collective-permute-start.5 = (bf16[128,1024]{0,1:T(8,128)(2,1)S(1)}, bf16[128,1024]{0,1:T(8,128)(2,1)S(1)}, u32[]{:S(2)}, u32[]{:S(2)}) collective-permute-start(bf16[128,1024]{0,1:T(8,128)(2,1)S(1)} %pad_maximum_fusion.4), channel_id=1, source_target_pairs={{0,2},{1,3},{2,0},{3,1},{4,6},{5,7},{6,4},{7,5},{8,10},{9,11},{10,... | collective-permute-start | bytes 786440 | tf_op jit(solution)/shard_map/ppermute | solution.py:270
  65.5 7.9 %collective-permute-done.5 = bf16[128,1024]{0,1:T(8,128)(2,1)S(1)} collective-permute-done((bf16[128,1024]{0,1:T(8,128)(2,1)S(1)}, bf16[128,1024]{0,1:T(8,128)(2,1)S(1)}, u32[]{:S(2)}, u32[]{:S(2)}) %collective-permute-start.5) | collective-permute-done | bytes 262176 | tf_op jit(solution)/shard_map/ppermute | solution.py:270
  73.6 2.7 %collective-permute-start.7 = (bf16[192,1024]{0,1:T(8,128)(2,1)S(1)}, bf16[192,1024]{0,1:T(8,128)(2,1)S(1)}, u32[]{:S(2)}, u32[]{:S(2)}) collective-permute-start(bf16[192,1024]{0,1:T(8,128)(2,1)S(1)} %pad_maximum_fusion.3), channel_id=1, source_target_pairs={{0,1},{1,0},{2,3},{3,2},{4,5},{5,4},{6,7},{7,6},{8,9},{9,8},{10,11... | collective-permute-start | bytes 1179656 | tf_op jit(solution)/shard_map/ppermute | solution.py:237
  76.3 1.9 %collective-permute-start.6 = (bf16[256,1024]{1,0:T(8,128)(2,1)S(1)}, bf16[256,1024]{1,0:T(8,128)(2,1)}, u32[]{:S(2)}, u32[]{:S(2)}) collective-permute-start(bf16[256,1024]{1,0:T(8,128)(2,1)S(1)} %collective-permute-done.4.refs_7_), channel_id=1, source_target_pairs={{2,0},{271,1},{18,16},{287,17},{34,32},{303,33},{50,48},{319,49},{... | collective-permute-start | bytes 1572872 | tf_op jit(solution)/shard_map/ppermute | solution.py:275
  79.3 8.2 %collective-permute-done.6.refs_8_ = bf16[256,1024]{1,0:T(8,128)(2,1)} collective-permute-done((bf16[256,1024]{1,0:T(8,128)(2,1)S(1)}, bf16[256,1024]{1,0:T(8,128)(2,1)}, u32[]{:S(2)}, u32[]{:S(2)}) %collective-permute-start.6) | collective-permute-done | bytes 524320 | tf_op jit(solution)/shard_map/ppermute | solution.py:275
  93.2 4.7 %collective-permute-done.9.refs_9_ = bf16[256,1024]{1,0:T(8,128)(2,1)S(1)} collective-permute-done((bf16[256,1024]{1,0:T(8,128)(2,1)}, bf16[256,1024]{1,0:T(8,128)(2,1)S(1)}, u32[]{:S(2)}, u32[]{:S(2)}) %collective-permute-start.9) | collective-permute-done | bytes 524320 | tf_op jit(solution)/shard_map/ppermute | solution.py:278
  98.8 12.9 %shard_map.76 = (bf16[1024,1024]{1,0:T(8,128)(2,1)}, bf16[16,16,16,256]{3,2,1,0:T(8,128)(2,1)}, f32[128,1024]{1,0:T(8,128)}, bf16[128,1024]{1,0:T(8,128)(2,1)}, ...) custom-call(s32[2]{0:T(128)} %pad_add_fusion.pos_ref, ...), custom_call_target="tpu_custom_call" | custom-call | flops 3500000000 | bytes 14000000 | tf_op jit(solution)/shard_map/pallas_call | solution.py:176
  111.8 6.9 %all-to-all-start = ((bf16[16,16,16,256]{3,2,1,0:T(8,128)(2,1)}), bf16[16,16,16,256]{3,2,1,0:T(8,128)(2,1)S(1)}, u32[]{:S(2)}, u32[]{:S(2)}) async-start(bf16[16,16,16,256]{3,2,1,0:T(8,128)(2,1)} %get-tuple-element.42), calls=%async_computation | async-start | bytes 4194304 | tf_op jit(solution)/shard_map/all_to_all | solution.py:287
  120.6 5.5 %collective-permute-done.11 = bf16[256,512]{1,0:T(8,128)(2,1)S(1)} collective-permute-done((bf16[256,512]{1,0:T(8,128)(2,1)S(1)}, bf16[256,512]{1,0:T(8,128)(2,1)S(1)}, u32[]{:S(2)}, u32[]{:S(2)}) %collective-permute-start.11) | collective-permute-done | bytes 262176 | tf_op jit(solution)/shard_map/ppermute | solution.py:305
  128.1 5.1 %collective-permute-start.10 = (bf16[128,1024]{1,0:T(8,128)(2,1)}, bf16[128,1024]{1,0:T(8,128)(2,1)S(1)}, u32[]{:S(2)}, u32[]{:S(2)}) collective-permute-start(bf16[128,1024]{1,0:T(8,128)(2,1)} %get-tuple-element.36), channel_id=1, source_target_pairs={{0,1},{1,0},{2,3},{3,2},{4,5},{5,4},{6,7},{7,6},{8,9},{9,8},{10,11... | collective-permute-start | bytes 786440 | tf_op jit(solution)/shard_map/ppermute | solution.py:237
  133.8 4.3 %collective-permute-start.13 = (bf16[32,512]{1,0:T(8,128)(2,1)S(1)}, bf16[32,512]{1,0:T(8,128)(2,1)S(1)}, u32[]{:S(2)}, u32[]{:S(2)}) collective-permute-start(bf16[32,512]{1,0:T(8,128)(2,1)S(1)} %fusion.13), channel_id=1, source_target_pairs={{0,8},{1,9},{2,10},{3,11},{4,12},{5,13},{6,14},{7,15},{8,0},{9,1},... | collective-permute-start | bytes 98312 | tf_op jit(solution)/shard_map/ppermute | solution.py:308
  138.3 5.8 %all-to-all-done = bf16[16,16,16,256]{3,2,1,0:T(8,128)(2,1)S(1)} async-done(((bf16[16,16,16,256]{3,2,1,0:T(8,128)(2,1)}), bf16[16,16,16,256]{3,2,1,0:T(8,128)(2,1)S(1)}, u32[]{:S(2)}, u32[]{:S(2)}) %all-to-all-start) | async-done | bytes 2097184 | tf_op jit(solution)/shard_map/all_to_all | solution.py:287
  145.1 11.1 %all-to-all-start.1 = ((bf16[32,16,256]{2,1,0:T(8,128)(2,1)}), bf16[32,16,256]{2,1,0:T(8,128)(2,1)S(1)}, u32[]{:S(2)}, u32[]{:S(2)}) async-start(bf16[32,16,256]{2,1,0:T(8,128)(2,1)} %bitcast.10), calls=%async_computation.1 | async-start | bytes 524288 | tf_op jit(solution)/shard_map/all_to_all | solution.py:293
  158.8 2.5 %collective-permute-start.14 = (bf16[128,1024]{1,0:T(8,128)(2,1)S(1)}, bf16[128,1024]{1,0:T(8,128)(2,1)S(1)}, u32[]{:S(2)}, u32[]{:S(2)}) collective-permute-start(bf16[128,1024]{1,0:T(8,128)(2,1)S(1)} %dynamic-slice_convert_fusion), channel_id=1, source_target_pairs={{0,1},{1,0},{2,3},{3,2},{4,5},{5,4},{6,7},{7,6},{8,9},{9,8},{10,11... | collective-permute-start | bytes 786440 | tf_op jit(solution)/shard_map/ppermute | solution.py:237
  161.2 16.8 %all-to-all-done.1 = bf16[32,16,256]{2,1,0:T(8,128)(2,1)S(1)} async-done(((bf16[32,16,256]{2,1,0:T(8,128)(2,1)}), bf16[32,16,256]{2,1,0:T(8,128)(2,1)S(1)}, u32[]{:S(2)}, u32[]{:S(2)}) %all-to-all-start.1) | async-done | bytes 262176 | tf_op jit(solution)/shard_map/all_to_all | solution.py:293
  178.8 3.5 %all-to-all-start.2 = ((bf16[16,2,16,256]{3,2,1,0:T(8,128)(2,1)}), bf16[16,2,16,256]{3,2,1,0:T(8,128)(2,1)S(1)}, u32[]{:S(2)}, u32[]{:S(2)}) async-start(bf16[16,2,16,256]{3,2,1,0:T(8,128)(2,1)} %broadcast_in_dim.21), calls=%async_computation.2 | async-start | bytes 524288 | tf_op jit(solution)/shard_map/all_to_all | solution.py:297
  183.9 5.9 %all-to-all-done.2 = bf16[16,2,16,256]{3,2,1,0:T(8,128)(2,1)S(1)} async-done(((bf16[16,2,16,256]{3,2,1,0:T(8,128)(2,1)}), bf16[16,2,16,256]{3,2,1,0:T(8,128)(2,1)S(1)}, u32[]{:S(2)}, u32[]{:S(2)}) %all-to-all-start.2) | async-done | bytes 262176 | tf_op jit(solution)/shard_map/all_to_all | solution.py:297
  (93 shorter events, 26.5 us)
Async XLA Ops:
  2.0 31.8 %collective-permute-start.1 = (bf16[16,1024]{0,1:T(8,128)(2,1)S(1)}, bf16[16,1024]{0,1:T(8,128)(2,1)S(1)}, u32[]{:S(2)}, u32[]{:S(2)}) collective-permute-start(bf16[16,1024]{0,1:T(8,128)(2,1)S(1)} %slice.66), channel_id=1, source_target_pairs={{0,8},{1,9},{2,10},{3,11},{4,12},{5,13},{6,14},{7,15},{8,0},{9,1},... | collective-permute-start | bytes 98312 | tf_op jit(solution)/shard_map/ppermute | solution.py:264
  11.7 35.0 %copy-start.3 = (bf16[1,128,1024]{2,1,0:T(8,128)(2,1)S(1)}, bf16[1,128,1024]{2,1,0:T(8,128)(2,1)}, u32[]{:S(2)}) copy-start(bf16[1,128,1024]{2,1,0:T(8,128)(2,1)} %param.5) | copy-start | bytes 786436
  12.8 34.1 %copy-start.8 = (bf16[1,128,1024]{2,1,0:T(8,128)(2,1)S(1)}, bf16[1,128,1024]{2,1,0:T(8,128)(2,1)}, u32[]{:S(2)}) copy-start(bf16[1,128,1024]{2,1,0:T(8,128)(2,1)} %param.6) | copy-start | bytes 786436
  12.8 21.2 %collective-permute-start = (bf16[64,1024]{1,0:T(8,128)(2,1)S(1)}, bf16[64,1024]{1,0:T(8,128)(2,1)S(1)}, u32[]{:S(2)}, u32[]{:S(2)}) collective-permute-start(bf16[64,1024]{1,0:T(8,128)(2,1)S(1)} %bitcast.49), channel_id=1, source_target_pairs={{0,1},{1,0},{2,3},{3,2},{4,5},{5,4},{6,7},{7,6},{8,9},{9,8},{10,11... | collective-permute-start | bytes 393224 | tf_op jit(solution)/shard_map/ppermute | solution.py:237
  34.2 15.3 %collective-permute-start.3 = (bf16[48,1024]{0,1:T(8,128)(2,1)S(1)}, bf16[48,1024]{0,1:T(8,128)(2,1)S(1)}, u32[]{:S(2)}, u32[]{:S(2)}) collective-permute-start(bf16[48,1024]{0,1:T(8,128)(2,1)S(1)} %copy.49), channel_id=1, source_target_pairs={{0,4},{1,5},{2,6},{3,7},{4,0},{5,1},{6,2},{7,3},{8,12},{9,13},{10,... | collective-permute-start | bytes 294920 | tf_op jit(solution)/shard_map/ppermute | solution.py:266
  36.2 14.4 %collective-permute-start.2 = (bf16[128,1024]{1,0:T(8,128)(2,1)S(1)}, bf16[128,1024]{1,0:T(8,128)(2,1)S(1)}, u32[]{:S(2)}, u32[]{:S(2)}) collective-permute-start(bf16[128,1024]{1,0:T(8,128)(2,1)S(1)} %maximum_select_fusion.2), channel_id=1, source_target_pairs={{2,0},{271,1},{18,16},{287,17},{34,32},{303,33},{50,48},{319,49},{... | collective-permute-start | bytes 786440 | tf_op jit(solution)/shard_map/ppermute | solution.py:267
  50.7 27.6 %copy-start.6 = (bf16[256,1024]{1,0:T(8,128)(2,1)}, bf16[256,1024]{1,0:T(8,128)(2,1)S(1)}, u32[]{:S(2)}) copy-start(bf16[256,1024]{1,0:T(8,128)(2,1)S(1)} %maximum_select_fusion.1.refs_6_) | copy-start | bytes 1572868
  50.7 22.9 %collective-permute-start.4 = (bf16[256,1024]{1,0:T(8,128)(2,1)S(1)}, bf16[256,1024]{1,0:T(8,128)(2,1)S(1)}, u32[]{:S(2)}, u32[]{:S(2)}) collective-permute-start(bf16[256,1024]{1,0:T(8,128)(2,1)S(1)} %maximum_select_fusion.1.refs_6_), channel_id=1, source_target_pairs={{270,0},{3,1},{286,16},{19,17},{302,32},{35,33},{318,48},{51,49},{... | collective-permute-start | bytes 1572872 | tf_op jit(solution)/shard_map/ppermute | solution.py:272
  55.9 22.3 %collective-permute-start.8 = (bf16[256,1024]{0,1:T(8,128)(2,1)S(1)}, bf16[256,1024]{0,1:T(8,128)(2,1)S(1)}, u32[]{:S(2)}, u32[]{:S(2)}) collective-permute-start(bf16[256,1024]{0,1:T(8,128)(2,1)S(1)} %pad_maximum_fusion.1), channel_id=1, source_target_pairs={{0,1},{1,0},{2,3},{3,2},{4,5},{5,4},{6,7},{7,6},{8,9},{9,8},{10,11... | collective-permute-start | bytes 1572872 | tf_op jit(solution)/shard_map/ppermute | solution.py:237
  63.5 9.8 %collective-permute-start.5 = (bf16[128,1024]{0,1:T(8,128)(2,1)S(1)}, bf16[128,1024]{0,1:T(8,128)(2,1)S(1)}, u32[]{:S(2)}, u32[]{:S(2)}) collective-permute-start(bf16[128,1024]{0,1:T(8,128)(2,1)S(1)} %pad_maximum_fusion.4), channel_id=1, source_target_pairs={{0,2},{1,3},{2,0},{3,1},{4,6},{5,7},{6,4},{7,5},{8,10},{9,11},{10,... | collective-permute-start | bytes 786440 | tf_op jit(solution)/shard_map/ppermute | solution.py:270
  73.6 5.1 %collective-permute-start.7 = (bf16[192,1024]{0,1:T(8,128)(2,1)S(1)}, bf16[192,1024]{0,1:T(8,128)(2,1)S(1)}, u32[]{:S(2)}, u32[]{:S(2)}) collective-permute-start(bf16[192,1024]{0,1:T(8,128)(2,1)S(1)} %pad_maximum_fusion.3), channel_id=1, source_target_pairs={{0,1},{1,0},{2,3},{3,2},{4,5},{5,4},{6,7},{7,6},{8,9},{9,8},{10,11... | collective-permute-start | bytes 1179656 | tf_op jit(solution)/shard_map/ppermute | solution.py:237
  76.3 11.2 %collective-permute-start.6 = (bf16[256,1024]{1,0:T(8,128)(2,1)S(1)}, bf16[256,1024]{1,0:T(8,128)(2,1)}, u32[]{:S(2)}, u32[]{:S(2)}) collective-permute-start(bf16[256,1024]{1,0:T(8,128)(2,1)S(1)} %collective-permute-done.4.refs_7_), channel_id=1, source_target_pairs={{2,0},{271,1},{18,16},{287,17},{34,32},{303,33},{50,48},{319,49},{... | collective-permute-start | bytes 1572872 | tf_op jit(solution)/shard_map/ppermute | solution.py:275
  87.6 10.4 %collective-permute-start.9 = (bf16[256,1024]{1,0:T(8,128)(2,1)}, bf16[256,1024]{1,0:T(8,128)(2,1)S(1)}, u32[]{:S(2)}, u32[]{:S(2)}) collective-permute-start(bf16[256,1024]{1,0:T(8,128)(2,1)} %collective-permute-done.6.refs_8_), channel_id=1, source_target_pairs={{270,0},{3,1},{286,16},{19,17},{302,32},{35,33},{318,48},{51,49},{... | collective-permute-start | bytes 1572872 | tf_op jit(solution)/shard_map/ppermute | solution.py:278
  111.7 26.3 %copy-start.11 = (bf16[256,64]{1,0:T(8,128)(2,1)S(1)}, bf16[256,64]{1,0:T(8,128)(2,1)}, u32[]{:S(2)}) copy-start(bf16[256,64]{1,0:T(8,128)(2,1)} %constant.29) | copy-start | bytes 98308
  111.8 32.4 %all-to-all-start = ((bf16[16,16,16,256]{3,2,1,0:T(8,128)(2,1)}), bf16[16,16,16,256]{3,2,1,0:T(8,128)(2,1)S(1)}, u32[]{:S(2)}, u32[]{:S(2)}) async-start(bf16[16,16,16,256]{3,2,1,0:T(8,128)(2,1)} %get-tuple-element.42), calls=%async_computation | async-start | bytes 4194304 | tf_op jit(solution)/shard_map/all_to_all | solution.py:287
  118.7 7.4 %collective-permute-start.11 = (bf16[256,512]{1,0:T(8,128)(2,1)S(1)}, bf16[256,512]{1,0:T(8,128)(2,1)S(1)}, u32[]{:S(2)}, u32[]{:S(2)}) collective-permute-start(bf16[256,512]{1,0:T(8,128)(2,1)S(1)} %copy-done.14), channel_id=1, source_target_pairs={{0,2},{1,3},{2,0},{3,1},{4,6},{5,7},{6,4},{7,5},{8,10},{9,11},{10,... | collective-permute-start | bytes 786440 | tf_op jit(solution)/shard_map/ppermute | solution.py:305
  126.2 7.6 %collective-permute-start.12 = (bf16[96,512]{1,0:T(8,128)(2,1)S(1)}, bf16[96,512]{1,0:T(8,128)(2,1)S(1)}, u32[]{:S(2)}, u32[]{:S(2)}) collective-permute-start(bf16[96,512]{1,0:T(8,128)(2,1)S(1)} %pad_maximum_fusion.7), channel_id=1, source_target_pairs={{0,4},{1,5},{2,6},{3,7},{4,0},{5,1},{6,2},{7,3},{8,12},{9,13},{10,... | collective-permute-start | bytes 294920 | tf_op jit(solution)/shard_map/ppermute | solution.py:307
  128.1 54.2 %collective-permute-start.10 = (bf16[128,1024]{1,0:T(8,128)(2,1)}, bf16[128,1024]{1,0:T(8,128)(2,1)S(1)}, u32[]{:S(2)}, u32[]{:S(2)}) collective-permute-start(bf16[128,1024]{1,0:T(8,128)(2,1)} %get-tuple-element.36), channel_id=1, source_target_pairs={{0,1},{1,0},{2,3},{3,2},{4,5},{5,4},{6,7},{7,6},{8,9},{9,8},{10,11... | collective-permute-start | bytes 786440 | tf_op jit(solution)/shard_map/ppermute | solution.py:237
  133.8 22.5 %collective-permute-start.13 = (bf16[32,512]{1,0:T(8,128)(2,1)S(1)}, bf16[32,512]{1,0:T(8,128)(2,1)S(1)}, u32[]{:S(2)}, u32[]{:S(2)}) collective-permute-start(bf16[32,512]{1,0:T(8,128)(2,1)S(1)} %fusion.13), channel_id=1, source_target_pairs={{0,8},{1,9},{2,10},{3,11},{4,12},{5,13},{6,14},{7,15},{8,0},{9,1},... | collective-permute-start | bytes 98312 | tf_op jit(solution)/shard_map/ppermute | solution.py:308
  138.2 18.2 %copy-start.9 = (bf16[256,128]{1,0:T(8,128)(2,1)S(1)}, bf16[256,128]{1,0:T(8,128)(2,1)}, u32[]{:S(2)}) copy-start(bf16[256,128]{1,0:T(8,128)(2,1)} %constant.28) | copy-start | bytes 196612
  145.1 32.9 %all-to-all-start.1 = ((bf16[32,16,256]{2,1,0:T(8,128)(2,1)}), bf16[32,16,256]{2,1,0:T(8,128)(2,1)S(1)}, u32[]{:S(2)}, u32[]{:S(2)}) async-start(bf16[32,16,256]{2,1,0:T(8,128)(2,1)} %bitcast.10), calls=%async_computation.1 | async-start | bytes 524288 | tf_op jit(solution)/shard_map/all_to_all | solution.py:293
  158.7 23.6 %copy-start.4 = (f32[128,1024]{1,0:T(8,128)S(1)}, f32[128,1024]{1,0:T(8,128)}, u32[]{:S(2)}) copy-start(f32[128,1024]{1,0:T(8,128)} %get-tuple-element.35) | copy-start | bytes 1572868
  158.8 24.3 %collective-permute-start.14 = (bf16[128,1024]{1,0:T(8,128)(2,1)S(1)}, bf16[128,1024]{1,0:T(8,128)(2,1)S(1)}, u32[]{:S(2)}, u32[]{:S(2)}) collective-permute-start(bf16[128,1024]{1,0:T(8,128)(2,1)S(1)} %dynamic-slice_convert_fusion), channel_id=1, source_target_pairs={{0,1},{1,0},{2,3},{3,2},{4,5},{5,4},{6,7},{7,6},{8,9},{9,8},{10,11... | collective-permute-start | bytes 786440 | tf_op jit(solution)/shard_map/ppermute | solution.py:237
  178.8 11.0 %all-to-all-start.2 = ((bf16[16,2,16,256]{3,2,1,0:T(8,128)(2,1)}), bf16[16,2,16,256]{3,2,1,0:T(8,128)(2,1)S(1)}, u32[]{:S(2)}, u32[]{:S(2)}) async-start(bf16[16,2,16,256]{3,2,1,0:T(8,128)(2,1)} %broadcast_in_dim.21), calls=%async_computation.2 | async-start | bytes 524288 | tf_op jit(solution)/shard_map/all_to_all | solution.py:297
  (11 other events, 101.4 us)
